TPU v7x, 32 devices: a whole 2x2x4 slice. The times are simulated.
32 devices in a mesh: rep: 2 (over core), ctx: 4 (over z), tp: 4 (over y, x).
Axes of the slice: x: 2, y: 2, z: 4, core: 2. Of those that a mesh axis runs over, the one named last changes fastest.
Arguments:
- q_mr: bfloat16 [2048, 8192], P(('rep', 'ctx'), 'tp'), parts along dimension 0, may hold values from -6 to 6
- k_mr: bfloat16 [2048, 8192], P(('rep', 'ctx'), 'tp'), parts along dimension 0, may hold values from -6 to 6
- v_mr: bfloat16 [2048, 8192], P(('rep', 'ctx'), 'tp'), parts along dimension 0, may hold values from -6 to 6
- q_li: bfloat16 [2048, 8192], P(('rep', 'ctx'), 'tp'), parts along dimension 0, may hold values from -6 to 6
- k_li: bfloat16 [2048, 8192], P(('rep', 'ctx'), 'tp'), parts along dimension 0, may hold values from -6 to 6
- mr_taps: bfloat16 [512, 128], P('tp'), may hold values from -0.5 to 0.5
- li_rate: float32 [512, 16], P('tp'), may hold values from 0 to 0.0625, as said below
- li_residue: float32 [512, 16], P('tp'), may hold values from -1.5 to 1.5
Outputs:
- mr_out: bfloat16 [2048, 8192], P(('rep', 'ctx'), 'tp'), parts along dimension 0
- li_out: bfloat16 [2048, 8192], P(('rep', 'ctx'), 'tp'), parts along dimension 0
There are 2 independent parts, one for each index of `rep`. A program takes and returns all parts, laid end to end along the dimension named above; an argument that names none is the same for every part. Nothing has to cross between parts.
Inputs may be any that keep to these rules, and one draw needn't show every extreme that they name: `li_rate`: positive decay rates per position.
All inputs are finite; a program needn't handle non-finite values.
Results may differ from a plain program's by a relative error of at most 0.013.
Values may be sent and summed in bfloat16 or wider, within the bound.
No kernel may reach another device: no remote copies, remote signals or barrier semaphores. Data moves between devices by JAX's collectives and lax.ppermute only.
A program may use at most 128 MiB of HBM per device.

v0:
```python
import jax
import jax.numpy as jnp
from jax import lax
from jax.sharding import PartitionSpec as P

highest = lax.Precision.HIGHEST


def shifted(array, axis, by):
    peers = lax.axis_size(axis)
    pairs = [(i, i + by) for i in range(peers) if 0 <= i + by < peers]
    return lax.ppermute(array, axis, pairs)


def modal_tables(li_rate, li_residue, block_len):
    positions = jnp.arange(block_len).astype(jnp.float32)
    rate_col = li_rate[:, :, None]
    res_scale = li_residue * jnp.sqrt(-jnp.expm1(-2.0 * li_rate))
    li_taps = jnp.einsum("gp,gpt->gt", res_scale, jnp.exp(-rate_col * positions), precision=highest)
    end_w = jnp.exp(-rate_col * (block_len - 1.0 - positions))
    carry_w = res_scale[:, :, None] * jnp.exp(-rate_col * (positions + 1.0))
    block_decay = jnp.exp(-li_rate * block_len)
    return (li_taps, end_w, carry_w, block_decay)


def lower_toeplitz(tap_rows):
    group_count, tap_len = tap_rows.shape
    flipped = jnp.concatenate(
        [tap_rows[:, ::-1], jnp.zeros((group_count, tap_len - 1), tap_rows.dtype)], axis=1
    )
    tiled = jnp.tile(flipped, (1, tap_len + 1))[:, : tap_len * 2 * tap_len]
    lower_table = tiled.reshape(group_count, tap_len, 2 * tap_len)[:, :, :tap_len]
    return lower_table[:, ::-1, :]


def split_product(pattern, matrix, operand):
    upper_part = matrix.astype(jnp.bfloat16)
    lower_part = (matrix - upper_part.astype(jnp.float32)).astype(jnp.bfloat16)
    first_sum = jnp.einsum(pattern, upper_part, operand, preferred_element_type=jnp.float32)
    return first_sum + jnp.einsum(pattern, lower_part, operand, preferred_element_type=jnp.float32)


def block_combine(earlier, follower):
    return (earlier[0] * follower[0], follower[0][..., None] * earlier[1] + follower[1])


def body(q_mr, k_mr, v_mr, q_li, k_li, mr_taps, li_rate, li_residue):
    seq_rows, channels = q_mr.shape
    groups, tap_count = mr_taps.shape
    group_width = channels // groups
    u_mr = k_mr * v_mr
    rim_rows = shifted(u_mr[seq_rows - (tap_count - 1) :], "ctx", 1)
    extended = jnp.concatenate([rim_rows, u_mr], axis=0)
    kernel = jnp.broadcast_to(mr_taps[:, None, ::-1], (groups, group_width, tap_count))
    kernel = kernel.reshape(channels, tap_count).T[:, None, :]
    conv_mr = lax.conv_general_dilated(
        extended[None],
        kernel,
        (1,),
        "VALID",
        dimension_numbers=("NWC", "WIO", "NWC"),
        feature_group_count=channels,
        preferred_element_type=jnp.float32,
    )[0]
    mr_out = (q_mr * conv_mr).astype(jnp.bfloat16)
    u_li = k_li * mr_out
    ctx_count = lax.axis_size("ctx")
    own_groups = groups // ctx_count
    first_group = lax.axis_index("ctx") * own_groups
    own_rate = lax.dynamic_slice_in_dim(li_rate, first_group, own_groups, 0)
    own_residue = lax.dynamic_slice_in_dim(li_residue, first_group, own_groups, 0)
    li_taps, end_w, carry_w, block_decay = modal_tables(own_rate, own_residue, seq_rows)
    li_table = lower_toeplitz(li_taps)
    arrived = lax.all_to_all(
        u_li.reshape(seq_rows, groups, group_width), "ctx", split_axis=1, concat_axis=0, tiled=True
    )
    item_count = arrived.shape[2]
    blocked = arrived.reshape(ctx_count, seq_rows, own_groups, item_count)
    near_part = split_product("gts,bsgc->btgc", li_table, blocked)
    local_state = split_product("gps,bsgc->bgpc", end_w, blocked)
    decays = jnp.broadcast_to(block_decay, (ctx_count,) + block_decay.shape)
    _, inclusive = lax.associative_scan(block_combine, (decays, local_state))
    entering = jnp.concatenate([jnp.zeros_like(inclusive[:1]), inclusive[:-1]], axis=0)
    far_part = jnp.einsum("gpt,bgpc->btgc", carry_w, entering, precision=highest)
    summed = (near_part + far_part).reshape(ctx_count * seq_rows, own_groups, item_count)
    conv_li = lax.all_to_all(summed, "ctx", split_axis=0, concat_axis=1, tiled=True)
    conv_li = conv_li.reshape(seq_rows, channels)
    li_out = (q_li * conv_li).astype(jnp.bfloat16)
    return (mr_out, li_out)


def solution(mesh):
    in_specs = (
        P(("rep", "ctx"), "tp"),
        P(("rep", "ctx"), "tp"),
        P(("rep", "ctx"), "tp"),
        P(("rep", "ctx"), "tp"),
        P(("rep", "ctx"), "tp"),
        P("tp", None),
        P("tp", None),
        P("tp", None),
    )
    out_specs = (P(("rep", "ctx"), "tp"), P(("rep", "ctx"), "tp"))
    return jax.shard_map(body, mesh=mesh, in_specs=in_specs, out_specs=out_specs, check_vma=False)
```

profile of v0, /device:TPU:0, one launch (start us, length us, event | category | flops | bytes accessed | tf_op | source)
XLA Modules:
  0.0 289.3 jit_solution(14442095852063862820)
XLA Ops:
  0.6 1.9 mul.101
  2.7 5.7 %collective-permute-start = (bf16[127,2048]{1,0:T(8,128)(2,1)S(1)}, bf16[127,2048]{1,0:T(8,128)(2,1)}, u32[]{:S(2)}, u32[]{:S(2)}) collective-permute-start(bf16[127,2048]{1,0:T(8,128)(2,1)S(1)} %slice.52), channel_id=1, source_target_pairs={{0,4},{4,8},{8,12},{1,5},{5,9},{9,13},{2,6},{6,10},{10,14},{3,7},{... | collective-permute-start | bytes 1560584 | tf_op jit(solution)/shard_map/ppermute | solution.py:12
  9.6 9.2 %collective-permute-done = bf16[127,2048]{1,0:T(8,128)(2,1)} collective-permute-done((bf16[127,2048]{1,0:T(8,128)(2,1)S(1)}, bf16[127,2048]{1,0:T(8,128)(2,1)}, u32[]{:S(2)}, u32[]{:S(2)}) %collective-permute-start) | collective-permute-done | bytes 520224 | tf_op jit(solution)/shard_map/ppermute | solution.py:12
  20.1 28.6 %fusion.5 = f32[1,256,2048]{2,0,1:T(1,128)S(1)} fusion(bf16[128,1,2048]{2,1,0:T(2,128)(2,1)S(1)} %copy.48, bf16[1,383,2048]{2,1,0:T(8,128)(2,1)S(1)} %maximum_bitcast_fusion), kind=kOutput, calls=%fused_computation.5 | convolution fusion | flops 134217728 | bytes 4190208 | tf_op jit(solution)/shard_map/conv_general_dilated | solution.py:56
  48.7 2.1 fusion.52
  52.1 5.9 %all-to-all-start = ((bf16[256,128,16]{0,2,1:T(8,128)(2,1)}), bf16[256,128,16]{0,2,1:T(8,128)(2,1)S(1)}, u32[]{:S(2)}, u32[]{:S(2)}) async-start(bf16[256,128,16]{0,2,1:T(8,128)(2,1)} %bitcast.4), calls=%async_computation | async-start | bytes 2097152 | tf_op jit(solution)/shard_map/all_to_all | solution.py:74
  59.2 8.1 %tile.4 = f32[32,257,511]{2,1,0:T(8,128)} broadcast(f32[32,511]{1,0:T(8,128)S(1)} %concatenate.13), dimensions={0,2} | broadcast | bytes 16875264 | tf_op jit(solution)/shard_map/tile | solution.py:31
  67.3 25.8 %tile.10 = f32[32,131327]{1,0:T(8,128)} reshape(f32[32,257,511]{2,1,0:T(8,128)} %tile.4) | data formatting | bytes 33619712 | tf_op jit(solution)/shard_map/tile | solution.py:31
  93.1 5.8 %slice-done = f32[32,131072]{1,0:T(8,128)S(1)} async-done(((f32[32,131327]{1,0:T(8,128)}), f32[32,131072]{1,0:T(8,128)S(1)}, s32[]{:S(2)}) %slice-start) | async-done | bytes 16777240 | tf_op jit(solution)/shard_map/slice | solution.py:31
  98.9 16.3 %copy.75 = f32[4,8,256,512]{3,2,1,0:T(8,128)S(1)} copy(f32[4,8,256,512]{3,1,2,0:T(8,128)S(1)} %bitcast.71) | data formatting | bytes 33554432
  115.2 4.3 %slice.54 = f32[32,256,256]{2,1,0:T(8,128)} slice(f32[32,256,512]{2,1,0:T(8,128)S(1)} %bitcast.72), slice={[0:32], [0:256], [0:256]} | slice | bytes 16777216 | tf_op jit(solution)/shard_map/slice | solution.py:32
  119.5 64.0 %rev.11 = f32[32,256,256]{2,1,0:T(8,128)} reverse(f32[32,256,256]{2,1,0:T(8,128)} %slice.54), dimensions={1} | reverse | bytes 16777216 | tf_op jit(solution)/shard_map/rev | solution.py:33
  186.1 7.2 %fusion.1 = f32[32,4,16,256]{3,2,1,0:T(8,128)S(1)} fusion(f32[32,256,256]{2,1,0:T(8,128)} %rev.11, bf16[256,4,32,16]{0,3,2,1:T(8,128)(2,1)S(1)} %bitcast.77), kind=kOutput, calls=%fused_computation.2 | convolution fusion | flops 276824064 | bytes 11534336 | tf_op jit(solution)/shard_map/gts,bsgc->btgc/dot_general | solution.py:40
  193.3 1.9 fusion.19
  195.2 4.8 %add_bitcast_fusion = f32[4,256,32,16]{1,3,0,2:T(8,128)S(1)} fusion(f32[32,4,16,256]{3,2,1,0:T(8,128)S(1)} %fusion.19, f32[32,4,16,256]{3,2,1,0:T(8,128)S(1)} %fusion.1, f32[32,256,256]{2,1,0:T(8,128)} %rev.11, bf16[256,4,32,16]{0,3,2,1:T(8,128)(2,1)S(1)} %bitcast.78), kind=kOutput, calls=%fused_computation.11 | convolution fusion | flops 271581184 | bytes 15728640 | tf_op jit(solution)/shard_map/gts,bsgc->btgc/dot_general | solution.py:39
  200.0 6.5 %copy.71 = f32[4,256,32,16]{2,3,1,0:T(8,128)} copy(f32[4,256,32,16]{1,3,0,2:T(8,128)S(1)} %add_bitcast_fusion) | data formatting | bytes 4194304 | tf_op jit(solution)/shard_map/reshape | solution.py:85
  206.5 7.1 %reshape.60 = f32[4,1,131072]{2,1,0:T(1,128)} reshape(f32[1024,16,32]{2,1,0:T(8,128)} %bitcast.73) | data formatting | bytes 4194304
  213.6 5.1 %all-to-all-start.1 = ((f32[4,1,131072]{2,1,0:T(1,128)}), f32[4,1,131072]{2,1,0:T(1,128)S(1)}, u32[]{:S(2)}, u32[]{:S(2)}) async-start(f32[4,1,131072]{2,1,0:T(1,128)} %reshape.60), calls=%async_computation.1 | async-start | bytes 4194304 | tf_op jit(solution)/shard_map/all_to_all | solution.py:86
  218.6 1.5 copy.49
  220.1 45.3 %all-to-all-done.1 = f32[4,1,131072]{2,1,0:T(1,128)S(1)} async-done(((f32[4,1,131072]{2,1,0:T(1,128)}), f32[4,1,131072]{2,1,0:T(1,128)S(1)}, u32[]{:S(2)}, u32[]{:S(2)}) %all-to-all-start.1) | async-done | bytes 2097184 | tf_op jit(solution)/shard_map/all_to_all | solution.py:86
  267.3 7.7 %reduce = f32[4,131072]{1,0:T(4,128)S(1)} reduce(f32[4,1,131072]{2,1,0:T(1,128)} %copy-done, f32[]{:T(128)} %broadcast.42), dimensions={1}, to_apply=%all_to_all.25.reduce_sub_computation | reduce | bytes 4194308 | tf_op jit(solution)/shard_map/all_to_all | solution.py:86
  275.0 6.1 %reshape.61 = f32[1024,16,32]{2,1,0:T(8,128)} reshape(f32[4,131072]{1,0:T(4,128)S(1)} %reduce) | data formatting | bytes 4194304
  281.1 6.0 %copy.72 = f32[4,256,32,16]{1,0,3,2:T(4,128)S(1)} copy(f32[4,256,32,16]{2,3,1,0:T(8,128)} %bitcast.74) | data formatting | bytes 4194304 | tf_op jit(solution)/shard_map/all_to_all | solution.py:86
  287.8 1.4 copy.61
  (46 shorter events, 10.1 us)
Async XLA Ops:
  0.6 7.8 %copy-start.3 = (bf16[128,128]{1,0:T(8,128)(2,1)S(1)}, bf16[128,128]{1,0:T(8,128)(2,1)}, u32[]{:S(2)}) copy-start(bf16[128,128]{1,0:T(8,128)(2,1)} %param.13) | copy-start | bytes 98308
  2.7 16.1 %collective-permute-start = (bf16[127,2048]{1,0:T(8,128)(2,1)S(1)}, bf16[127,2048]{1,0:T(8,128)(2,1)}, u32[]{:S(2)}, u32[]{:S(2)}) collective-permute-start(bf16[127,2048]{1,0:T(8,128)(2,1)S(1)} %slice.52), channel_id=1, source_target_pairs={{0,4},{4,8},{8,12},{1,5},{5,9},{9,13},{2,6},{6,10},{10,14},{3,7},{... | collective-permute-start | bytes 1560584 | tf_op jit(solution)/shard_map/ppermute | solution.py:12
  20.1 28.6 %copy-start.1 = (bf16[256,2048]{1,0:T(8,128)(2,1)S(1)}, bf16[256,2048]{1,0:T(8,128)(2,1)}, u32[]{:S(2)}) copy-start(bf16[256,2048]{1,0:T(8,128)(2,1)} %param.12) | copy-start | bytes 3145732
  20.1 28.6 %copy-start.2 = (bf16[256,2048]{1,0:T(8,128)(2,1)S(1)}, bf16[256,2048]{1,0:T(8,128)(2,1)}, u32[]{:S(2)}) copy-start(bf16[256,2048]{1,0:T(8,128)(2,1)} %param.8) | copy-start | bytes 3145732
  50.8 7.2 %copy-start.4 = (f32[128,16]{0,1:T(8,128)S(1)}, f32[128,16]{0,1:T(8,128)}, u32[]{:S(2)}) copy-start(f32[128,16]{0,1:T(8,128)} %param.14) | copy-start | bytes 24580
  50.8 7.2 %copy-start.5 = (f32[128,16]{0,1:T(8,128)S(1)}, f32[128,16]{0,1:T(8,128)}, u32[]{:S(2)}) copy-start(f32[128,16]{0,1:T(8,128)} %param.15) | copy-start | bytes 24580
  52.1 131.4 %all-to-all-start = ((bf16[256,128,16]{0,2,1:T(8,128)(2,1)}), bf16[256,128,16]{0,2,1:T(8,128)(2,1)S(1)}, u32[]{:S(2)}, u32[]{:S(2)}) async-start(bf16[256,128,16]{0,2,1:T(8,128)(2,1)} %bitcast.4), calls=%async_computation | async-start | bytes 2097152 | tf_op jit(solution)/shard_map/all_to_all | solution.py:74
  93.1 5.8 %slice-start = ((f32[32,131327]{1,0:T(8,128)}), f32[32,131072]{1,0:T(8,128)S(1)}, s32[]{:S(2)}) async-start(f32[32,131327]{1,0:T(8,128)} %tile.10), calls=%async_computation.2 | async-start | bytes 33554432 | tf_op jit(solution)/shard_map/slice | solution.py:31
  213.6 51.9 %all-to-all-start.1 = ((f32[4,1,131072]{2,1,0:T(1,128)}), f32[4,1,131072]{2,1,0:T(1,128)S(1)}, u32[]{:S(2)}, u32[]{:S(2)}) async-start(f32[4,1,131072]{2,1,0:T(1,128)} %reshape.60), calls=%async_computation.1 | async-start | bytes 4194304 | tf_op jit(solution)/shard_map/all_to_all | solution.py:86
  265.4 1.3 copy-start
where the time goes:
time: 295 us; the launch traced here: 289 us
  local copies, waits for them, and re-layouts  160 us (54%)
  waiting for transfers between devices  54.5 us (18%)
  matrix products  43.9 us (15%)
  starting transfers between devices  16.7 us (6%)
  other arithmetic  13.7 us (5%)
    rev x1, local copies, waits for them, and re-layouts, lower_toeplitz(): return lower_table[:, ::-1, :]  64 us
    all_to_all x1, waiting for transfers between devices, body(): lax.all_to_all(summed, 'ctx', split_axis=0, concat_axis=1, tiled=True)  45.3 us
    unnamed x18, local copies, waits for them, and re-layouts  34.4 us
    another operation x2, local copies, waits for them, and re-layouts, lower_toeplitz(): tiled = jnp.tile(flipped, (1, tap_len + 1))[:, :tap_len * 2 * tap_len]  33.9 us
    conv_general_dilated x1, matrix products, body(): lax.conv_general_dilated(extended[None], kernel, (1,), 'VALID', dimension...  28.6 us
    ppermute x1, waiting for transfers between devices, shifted(): return lax.ppermute(array, axis, pairs)  9.25 us
    all_to_all x1, other arithmetic, body(): lax.all_to_all(summed, 'ctx', split_axis=0, concat_axis=1, tiled=True)  7.72 us
    dot_general x2, matrix products, split_product(): jnp.einsum(pattern, lower_part, operand, preferred_element_type=jnp.float32)  7.65 us
  transfers between devices with their start and end apart: 3, of which 2 were waited for; matrix products, arithmetic and copies ran while one was open for 42% of the time, Pallas kernels for 0%

commit v1 on v0

v1 whole, which is shorter than its diff:
```python
import functools

import jax
import jax.numpy as jnp
from jax import lax
from jax.experimental import pallas as pl
from jax.experimental.pallas import tpu as pltpu
from jax.sharding import PartitionSpec as P

F32 = jnp.float32
BF16 = jnp.bfloat16
WIDE = 256


def shifted(array, axis, by):
    peers = lax.axis_size(axis)
    pairs = [(i, i + by) for i in range(peers) if 0 <= i + by < peers]
    return lax.ppermute(array, axis, pairs)


def iota(shape, dim):
    return lax.broadcasted_iota(jnp.int32, shape, dim)


def dot(a, b):
    return jnp.dot(a, b, preferred_element_type=F32)


def same_group(width, dtype):
    rows, cols = iota((WIDE, WIDE), 0), iota((WIDE, WIDE), 1)
    return jnp.where(rows // width == cols // width, 1.0, 0.0).astype(F32).astype(dtype)


def spread(compact, mask):
    copies = WIDE // compact.shape[0]
    return jnp.concatenate([compact] * copies, axis=0) * mask


def split(array):
    upper = array.astype(BF16)
    return upper, (array - upper.astype(F32)).astype(BF16)


def one_minus_exp(x):
    series = 1.0 - x / 7.0
    for n in (6.0, 5.0, 4.0, 3.0, 2.0):
        series = 1.0 - x / n * series
    return jnp.where(x < 0.25, x * series, 1.0 - jnp.exp(-x))


def expand_groups(per_group, width):
    groups = per_group.shape[0]
    pick = (iota((groups, WIDE), 1) // width == iota((groups, WIDE), 0)).astype(F32)
    return lax.dot_general(
        per_group.astype(F32),
        pick,
        (((0,), (0,)), ((), ())),
        precision=lax.Precision.HIGHEST,
        preferred_element_type=F32,
    )


def local_kernel(
    q_ref, k_ref, v_ref, kli_ref, taps_ref, rate_ref, residue_ref,
    mr_ref, part_ref, near_ref, state_ref, taptab_ref, litab_ref, powers_ref, rates_ref, scale_ref,
    mask_ref, acc_ref,
):
    rows = k_ref.shape[0]
    groups, tap_count = taps_ref.shape
    width = WIDE // groups
    half = tap_count

    @pl.when(pl.program_id(0) == 0)
    def _():
        mask_ref[...] = same_group(width, BF16)

    mask = mask_ref[...]
    lane_item = iota((tap_count + width, WIDE), 1) % width

    table = expand_groups(taps_ref[...], width)
    table = jnp.concatenate([table, jnp.zeros((width, WIDE), F32)], axis=0)
    step = 1
    while step < width:
        table = jnp.where((lane_item & step) != 0, pltpu.roll(table, step, 0), table)
        step *= 2
    table = table.astype(BF16)
    taptab_ref[...] = table

    rates = expand_groups(rate_ref[...], width)
    scale = expand_groups(residue_ref[...], width) * jnp.sqrt(one_minus_exp(2.0 * rates))
    rates_ref[...] = rates
    scale_ref[...] = scale
    poles = rates.shape[0]
    item = (iota((poles, WIDE), 1) % width).astype(F32)
    rate_row = jnp.sum(jnp.where(iota((poles, WIDE), 0) == iota((poles, WIDE), 1) % width, rates, 0.0), axis=0, keepdims=True)
    times = iota((half, WIDE), 0).astype(F32)
    powers_ref[...] = jnp.exp(-rate_row * (times + 1.0)).astype(BF16)
    power_hi, power_lo = split(jnp.exp(-rate_row * times))
    lift_hi, lift_lo = split(scale * jnp.exp(rates * item))
    lift_hi, lift_lo = spread(lift_hi, mask), spread(lift_lo, mask)
    li_taps = dot(power_hi, lift_hi) + dot(power_hi, lift_lo) + dot(power_lo, lift_hi)
    li_taps = jnp.where(iota((half, WIDE), 0) >= iota((half, WIDE), 1) % width, li_taps, 0.0)
    ends = jnp.exp(-rates * (width - 1.0 - item))
    li_table = jnp.concatenate([ends, li_taps], axis=0).astype(BF16)
    litab_ref[...] = li_table

    u = k_ref[...] * v_ref[...]
    acc_ref[...] = jnp.zeros_like(acc_ref)
    for first in range(0, rows, width):
        count = min(tap_count + width, rows - first)
        acc_ref[pl.ds(first, count), :] += dot(table[:count], spread(u[first : first + width], mask))
    part_ref[...] = acc_ref[:half, :]
    mr = (q_ref[half:, :].astype(F32) * acc_ref[half:, :]).astype(BF16)
    mr_ref[...] = mr
    near, state = near_block(mr * kli_ref[...], li_table, rates, mask, width, acc_ref)
    near_ref[...] = near
    state_ref[...] = state


def near_block(u, li_table, rates, mask, width, acc_ref):
    rows = u.shape[0]
    poles = rates.shape[0]
    chunk_decay = jnp.exp(-rates * width)
    state = jnp.zeros((poles, WIDE), F32)
    acc_ref[:rows, :] = jnp.zeros((rows, WIDE), F32)
    for first in range(0, rows, width):
        got = dot(li_table[: poles + rows - first], spread(u[first : first + width], mask))
        state = state * chunk_decay + got[:poles]
        acc_ref[pl.ds(first, rows - first), :] += got[poles:]
    return acc_ref[:rows, :], state


def rim_kernel(
    rim_ref, part_ref, q_ref, kli_ref, taptab_ref, litab_ref, rates_ref, late_ref, mr_in_ref,
    mr_ref, near_ref, early_ref, total_ref,
    mask_ref, acc_ref,
):
    del mr_in_ref
    half = rim_ref.shape[0]
    width = taptab_ref.shape[0] - half

    @pl.when(pl.program_id(0) == 0)
    def _():
        mask_ref[...] = same_group(width, BF16)

    mask = mask_ref[...]
    rates = rates_ref[...]
    rim = rim_ref[...]
    acc_ref[...] = part_ref[...]
    for first in range(0, half, width):
        acc_ref[: first + width, :] += dot(taptab_ref[half - first :, :], spread(rim[first : first + width], mask))
    mr = (q_ref[...].astype(F32) * acc_ref[...]).astype(BF16)
    mr_ref[...] = mr
    near, state = near_block(mr * kli_ref[...], litab_ref[...], rates, mask, width, acc_ref)
    near_ref[...] = near
    early_ref[...] = state
    total_ref[...] = (late_ref[...] + state * jnp.exp(-rates * half)).astype(BF16)


def far_kernel(
    n_arrived, *refs,
):
    arrived = refs[:n_arrived]
    q_ref, near_early_ref, near_late_ref, early_ref, powers_ref, rates_ref, scale_ref, out_ref, mask_ref = refs[n_arrived:]
    half = near_early_ref.shape[0]
    width = WIDE * early_ref.shape[0] // WIDE

    @pl.when(pl.program_id(0) == 0)
    def _():
        mask_ref[...] = same_group(width, BF16)

    mask = mask_ref[...]
    rates = rates_ref[...]
    block_decay = jnp.exp(-rates * (2.0 * half))
    entering = arrived[-1][...].astype(F32)
    for ref in arrived[-2::-1]:
        entering = entering * block_decay + ref[...].astype(F32)
    middle = entering * jnp.exp(-rates * half) + early_ref[...]
    powers = powers_ref[...]
    for at, state, near_ref in ((0, entering, near_early_ref), (half, middle, near_late_ref)):
        far = dot(powers, spread((state * scale_ref[...]).astype(BF16), mask))
        out_ref[at : at + half, :] = (q_ref[at : at + half, :].astype(F32) * (near_ref[...] + far)).astype(BF16)


def columns(rows, at=0):
    return pl.BlockSpec((rows, WIDE), lambda i: (at, i))


def body(q_mr, k_mr, v_mr, q_li, k_li, mr_taps, li_rate, li_residue):
    rows, channels = q_mr.shape
    groups, tap_count = mr_taps.shape
    poles = li_rate.shape[1]
    width = channels // groups
    half = tap_count
    assert rows == 2 * half and poles == width
    steps = channels // WIDE
    wide_groups = WIDE // width
    shape = jax.ShapeDtypeStruct
    params = pltpu.CompilerParams(vmem_limit_bytes=32 * 1024 * 1024)

    rim = shifted(k_mr[half:] * v_mr[half:], "ctx", 1)

    per_group = lambda n: pl.BlockSpec((wide_groups, n), lambda i: (i, 0))
    mr_out, part, near_late, late, taptab, litab, powers, rates, scale = pl.pallas_call(
        local_kernel,
        grid=(steps,),
        in_specs=[
            columns(rows), columns(rows), columns(rows), columns(half, 1),
            per_group(tap_count), per_group(poles), per_group(poles),
        ],
        out_specs=[
            columns(half, 1), columns(half), columns(half), columns(poles),
            columns(half + width), columns(half + poles), columns(half), columns(poles), columns(poles),
        ],
        out_shape=[
            shape((rows, channels), BF16), shape((half, channels), F32), shape((half, channels), F32),
            shape((poles, channels), F32), shape((half + width, channels), BF16), shape((half + poles, channels), BF16),
            shape((half, channels), BF16), shape((poles, channels), F32), shape((poles, channels), F32),
        ],
        scratch_shapes=[pltpu.VMEM((WIDE, WIDE), BF16), pltpu.VMEM((rows, WIDE), F32)],
        cost_estimate=pl.CostEstimate(flops=4 * 10**9, bytes_accessed=10 * 2**20, transcendentals=10**6),
        compiler_params=params,
        name="local_rows",
    )(q_mr, k_mr, v_mr, k_li, mr_taps, li_rate, li_residue)

    mr_out, near_early, early, total = pl.pallas_call(
        rim_kernel,
        grid=(steps,),
        in_specs=[
            columns(half), columns(half), columns(half), columns(half),
            columns(half + width), columns(half + poles), columns(poles), columns(poles), pl.BlockSpec(memory_space=pl.ANY),
        ],
        out_specs=[columns(half), columns(half), columns(poles), columns(poles)],
        out_shape=[
            shape((rows, channels), BF16), shape((half, channels), F32),
            shape((poles, channels), F32), shape((poles, channels), BF16),
        ],
        scratch_shapes=[pltpu.VMEM((WIDE, WIDE), BF16), pltpu.VMEM((half, WIDE), F32)],
        input_output_aliases={8: 0},
        cost_estimate=pl.CostEstimate(flops=2 * 10**9, bytes_accessed=4 * 2**20, transcendentals=10**4),
        compiler_params=params,
        name="rim_rows",
    )(rim, part, q_mr, k_li, taptab, litab, rates, late, mr_out)

    peers = lax.axis_size("ctx")
    reach = min(3, max(peers - 1, 1))
    arrived = [shifted(total, "ctx", by) for by in range(1, reach + 1)]
    while reach < peers - 1:
        decay = jnp.exp(-rates * rows)
        window = arrived[-1].astype(F32)
        for piece in arrived[-2::-1]:
            window = window * decay + piece.astype(F32)
        merged = window
        for times in (1, 2, 3):
            if times * reach < peers:
                far = shifted(window, "ctx", times * reach)
                merged = merged + far * jnp.exp(-rates * (rows * reach * times))
        arrived = [merged]
        reach *= 4

    li_out = pl.pallas_call(
        functools.partial(far_kernel, len(arrived)),
        grid=(steps,),
        in_specs=[columns(poles)] * len(arrived) + [
            columns(rows), columns(half), columns(half), columns(poles), columns(half), columns(poles), columns(poles),
        ],
        out_specs=columns(rows),
        out_shape=shape((rows, channels), BF16),
        scratch_shapes=[pltpu.VMEM((WIDE, WIDE), BF16)],
        cost_estimate=pl.CostEstimate(flops=10**9, bytes_accessed=5 * 2**20, transcendentals=10**4),
        compiler_params=params,
        name="far_rows",
    )(*arrived, q_li, near_early, near_late, early, powers, rates, scale)
    return (mr_out, li_out)


def solution(mesh):
    seq = P(("rep", "ctx"), "tp")
    in_specs = (seq, seq, seq, seq, seq, P("tp", None), P("tp", None), P("tp", None))
    return jax.shard_map(body, mesh=mesh, in_specs=in_specs, out_specs=(seq, seq), check_vma=False)
```

time: 295 us -> 44.1 us (0.15); the launches traced: 289 us -> 43.7 us
  local copies, waits for them, and re-layouts: 160 us -> 4.54 us
  waiting for transfers between devices: 54.5 us -> 1.88 us
  matrix products: 43.9 us -> 0 us
  Pallas kernels: 0 us -> 23.2 us
  other arithmetic: 13.7 us -> 1.35 us
  starting transfers between devices: 16.7 us -> 12 us
    rev x3 -> x0, local copies, waits for them, and re-layouts: 64.3 us -> none  [the longest x1 64 us: lower_toeplitz(): return lower_table[:, ::-1, :]]
    all_to_all x2 -> x0, waiting for transfers between devices: 45.3 us -> none  [the longest x1 45.3 us: body(): lax.all_to_all(summed, 'ctx', split_axis=0, concat_axis=1, tiled=True)]
    another operation x2 -> x0, local copies, waits for them, and re-layouts: 33.9 us -> none  [lower_toeplitz(): tiled = jnp.tile(flipped, (1, tap_len + 1))[:, :tap_len * 2 * tap_len]]
    unnamed x18, local copies, waits for them, and re-layouts: 34.4 us -> 4.54 us
    conv_general_dilated x1 -> x0, matrix products: 28.6 us -> none  [body(): lax.conv_general_dilated(extended[None], kernel, (1,), 'VALID', dimension...]
    pallas_call x0 -> x3, Pallas kernels: none -> 23.2 us  [the longest x1 11.2 us: body(): pl.pallas_call(local_kernel, grid=(steps,), in_specs=[columns(rows), colu...]
    dot_general x6 -> x0, matrix products: 15.3 us -> none  [the longest x2 7.65 us: split_product(): jnp.einsum(pattern, lower_part, operand, preferred_element_type=jnp.float32)]
    all_to_all x2 -> x0, starting transfers between devices: 11 us -> none  [the longest x1 5.88 us: body(): lax.all_to_all(u_li.reshape(seq_rows, groups, group_width), 'ctx', split_...]
  transfers between devices with their start and end apart: 3 -> 4, of which waited for: 2 -> 2; matrix products, arithmetic and copies ran while one was open for 42% -> 0% of each run, Pallas kernels for 0% -> 26%
where the time goes in v1:
time: 44.1 us; the launch traced here: 43.7 us
  Pallas kernels  23.2 us (53%)
  starting transfers between devices  12 us (27%)
  local copies, waits for them, and re-layouts  4.54 us (10%)
  waiting for transfers between devices  1.88 us (4%)
  other arithmetic  1.35 us (3%)
  between operations  0.73 us (2%)
    ppermute x4, starting transfers between devices, shifted(): return lax.ppermute(array, axis, pairs)  12 us
    pallas_call x1, Pallas kernels, body(): pl.pallas_call(local_kernel, grid=(steps,), in_specs=[columns(rows), colu...  11.2 us
    pallas_call x1, Pallas kernels, body(): pl.pallas_call(rim_kernel, grid=(steps,), in_specs=[columns(half), column...  7.84 us
    unnamed x18, local copies, waits for them, and re-layouts  4.54 us
    pallas_call x1, Pallas kernels, body(): pl.pallas_call(functools.partial(far_kernel, len(arrived)), grid=(steps,)...  4.13 us
    ppermute x4, waiting for transfers between devices, shifted(): return lax.ppermute(array, axis, pairs)  1.88 us
    mul x1, other arithmetic, body(): rim = shifted(k_mr[half:] * v_mr[half:], 'ctx', 1)  1.35 us
  transfers between devices with their start and end apart: 4, of which 2 were waited for; matrix products, arithmetic and copies ran while one was open for 0% of the time, Pallas kernels for 26%

profile of v1, /device:TPU:0, one launch (start us, length us, event | category | flops | bytes accessed | tf_op | source)
XLA Modules:
  0.0 43.7 jit_solution(6501585536556412036)
XLA Ops:
  0.6 0.0 copy-start.1
  0.6 0.0 copy-start.6
  0.6 1.3 %slice_multiply_fusion = bf16[128,2048]{1,0:T(8,128)(2,1)S(1)} fusion(bf16[256,2048]{1,0:T(8,128)(2,1)} %v_ref.1, bf16[256,2048]{1,0:T(8,128)(2,1)} %k_ref.1), kind=kLoop, calls=%fused_computation | loop fusion | flops 262144 | bytes 1572864 | tf_op jit(solution)/shard_map/mul | solution.py:201
  2.0 0.0 copy-start.7
  2.0 5.0 %collective-permute-start = (bf16[128,2048]{1,0:T(8,128)(2,1)S(1)}, bf16[128,2048]{1,0:T(8,128)(2,1)S(1)}, u32[]{:S(2)}, u32[]{:S(2)}) collective-permute-start(bf16[128,2048]{1,0:T(8,128)(2,1)S(1)} %slice_multiply_fusion), channel_id=1, source_target_pairs={{0,4},{4,8},{8,12},{1,5},{5,9},{9,13},{2,6},{6,10},{10,14},{3,7},{... | collective-permute-start | bytes 1572872 | tf_op jit(solution)/shard_map/ppermute | solution.py:18
  7.0 0.0 copy-done.6
  7.0 0.1 copy.11.rate_ref
  7.1 0.0 copy-start.5
  7.1 0.1 copy.12.residue_ref
  7.2 0.6 %copy-done.5 = bf16[128,128]{1,0:T(8,128)(2,1)S(1)} copy-done((bf16[128,128]{1,0:T(8,128)(2,1)S(1)}, bf16[128,128]{1,0:T(8,128)(2,1)}, u32[]{:S(2)}) %copy-start.5) | copy-done | bytes 32792
  7.9 1.2 %copy-done.2 = bf16[256,2048]{1,0:T(8,128)(2,1)S(1)} copy-done((bf16[256,2048]{1,0:T(8,128)(2,1)S(1)}, bf16[256,2048]{1,0:T(8,128)(2,1)}, u32[]{:S(2)}) %copy-start.2) | copy-done | bytes 1048600
  9.1 1.2 %copy-done.3 = bf16[256,2048]{1,0:T(8,128)(2,1)S(1)} copy-done((bf16[256,2048]{1,0:T(8,128)(2,1)S(1)}, bf16[256,2048]{1,0:T(8,128)(2,1)}, u32[]{:S(2)}) %copy-start.3) | copy-done | bytes 1048600
  10.3 1.2 %copy-done.4 = bf16[256,2048]{1,0:T(8,128)(2,1)S(1)} copy-done((bf16[256,2048]{1,0:T(8,128)(2,1)S(1)}, bf16[256,2048]{1,0:T(8,128)(2,1)}, u32[]{:S(2)}) %copy-start.4) | copy-done | bytes 1048600
  11.5 11.2 %local_rows.1 = (bf16[256,2048]{1,0:T(8,128)(2,1)}, f32[128,2048]{1,0:T(8,128)S(1)}, f32[128,2048]{1,0:T(8,128)S(1)}, f32[16,2048]{1,0:T(8,128)S(1)}, bf16[144,2...) custom-call(bf16[256,2048]{1,0:T(8,128)(2,1)S(1)} %copy-done.3, ...), custom_call_target="tpu_custom_call" | custom-call | flops 4000000000 | bytes 10485760 | tf_op jit(solution)/shard_map/local_rows/pallas_call | solution.py:204
  22.8 0.0 collective-permute-done.rim_ref
  22.8 7.8 %rim_rows.1 = (bf16[256,2048]{1,0:T(8,128)(2,1)}, f32[128,2048]{1,0:T(8,128)S(1)}, f32[16,2048]{1,0:T(8,128)S(1)}, bf16[16,2048]{1,0:T(8,128)(2,1)S(1)}) custom-call(bf16[128,2048]{1,0:T(8,128)(2,1)S(1)} %collective-permute-done.rim_ref, f32[128,2048]{1,0:T(8,128)S(1)} %get-tuple-element.15.part_ref, ...), custom_call_target="tpu_custom_call", output_to_operand_aliasing={{0}: (8, {})} | custom-call | flops 2000000000 | bytes 4194304 | tf_op jit(solution)/shard_map/rim_rows/pallas_call | solution.py:226
  30.6 3.3 %collective-permute-start.3 = (bf16[16,2048]{1,0:T(8,128)(2,1)S(1)}, bf16[16,2048]{1,0:T(8,128)(2,1)S(1)}, u32[]{:S(2)}, u32[]{:S(2)}) collective-permute-start(bf16[16,2048]{1,0:T(8,128)(2,1)S(1)} %get-tuple-element.22), channel_id=1, source_target_pairs={{0,12},{1,13},{2,14},{3,15},{16,28},{17,29},{18,30},{19,31}} | collective-permute-start | bytes 196616 | tf_op jit(solution)/shard_map/ppermute | solution.py:18
  33.9 1.8 %collective-permute-start.2 = (bf16[16,2048]{1,0:T(8,128)(2,1)S(1)}, bf16[16,2048]{1,0:T(8,128)(2,1)S(1)}, u32[]{:S(2)}, u32[]{:S(2)}) collective-permute-start(bf16[16,2048]{1,0:T(8,128)(2,1)S(1)} %get-tuple-element.22), channel_id=1, source_target_pairs={{0,8},{4,12},{1,9},{5,13},{2,10},{6,14},{3,11},{7,15},{16,24},{20,... | collective-permute-start | bytes 196616 | tf_op jit(solution)/shard_map/ppermute | solution.py:18
  35.8 1.9 %collective-permute-start.1 = (bf16[16,2048]{1,0:T(8,128)(2,1)S(1)}, bf16[16,2048]{1,0:T(8,128)(2,1)S(1)}, u32[]{:S(2)}, u32[]{:S(2)}) collective-permute-start(bf16[16,2048]{1,0:T(8,128)(2,1)S(1)} %get-tuple-element.22), channel_id=1, source_target_pairs={{0,4},{4,8},{8,12},{1,5},{5,9},{9,13},{2,6},{6,10},{10,14},{3,7},{... | collective-permute-start | bytes 196616 | tf_op jit(solution)/shard_map/ppermute | solution.py:18
  37.7 0.0 collective-permute-done.3.refs_2_
  37.7 0.1 collective-permute-done.2.refs_1_
  37.8 1.8 %collective-permute-done.1.refs_0_ = bf16[16,2048]{1,0:T(8,128)(2,1)S(1)} collective-permute-done((bf16[16,2048]{1,0:T(8,128)(2,1)S(1)}, bf16[16,2048]{1,0:T(8,128)(2,1)S(1)}, u32[]{:S(2)}, u32[]{:S(2)}) %collective-permute-start.1) | collective-permute-done | bytes 65568 | tf_op jit(solution)/shard_map/ppermute | solution.py:18
  39.6 0.0 copy-done
  39.6 4.1 %far_rows.1 = bf16[256,2048]{1,0:T(8,128)(2,1)} custom-call(bf16[16,2048]{1,0:T(8,128)(2,1)S(1)} %collective-permute-done.1.refs_0_, bf16[16,2048]{1,0:T(8,128)(2,1)S(1)} %collective-permute-done.2.refs_1_, bf16[16,2048]{1,0:T(8,128)(2,1)S(1)} %collective-permute-done.3.refs_2_, bf16[256,2048]{1,0:T(8,128)(2,1)S(1)} %copy-done, ...), custom_call_target="tpu_custom_call" | custom-call | flops 1000000000 | bytes 5242880 | tf_op jit(solution)/shard_map/far_rows/pallas_call | solution.py:261
  (6 shorter events, 0.0 us)
Async XLA Ops:
  0.6 6.6 %copy-start.1 = (bf16[256,2048]{1,0:T(8,128)(2,1)S(1)}, bf16[256,2048]{1,0:T(8,128)(2,1)}, u32[]{:S(2)}) copy-start(bf16[256,2048]{1,0:T(8,128)(2,1)} %v_ref.1) | copy-start | bytes 3145732
  0.6 6.3 %copy-start.6 = (f32[128,16]{0,1:T(8,128)S(1)}, f32[128,16]{0,1:T(8,128)}, u32[]{:S(2)}) copy-start(f32[128,16]{0,1:T(8,128)} %param.14) | copy-start | bytes 24580
  2.0 5.1 %copy-start.7 = (f32[128,16]{0,1:T(8,128)S(1)}, f32[128,16]{0,1:T(8,128)}, u32[]{:S(2)}) copy-start(f32[128,16]{0,1:T(8,128)} %param.15) | copy-start | bytes 24580
  2.0 20.8 %collective-permute-start = (bf16[128,2048]{1,0:T(8,128)(2,1)S(1)}, bf16[128,2048]{1,0:T(8,128)(2,1)S(1)}, u32[]{:S(2)}, u32[]{:S(2)}) collective-permute-start(bf16[128,2048]{1,0:T(8,128)(2,1)S(1)} %slice_multiply_fusion), channel_id=1, source_target_pairs={{0,4},{4,8},{8,12},{1,5},{5,9},{9,13},{2,6},{6,10},{10,14},{3,7},{... | collective-permute-start | bytes 1572872 | tf_op jit(solution)/shard_map/ppermute | solution.py:18
  7.1 0.8 %copy-start.5 = (bf16[128,128]{1,0:T(8,128)(2,1)S(1)}, bf16[128,128]{1,0:T(8,128)(2,1)}, u32[]{:S(2)}) copy-start(bf16[128,128]{1,0:T(8,128)(2,1)} %taps_ref.1) | copy-start | bytes 98308
  7.9 1.2 %copy-start.2 = (bf16[256,2048]{1,0:T(8,128)(2,1)S(1)}, bf16[256,2048]{1,0:T(8,128)(2,1)}, u32[]{:S(2)}) copy-start(bf16[256,2048]{1,0:T(8,128)(2,1)} %k_ref.1) | copy-start | bytes 3145732
  9.1 1.2 %copy-start.3 = (bf16[256,2048]{1,0:T(8,128)(2,1)S(1)}, bf16[256,2048]{1,0:T(8,128)(2,1)}, u32[]{:S(2)}) copy-start(bf16[256,2048]{1,0:T(8,128)(2,1)} %q_ref.3) | copy-start | bytes 3145732
  10.3 1.2 %copy-start.4 = (bf16[256,2048]{1,0:T(8,128)(2,1)S(1)}, bf16[256,2048]{1,0:T(8,128)(2,1)}, u32[]{:S(2)}) copy-start(bf16[256,2048]{1,0:T(8,128)(2,1)} %kli_ref.3) | copy-start | bytes 3145732
  22.8 16.8 %copy-start = (bf16[256,2048]{1,0:T(8,128)(2,1)S(1)}, bf16[256,2048]{1,0:T(8,128)(2,1)}, u32[]{:S(2)}) copy-start(bf16[256,2048]{1,0:T(8,128)(2,1)} %refs_3_.1) | copy-start | bytes 3145732
  30.6 7.1 %collective-permute-start.3 = (bf16[16,2048]{1,0:T(8,128)(2,1)S(1)}, bf16[16,2048]{1,0:T(8,128)(2,1)S(1)}, u32[]{:S(2)}, u32[]{:S(2)}) collective-permute-start(bf16[16,2048]{1,0:T(8,128)(2,1)S(1)} %get-tuple-element.22), channel_id=1, source_target_pairs={{0,12},{1,13},{2,14},{3,15},{16,28},{17,29},{18,30},{19,31}} | collective-permute-start | bytes 196616 | tf_op jit(solution)/shard_map/ppermute | solution.py:18
  33.9 3.9 %collective-permute-start.2 = (bf16[16,2048]{1,0:T(8,128)(2,1)S(1)}, bf16[16,2048]{1,0:T(8,128)(2,1)S(1)}, u32[]{:S(2)}, u32[]{:S(2)}) collective-permute-start(bf16[16,2048]{1,0:T(8,128)(2,1)S(1)} %get-tuple-element.22), channel_id=1, source_target_pairs={{0,8},{4,12},{1,9},{5,13},{2,10},{6,14},{3,11},{7,15},{16,24},{20,... | collective-permute-start | bytes 196616 | tf_op jit(solution)/shard_map/ppermute | solution.py:18
  35.8 3.8 %collective-permute-start.1 = (bf16[16,2048]{1,0:T(8,128)(2,1)S(1)}, bf16[16,2048]{1,0:T(8,128)(2,1)S(1)}, u32[]{:S(2)}, u32[]{:S(2)}) collective-permute-start(bf16[16,2048]{1,0:T(8,128)(2,1)S(1)} %get-tuple-element.22), channel_id=1, source_target_pairs={{0,4},{4,8},{8,12},{1,5},{5,9},{9,13},{2,6},{6,10},{10,14},{3,7},{... | collective-permute-start | bytes 196616 | tf_op jit(solution)/shard_map/ppermute | solution.py:18

commit v2 on v1

v2 whole, which is shorter than its diff:
```python
import functools

import jax
import jax.numpy as jnp
from jax import lax
from jax.experimental import pallas as pl
from jax.experimental.pallas import tpu as pltpu
from jax.sharding import PartitionSpec as P

F32 = jnp.float32
BF16 = jnp.bfloat16
WIDE = 256


def shifted(array, axis, by):
    peers = lax.axis_size(axis)
    pairs = [(i, i + by) for i in range(peers) if 0 <= i + by < peers]
    return lax.ppermute(array, axis, pairs)


def iota(shape, dim):
    return lax.broadcasted_iota(jnp.int32, shape, dim)


def dot(a, b):
    return jnp.dot(a, b, preferred_element_type=F32)


def same_group(width, dtype):
    rows, cols = iota((WIDE, WIDE), 0), iota((WIDE, WIDE), 1)
    return jnp.where(rows // width == cols // width, 1.0, 0.0).astype(F32).astype(dtype)


def spread(compact, mask):
    copies = WIDE // compact.shape[0]
    return jnp.concatenate([compact] * copies, axis=0) * mask


def split(array):
    upper = array.astype(BF16)
    return upper, (array - upper.astype(F32)).astype(BF16)


def one_minus_exp(x):
    series = 1.0 - x / 7.0
    for n in (6.0, 5.0, 4.0, 3.0, 2.0):
        series = 1.0 - x / n * series
    return jnp.where(x < 0.25, x * series, 1.0 - jnp.exp(-x))


def expand_groups(per_group, width):
    groups = per_group.shape[0]
    pick = (iota((groups, WIDE), 1) // width == iota((groups, WIDE), 0)).astype(F32)
    return lax.dot_general(
        per_group.astype(F32),
        pick,
        (((0,), (0,)), ((), ())),
        precision=lax.Precision.HIGHEST,
        preferred_element_type=F32,
    )


def cols(i):
    return pl.ds(pl.multiple_of(i * WIDE, WIDE), WIDE)


def local_kernel(
    q_hbm, k_hbm, v_hbm, kli_hbm, qli_hbm, taps_ref, rate_ref, residue_ref,
    mr_hbm, part_ref, near_ref, state_ref, taptab_ref, litab_ref, powers_ref, rates_ref, scale_ref,
    qe_ref, klie_ref, qli_ref,
    k_ref, v_ref, q_ref, kli_ref, mr_ref, mask_ref, acc_ref, in_sem, side_sem, out_sem,
):
    rows, channels = k_hbm.shape
    groups, tap_count = taps_ref.shape
    steps = channels // WIDE
    width = channels // groups
    wide_groups = WIDE // width
    poles = rate_ref.shape[1]
    half = tap_count

    def fetch(i):
        at = cols(i)
        late = pl.ds(half, rows - half)
        return (
            pltpu.make_async_copy(k_hbm.at[:, at], k_ref.at[:, at], in_sem.at[0, i]),
            pltpu.make_async_copy(v_hbm.at[:, at], v_ref.at[:, at], in_sem.at[1, i]),
            pltpu.make_async_copy(q_hbm.at[late, at], q_ref.at[:, at], in_sem.at[2, i]),
            pltpu.make_async_copy(kli_hbm.at[late, at], kli_ref.at[:, at], in_sem.at[3, i]),
        )

    def put(i):
        return pltpu.make_async_copy(mr_ref.at[:, cols(i)], mr_hbm.at[pl.ds(half, rows - half), cols(i)], out_sem.at[i])

    side = (
        pltpu.make_async_copy(q_hbm.at[pl.ds(0, half)], qe_ref, side_sem.at[0]),
        pltpu.make_async_copy(kli_hbm.at[pl.ds(0, half)], klie_ref, side_sem.at[1]),
        pltpu.make_async_copy(qli_hbm, qli_ref, side_sem.at[2]),
    )
    for i in range(steps):
        for copy in fetch(i):
            copy.start()
    for copy in side:
        copy.start()

    mask_ref[...] = same_group(width, BF16)
    lane_item = iota((tap_count + width, WIDE), 1) % width
    item = (iota((poles, WIDE), 1) % width).astype(F32)
    times = iota((half, WIDE), 0).astype(F32)

    @pl.loop(0, steps)
    def _(i):
        at = cols(i)
        mask = mask_ref[...]
        own = pl.ds(pl.multiple_of(i * wide_groups, wide_groups), wide_groups)

        table = expand_groups(taps_ref[own, :], width)
        table = jnp.concatenate([table, jnp.zeros((width, WIDE), F32)], axis=0)
        step = 1
        while step < width:
            table = jnp.where((lane_item & step) != 0, pltpu.roll(table, step, 0), table)
            step *= 2
        table = table.astype(BF16)
        taptab_ref[:, at] = table

        rates = expand_groups(rate_ref[own, :], width)
        scale = expand_groups(residue_ref[own, :], width) * jnp.sqrt(one_minus_exp(2.0 * rates))
        rates_ref[:, at] = rates
        scale_ref[:, at] = scale
        on_diagonal = iota((poles, WIDE), 0) == iota((poles, WIDE), 1) % width
        rate_row = jnp.sum(jnp.where(on_diagonal, rates, 0.0), axis=0, keepdims=True)
        power = jnp.exp(-rate_row * times)
        powers_ref[:, at] = (power * jnp.exp(-rate_row)).astype(BF16)
        power_hi, power_lo = split(power)
        lift_hi, lift_lo = split(scale * jnp.exp(rates * item))
        lift_hi, lift_lo = spread(lift_hi, mask), spread(lift_lo, mask)
        li_taps = dot(power_hi, lift_hi) + dot(power_hi, lift_lo) + dot(power_lo, lift_hi)
        li_taps = jnp.where(iota((half, WIDE), 0) >= iota((half, WIDE), 1) % width, li_taps, 0.0)
        ends = jnp.exp(-rates * (width - 1.0 - item))
        li_table = jnp.concatenate([ends, li_taps], axis=0).astype(BF16)
        litab_ref[:, at] = li_table

        for copy in fetch(i):
            copy.wait()
        u = k_ref[:, at] * v_ref[:, at]
        acc_ref[...] = jnp.zeros_like(acc_ref)
        for first in range(0, rows, width):
            count = min(tap_count + width, rows - first)
            acc_ref[pl.ds(first, count), :] += dot(table[:count], spread(u[first : first + width], mask))
        part_ref[:, at] = acc_ref[:half, :]
        mr = (q_ref[:, at].astype(F32) * acc_ref[half:, :]).astype(BF16)
        mr_ref[:, at] = mr
        put(i).start()
        near, state = near_block(mr * kli_ref[:, at], li_table, rates, mask, width, acc_ref)
        near_ref[:, at] = near
        state_ref[:, at] = state

    for copy in side:
        copy.wait()
    for i in range(steps):
        put(i).wait()


def near_block(u, li_table, rates, mask, width, acc_ref):
    rows = u.shape[0]
    poles = rates.shape[0]
    chunk_decay = jnp.exp(-rates * width)
    state = jnp.zeros((poles, WIDE), F32)
    acc_ref[:rows, :] = jnp.zeros((rows, WIDE), F32)
    for first in range(0, rows, width):
        got = dot(li_table[: poles + rows - first], spread(u[first : first + width], mask))
        state = state * chunk_decay + got[:poles]
        acc_ref[pl.ds(first, rows - first), :] += got[poles:]
    return acc_ref[:rows, :], state


def rim_kernel(
    rim_ref, part_ref, q_ref, kli_ref, taptab_ref, litab_ref, rates_ref, late_ref, mr_in_hbm,
    mr_hbm, near_ref, early_ref, total_ref,
    mr_ref, mask_ref, acc_ref, out_sem,
):
    del mr_in_hbm
    half, channels = rim_ref.shape
    width = taptab_ref.shape[0] - half
    steps = channels // WIDE

    def put(i):
        return pltpu.make_async_copy(mr_ref.at[:, cols(i)], mr_hbm.at[pl.ds(0, half), cols(i)], out_sem.at[i])

    mask_ref[...] = same_group(width, BF16)

    @pl.loop(0, steps)
    def _(i):
        at = cols(i)
        mask = mask_ref[...]
        rates = rates_ref[:, at]
        rim = rim_ref[:, at]
        acc_ref[...] = part_ref[:, at]
        for first in range(0, half, width):
            acc_ref[: first + width, :] += dot(taptab_ref[half - first :, at], spread(rim[first : first + width], mask))
        mr = (q_ref[:, at].astype(F32) * acc_ref[...]).astype(BF16)
        mr_ref[:, at] = mr
        put(i).start()
        near, state = near_block(mr * kli_ref[:, at], litab_ref[:, at], rates, mask, width, acc_ref)
        near_ref[:, at] = near
        early_ref[:, at] = state
        total_ref[:, at] = (late_ref[:, at] + state * jnp.exp(-rates * half)).astype(BF16)

    for i in range(steps):
        put(i).wait()


def far_kernel(n_arrived, *refs):
    arrived = refs[:n_arrived]
    (
        q_ref, near_early_ref, near_late_ref, early_ref, powers_ref, rates_ref, scale_ref,
        out_hbm, out_ref, mask_ref, out_sem,
    ) = refs[n_arrived:]
    half, channels = near_early_ref.shape
    width = early_ref.shape[0]
    steps = channels // WIDE

    def put(i):
        return pltpu.make_async_copy(out_ref.at[:, cols(i)], out_hbm.at[:, cols(i)], out_sem.at[i])

    mask_ref[...] = same_group(width, BF16)

    @pl.loop(0, steps)
    def _(i):
        at = cols(i)
        mask = mask_ref[...]
        rates = rates_ref[:, at]
        scale = scale_ref[:, at]
        block_decay = jnp.exp(-rates * (2.0 * half))
        entering = arrived[-1][:, at].astype(F32)
        for ref in arrived[-2::-1]:
            entering = entering * block_decay + ref[:, at].astype(F32)
        middle = entering * jnp.exp(-rates * half) + early_ref[:, at]
        powers = powers_ref[:, at]
        for first, state, near_ref in ((0, entering, near_early_ref), (half, middle, near_late_ref)):
            far = dot(powers, spread((state * scale).astype(BF16), mask))
            gate = q_ref[first : first + half, at].astype(F32)
            out_ref[first : first + half, at] = (gate * (near_ref[:, at] + far)).astype(BF16)
        put(i).start()

    for i in range(steps):
        put(i).wait()


def body(q_mr, k_mr, v_mr, q_li, k_li, mr_taps, li_rate, li_residue):
    rows, channels = q_mr.shape
    groups, tap_count = mr_taps.shape
    poles = li_rate.shape[1]
    width = channels // groups
    half = tap_count
    assert rows == 2 * half and poles == width
    steps = channels // WIDE
    params = pltpu.CompilerParams(vmem_limit_bytes=40 * 1024 * 1024)
    vmem, hbm = pl.BlockSpec(memory_space=pltpu.VMEM), pl.BlockSpec(memory_space=pl.ANY)
    in_hbm = lambda array: pltpu.with_memory_space_constraint(array, pltpu.HBM)
    dma = pltpu.SemaphoreType.DMA

    rim = shifted(k_mr[half:] * v_mr[half:], "ctx", 1)

    mr_out, part, near_late, late, taptab, litab, powers, rates, scale, q_early, kli_early, qli = pl.pallas_call(
        local_kernel,
        in_specs=[hbm] * 5 + [vmem] * 3,
        out_specs=[hbm] + [vmem] * 11,
        out_shape=[
            pltpu.HBM((rows, channels), BF16),
            pltpu.VMEM((half, channels), F32),
            pltpu.VMEM((half, channels), F32),
            pltpu.VMEM((poles, channels), F32),
            pltpu.VMEM((half + width, channels), BF16),
            pltpu.VMEM((half + poles, channels), BF16),
            pltpu.VMEM((half, channels), BF16),
            pltpu.VMEM((poles, channels), F32),
            pltpu.VMEM((poles, channels), F32),
            pltpu.VMEM((half, channels), BF16),
            pltpu.VMEM((half, channels), BF16),
            pltpu.VMEM((rows, channels), BF16),
        ],
        scratch_shapes=[
            pltpu.VMEM((rows, channels), BF16),
            pltpu.VMEM((rows, channels), BF16),
            pltpu.VMEM((half, channels), BF16),
            pltpu.VMEM((half, channels), BF16),
            pltpu.VMEM((half, channels), BF16),
            pltpu.VMEM((WIDE, WIDE), BF16),
            pltpu.VMEM((rows, WIDE), F32),
            dma((4, steps)),
            dma((3,)),
            dma((steps,)),
        ],
        cost_estimate=pl.CostEstimate(flops=4 * 10**9, bytes_accessed=10 * 2**20, transcendentals=10**6),
        compiler_params=params,
        name="local_rows",
    )(*map(in_hbm, (q_mr, k_mr, v_mr, k_li, q_li)), mr_taps, li_rate, li_residue)

    mr_out, near_early, early, total = pl.pallas_call(
        rim_kernel,
        in_specs=[vmem] * 8 + [hbm],
        out_specs=[hbm] + [vmem] * 3,
        out_shape=[
            pltpu.HBM((rows, channels), BF16),
            pltpu.VMEM((half, channels), F32),
            pltpu.VMEM((poles, channels), F32),
            pltpu.VMEM((poles, channels), BF16),
        ],
        scratch_shapes=[
            pltpu.VMEM((half, channels), BF16),
            pltpu.VMEM((WIDE, WIDE), BF16),
            pltpu.VMEM((half, WIDE), F32),
            dma((steps,)),
        ],
        input_output_aliases={8: 0},
        cost_estimate=pl.CostEstimate(flops=2 * 10**9, bytes_accessed=4 * 2**20, transcendentals=10**4),
        compiler_params=params,
        name="rim_rows",
    )(rim, part, q_early, kli_early, taptab, litab, rates, late, mr_out)

    peers = lax.axis_size("ctx")
    reach = min(3, max(peers - 1, 1))
    arrived = [shifted(total, "ctx", by) for by in range(1, reach + 1)]
    while reach < peers - 1:
        decay = jnp.exp(-rates * rows)
        window = arrived[-1].astype(F32)
        for piece in arrived[-2::-1]:
            window = window * decay + piece.astype(F32)
        merged = window
        for times in (1, 2, 3):
            if times * reach < peers:
                far = shifted(window, "ctx", times * reach)
                merged = merged + far * jnp.exp(-rates * (rows * reach * times))
        arrived = [merged]
        reach *= 4

    li_out = pl.pallas_call(
        functools.partial(far_kernel, len(arrived)),
        in_specs=[vmem] * (len(arrived) + 7),
        out_specs=hbm,
        out_shape=jax.ShapeDtypeStruct((rows, channels), BF16),
        scratch_shapes=[pltpu.VMEM((rows, channels), BF16), pltpu.VMEM((WIDE, WIDE), BF16), dma((steps,))],
        cost_estimate=pl.CostEstimate(flops=10**9, bytes_accessed=5 * 2**20, transcendentals=10**4),
        compiler_params=params,
        name="far_rows",
    )(*arrived, qli, near_early, near_late, early, powers, rates, scale)
    return (mr_out, li_out)


def solution(mesh):
    seq = P(("rep", "ctx"), "tp")
    in_specs = (seq, seq, seq, seq, seq, P("tp", None), P("tp", None), P("tp", None))
    return jax.shard_map(body, mesh=mesh, in_specs=in_specs, out_specs=(seq, seq), check_vma=False)
```

time: 44.1 us -> 39.9 us (0.905)
  local copies, waits for them, and re-layouts: 4.54 us -> 0.86 us
  Pallas kernels: 23.2 us -> 21.5 us
  starting transfers between devices: 12 us -> 13.4 us
    unnamed x18 -> x8, local copies, waits for them, and re-layouts: 4.54 us -> 0.86 us
    pallas_call x3, Pallas kernels: 23.2 us -> 21.5 us  [the longest x1 12 us: body(): pl.pallas_call(local_kernel, in_specs=[hbm] * 5 + [vmem] * 3, out_specs=[...]
    ppermute x4, starting transfers between devices: 12 us -> 13.4 us  [shifted(): return lax.ppermute(array, axis, pairs)]
  transfers between devices with their start and end apart: 4 -> 4, of which waited for: 2 -> 1; matrix products, arithmetic and copies ran while one was open for 0% -> 1% of each run, Pallas kernels for 26% -> 30%
where the time goes in v2:
time: 39.9 us; the launch traced here: 39.6 us
  Pallas kernels  21.5 us (54%)
  starting transfers between devices  13.4 us (34%)
  waiting for transfers between devices  1.87 us (5%)
  other arithmetic  1.26 us (3%)
  local copies, waits for them, and re-layouts  0.86 us (2%)
  between operations  0.74 us (2%)
    ppermute x4, starting transfers between devices, shifted(): return lax.ppermute(array, axis, pairs)  13.4 us
    pallas_call x1, Pallas kernels, body(): pl.pallas_call(local_kernel, in_specs=[hbm] * 5 + [vmem] * 3, out_specs=[...  12 us
    pallas_call x1, Pallas kernels, body(): pl.pallas_call(rim_kernel, in_specs=[vmem] * 8 + [hbm], out_specs=[hbm] +...  7.02 us
    pallas_call x1, Pallas kernels, body(): pl.pallas_call(functools.partial(far_kernel, len(arrived)), in_specs=[vme...  2.47 us
    ppermute x4, waiting for transfers between devices, shifted(): return lax.ppermute(array, axis, pairs)  1.87 us
    mul x1, other arithmetic, body(): rim = shifted(k_mr[half:] * v_mr[half:], 'ctx', 1)  1.26 us
    unnamed x8, local copies, waits for them, and re-layouts  0.86 us
  transfers between devices with their start and end apart: 4, of which 1 were waited for; matrix products, arithmetic and copies ran while one was open for 1% of the time, Pallas kernels for 30%

profile of v2, /device:TPU:0, one launch (start us, length us, event | category | flops | bytes accessed | tf_op | source)
XLA Modules:
  0.0 39.6 jit_solution(8258914834630103655)
XLA Ops:
  0.6 0.0 copy-start.1
  0.6 1.3 %slice_multiply_fusion = bf16[128,2048]{1,0:T(8,128)(2,1)S(1)} fusion(bf16[256,2048]{1,0:T(8,128)(2,1)} %v_hbm.1, bf16[256,2048]{1,0:T(8,128)(2,1)} %k_hbm.1), kind=kLoop, calls=%fused_computation | loop fusion | flops 262144 | bytes 1572864 | tf_op jit(solution)/shard_map/mul | solution.py:262
  1.9 0.0 copy-start.2
  1.9 5.0 %collective-permute-start = (bf16[128,2048]{1,0:T(8,128)(2,1)S(1)}, bf16[128,2048]{1,0:T(8,128)(2,1)S(1)}, u32[]{:S(2)}, u32[]{:S(2)}) collective-permute-start(bf16[128,2048]{1,0:T(8,128)(2,1)S(1)} %slice_multiply_fusion), channel_id=1, source_target_pairs={{0,4},{4,8},{8,12},{1,5},{5,9},{9,13},{2,6},{6,10},{10,14},{3,7},{... | collective-permute-start | bytes 1572872 | tf_op jit(solution)/shard_map/ppermute | solution.py:18
  6.9 0.0 copy-done.1
  6.9 0.1 copy.11.rate_ref
  7.0 0.0 copy-done.2
  7.0 0.0 copy-start
  7.0 0.1 copy.12.residue_ref
  7.1 0.6 %copy-done = bf16[128,128]{1,0:T(8,128)(2,1)S(1)} copy-done((bf16[128,128]{1,0:T(8,128)(2,1)S(1)}, bf16[128,128]{1,0:T(8,128)(2,1)}, u32[]{:S(2)}) %copy-start) | copy-done | bytes 32792
  7.8 12.0 %local_rows.1 = (bf16[256,2048]{1,0:T(8,128)(2,1)}, f32[128,2048]{1,0:T(8,128)S(1)}, f32[128,2048]{1,0:T(8,128)S(1)}, f32[16,2048]{1,0:T(8,128)S(1)}, bf16[144,2...) custom-call(bf16[256,2048]{1,0:T(8,128)(2,1)} %q_hbm.1, ...), custom_call_target="tpu_custom_call" | custom-call | flops 4000000000 | bytes 10485760 | tf_op jit(solution)/shard_map/local_rows/pallas_call | solution.py:264
  19.8 0.0 collective-permute-done.rim_ref
  19.8 7.0 %rim_rows.1 = (bf16[256,2048]{1,0:T(8,128)(2,1)}, f32[128,2048]{1,0:T(8,128)S(1)}, f32[16,2048]{1,0:T(8,128)S(1)}, bf16[16,2048]{1,0:T(8,128)(2,1)S(1)}) custom-call(bf16[128,2048]{1,0:T(8,128)(2,1)S(1)} %collective-permute-done.rim_ref, f32[128,2048]{1,0:T(8,128)S(1)} %get-tuple-element.18.part_ref, ...), custom_call_target="tpu_custom_call", output_to_operand_aliasing={{0}: (8, {})} | custom-call | flops 2000000000 | bytes 4194304 | tf_op jit(solution)/shard_map/rim_rows/pallas_call | solution.py:299
  26.8 4.7 %collective-permute-start.3 = (bf16[16,2048]{1,0:T(8,128)(2,1)S(1)}, bf16[16,2048]{1,0:T(8,128)(2,1)S(1)}, u32[]{:S(2)}, u32[]{:S(2)}) collective-permute-start(bf16[16,2048]{1,0:T(8,128)(2,1)S(1)} %get-tuple-element.27), channel_id=1, source_target_pairs={{0,12},{1,13},{2,14},{3,15},{16,28},{17,29},{18,30},{19,31}} | collective-permute-start | bytes 196616 | tf_op jit(solution)/shard_map/ppermute | solution.py:18
  31.5 1.3 %collective-permute-start.2 = (bf16[16,2048]{1,0:T(8,128)(2,1)S(1)}, bf16[16,2048]{1,0:T(8,128)(2,1)S(1)}, u32[]{:S(2)}, u32[]{:S(2)}) collective-permute-start(bf16[16,2048]{1,0:T(8,128)(2,1)S(1)} %get-tuple-element.27), channel_id=1, source_target_pairs={{0,8},{4,12},{1,9},{5,13},{2,10},{6,14},{3,11},{7,15},{16,24},{20,... | collective-permute-start | bytes 196616 | tf_op jit(solution)/shard_map/ppermute | solution.py:18
  32.8 2.5 %collective-permute-start.1 = (bf16[16,2048]{1,0:T(8,128)(2,1)S(1)}, bf16[16,2048]{1,0:T(8,128)(2,1)S(1)}, u32[]{:S(2)}, u32[]{:S(2)}) collective-permute-start(bf16[16,2048]{1,0:T(8,128)(2,1)S(1)} %get-tuple-element.27), channel_id=1, source_target_pairs={{0,4},{4,8},{8,12},{1,5},{5,9},{9,13},{2,6},{6,10},{10,14},{3,7},{... | collective-permute-start | bytes 196616 | tf_op jit(solution)/shard_map/ppermute | solution.py:18
  35.2 0.0 collective-permute-done.3.refs_2_
  35.2 0.0 collective-permute-done.2.refs_1_
  35.3 1.9 %collective-permute-done.1.refs_0_ = bf16[16,2048]{1,0:T(8,128)(2,1)S(1)} collective-permute-done((bf16[16,2048]{1,0:T(8,128)(2,1)S(1)}, bf16[16,2048]{1,0:T(8,128)(2,1)S(1)}, u32[]{:S(2)}, u32[]{:S(2)}) %collective-permute-start.1) | collective-permute-done | bytes 65568 | tf_op jit(solution)/shard_map/ppermute | solution.py:18
  37.1 2.5 %far_rows.1 = bf16[256,2048]{1,0:T(8,128)(2,1)} custom-call(bf16[16,2048]{1,0:T(8,128)(2,1)S(1)} %collective-permute-done.1.refs_0_, bf16[16,2048]{1,0:T(8,128)(2,1)S(1)} %collective-permute-done.2.refs_1_, bf16[16,2048]{1,0:T(8,128)(2,1)S(1)} %collective-permute-done.3.refs_2_, bf16[256,2048]{1,0:T(8,128)(2,1)S(1)} %get-tuple-element.28.refs_3_, ...), custom_call_target="tpu_custom_call" | custom-call | flops 1000000000 | bytes 5242880 | tf_op jit(solution)/shard_map/far_rows/pallas_call | solution.py:337
Async XLA Ops:
  0.6 6.3 %copy-start.1 = (f32[128,16]{0,1:T(8,128)S(1)}, f32[128,16]{0,1:T(8,128)}, u32[]{:S(2)}) copy-start(f32[128,16]{0,1:T(8,128)} %param.14) | copy-start | bytes 24580
  1.9 5.1 %copy-start.2 = (f32[128,16]{0,1:T(8,128)S(1)}, f32[128,16]{0,1:T(8,128)}, u32[]{:S(2)}) copy-start(f32[128,16]{0,1:T(8,128)} %param.15) | copy-start | bytes 24580
  1.9 17.8 %collective-permute-start = (bf16[128,2048]{1,0:T(8,128)(2,1)S(1)}, bf16[128,2048]{1,0:T(8,128)(2,1)S(1)}, u32[]{:S(2)}, u32[]{:S(2)}) collective-permute-start(bf16[128,2048]{1,0:T(8,128)(2,1)S(1)} %slice_multiply_fusion), channel_id=1, source_target_pairs={{0,4},{4,8},{8,12},{1,5},{5,9},{9,13},{2,6},{6,10},{10,14},{3,7},{... | collective-permute-start | bytes 1572872 | tf_op jit(solution)/shard_map/ppermute | solution.py:18
  7.0 0.8 %copy-start = (bf16[128,128]{1,0:T(8,128)(2,1)S(1)}, bf16[128,128]{1,0:T(8,128)(2,1)}, u32[]{:S(2)}) copy-start(bf16[128,128]{1,0:T(8,128)(2,1)} %taps_ref.1) | copy-start | bytes 98308
  26.8 8.4 %collective-permute-start.3 = (bf16[16,2048]{1,0:T(8,128)(2,1)S(1)}, bf16[16,2048]{1,0:T(8,128)(2,1)S(1)}, u32[]{:S(2)}, u32[]{:S(2)}) collective-permute-start(bf16[16,2048]{1,0:T(8,128)(2,1)S(1)} %get-tuple-element.27), channel_id=1, source_target_pairs={{0,12},{1,13},{2,14},{3,15},{16,28},{17,29},{18,30},{19,31}} | collective-permute-start | bytes 196616 | tf_op jit(solution)/shard_map/ppermute | solution.py:18
  31.5 3.8 %collective-permute-start.2 = (bf16[16,2048]{1,0:T(8,128)(2,1)S(1)}, bf16[16,2048]{1,0:T(8,128)(2,1)S(1)}, u32[]{:S(2)}, u32[]{:S(2)}) collective-permute-start(bf16[16,2048]{1,0:T(8,128)(2,1)S(1)} %get-tuple-element.27), channel_id=1, source_target_pairs={{0,8},{4,12},{1,9},{5,13},{2,10},{6,14},{3,11},{7,15},{16,24},{20,... | collective-permute-start | bytes 196616 | tf_op jit(solution)/shard_map/ppermute | solution.py:18
  32.8 4.4 %collective-permute-start.1 = (bf16[16,2048]{1,0:T(8,128)(2,1)S(1)}, bf16[16,2048]{1,0:T(8,128)(2,1)S(1)}, u32[]{:S(2)}, u32[]{:S(2)}) collective-permute-start(bf16[16,2048]{1,0:T(8,128)(2,1)S(1)} %get-tuple-element.27), channel_id=1, source_target_pairs={{0,4},{4,8},{8,12},{1,5},{5,9},{9,13},{2,6},{6,10},{10,14},{3,7},{... | collective-permute-start | bytes 196616 | tf_op jit(solution)/shard_map/ppermute | solution.py:18

commit v3 on v0

v3 whole, which is shorter than its diff:
```python
import functools

import jax
import jax.numpy as jnp
from jax import lax
from jax.experimental import pallas as pl
from jax.experimental.pallas import tpu as pltpu
from jax.sharding import PartitionSpec as P

F32 = jnp.float32
BF16 = jnp.bfloat16
WIDE = 256
CHUNK = 16


def shifted(array, axis, by):
    peers = lax.axis_size(axis)
    pairs = [(i, i + by) for i in range(peers) if 0 <= i + by < peers]
    return lax.ppermute(array, axis, pairs)


def iota(shape, dim):
    return lax.broadcasted_iota(jnp.int32, shape, dim)


def dot(a, b):
    return jnp.dot(a, b, preferred_element_type=F32)


def same_group(width, dtype):
    rows, cols = iota((WIDE, WIDE), 0), iota((WIDE, WIDE), 1)
    return jnp.where(rows // width == cols // width, 1.0, 0.0).astype(F32).astype(dtype)


def spread(compact, mask):
    copies = WIDE // compact.shape[0]
    return jnp.concatenate([compact] * copies, axis=0) * mask


def split(array):
    upper = array.astype(BF16)
    return upper, (array - upper.astype(F32)).astype(BF16)


def one_minus_exp(x):
    series = 1.0 - x / 7.0
    for n in (6.0, 5.0, 4.0, 3.0, 2.0):
        series = 1.0 - x / n * series
    return jnp.where(x < 0.25, x * series, 1.0 - jnp.exp(-x))


def expand_groups(per_group, first_group, width, precision=None):
    groups = per_group.shape[1]
    pick = iota((groups, WIDE), 1) // width + first_group == iota((groups, WIDE), 0)
    return jnp.dot(per_group, pick.astype(F32).astype(per_group.dtype), precision=precision, preferred_element_type=F32)


def pipelined(steps, *stages):
    for turn in range(steps + len(stages) - 1):
        for lag, stage in enumerate(stages):
            if 0 <= turn - lag < steps:
                i = turn - lag
                stage(i, slice(i * WIDE, (i + 1) * WIDE))


def rates_along(rates, width):
    on_diagonal = iota(rates.shape, 0) == iota(rates.shape, 1) % width
    return jnp.sum(jnp.where(on_diagonal, rates, 0.0), axis=0, keepdims=True)


def pole_sums(ends, u, fold_ref, poles):
    every = dot(ends, u)
    parts = []
    lanes = 128
    for at in range(0, WIDE, lanes):
        own = every[at : at + lanes, at : at + lanes] * fold_ref[at : at + lanes, at : at + lanes]
        parts.append(functools.reduce(jnp.add, [own[p : p + poles] for p in range(0, lanes, poles)]))
    return jnp.concatenate(parts, axis=1)


def local_kernel(
    q_hbm, k_hbm, v_hbm, kli_hbm, taps_hbm, rate_hbm,
    mr_ref, part_ref, ulate_ref, late_ref, first_ref, taptab_ref, ends_ref, decay_ref, q_ref, kli_ref,
    k_ref, v_ref, taps_ref, rate_ref, mask_ref, fold_ref, acc_ref, in_sem, small_sem,
):
    rows, channels = k_hbm.shape
    groups, tap_count = taps_hbm.shape
    steps = channels // WIDE
    width = channels // groups
    wide_groups = WIDE // width
    poles = rate_hbm.shape[0]
    half = tap_count
    block = 2 * WIDE

    small = (
        pltpu.make_async_copy(taps_hbm, taps_ref, small_sem.at[0]),
        pltpu.make_async_copy(rate_hbm, rate_ref, small_sem.at[1]),
    )
    for copy in small:
        copy.start()

    def fetch(n):
        at = slice(n * block, (n + 1) * block)
        pairs = ((k_hbm, k_ref), (v_hbm, v_ref), (q_hbm, q_ref), (kli_hbm, kli_ref))
        return [pltpu.make_async_copy(a.at[:, at], b.at[:, at], in_sem.at[m, n]) for m, (a, b) in enumerate(pairs)]

    blocks = [fetch(n) for n in range(channels // block)]
    for copies in blocks:
        for copy in copies:
            copy.start()

    mask_ref[...] = same_group(width, BF16)
    fold_ref[...] = same_group(width, F32)
    for copy in small:
        copy.wait()

    def tables(i, at):
        lane_item = iota((tap_count + width, WIDE), 1) % width
        own = slice(i * wide_groups, (i + 1) * wide_groups)
        pick = (iota((wide_groups, WIDE), 1) // width == iota((wide_groups, WIDE), 0)).astype(F32).astype(BF16)
        table = lax.dot_general(taps_ref[own, :], pick, (((0,), (0,)), ((), ())), preferred_element_type=F32)
        table = jnp.concatenate([table, jnp.zeros((width, WIDE), F32)], axis=0)
        step = 1
        while step < width:
            table = jnp.where((lane_item & step) != 0, pltpu.roll(table, step, 0), table)
            step *= 2
        taptab_ref[:, at] = table.astype(BF16)
        rates = expand_groups(rate_ref[...], i * wide_groups, width, lax.Precision.HIGHEST)
        decay_ref[:, at] = jnp.exp(-rates * half)
        left = half - 1.0 - iota((half, WIDE), 0).astype(F32)
        ends_ref[at, :] = jnp.transpose(jnp.exp(-rates_along(rates, width) * left)).astype(BF16)

    def convolve(i, at):
        if i * WIDE % block == 0:
            for copy in blocks[i * WIDE // block]:
                copy.wait()
        mask = mask_ref[...]
        u = k_ref[:, at] * v_ref[:, at]
        acc_ref[:, at] = jnp.zeros((rows, WIDE), F32)
        for first in range(0, rows, width):
            count = min(tap_count + width, rows - first)
            acc_ref[first : first + count, at] += dot(taptab_ref[:count, at], spread(u[first : first + width], mask))

    def gate(i, at):
        early, late = acc_ref[:half, at], acc_ref[half:, at]
        part_ref[:, at] = early
        mr = (q_ref[half:, at].astype(F32) * late).astype(BF16)
        mr_ref[:, at] = mr
        u_late = mr * kli_ref[half:, at]
        ulate_ref[:, at] = u_late
        u_early = (q_ref[:half, at].astype(F32) * early).astype(BF16) * kli_ref[:half, at]
        ends = ends_ref[at, :]
        late_state = pole_sums(ends, u_late, fold_ref, poles)
        early_state = pole_sums(ends, u_early, fold_ref, poles)
        late_ref[:, at] = late_state
        first_ref[:, at] = (late_state + early_state * decay_ref[:, at]).astype(BF16)

    pipelined(steps, tables, convolve, gate)


def near_rows(u_ref, litab_ref, near_ref, mask_ref, width):
    half = u_ref.shape[0]

    def work(i, at):
        mask = mask_ref[...]
        near_ref[:, at] = jnp.zeros((half, WIDE), F32)
        u = u_ref[:, at]
        for first in range(0, half, width):
            near_ref[first:half, at] += dot(litab_ref[: half - first, at], spread(u[first : first + width], mask))

    return work


def filter_kernel(
    qli_hbm, rate_hbm, residue_hbm, ulate_ref,
    near_ref, litab_ref, powers_ref, decay_ref, scale_ref, qli_ref,
    rate_ref, residue_ref, mask_ref, sem,
):
    half, channels = ulate_ref.shape
    poles, groups = rate_hbm.shape
    steps = channels // WIDE
    width = channels // groups
    wide_groups = WIDE // width
    copies = (
        pltpu.make_async_copy(rate_hbm, rate_ref, sem.at[0]),
        pltpu.make_async_copy(residue_hbm, residue_ref, sem.at[1]),
        pltpu.make_async_copy(qli_hbm, qli_ref, sem.at[2]),
    )
    for copy in copies:
        copy.start()
    mask_ref[...] = same_group(width, BF16)
    for copy in copies[:2]:
        copy.wait()

    def tables(i, at):
        mask = mask_ref[...]
        rates = expand_groups(rate_ref[...], i * wide_groups, width, lax.Precision.HIGHEST)
        residue = expand_groups(residue_ref[...], i * wide_groups, width, lax.Precision.HIGHEST)
        scale = residue * jnp.sqrt(one_minus_exp(2.0 * rates))
        decay_ref[:, at] = jnp.exp(-rates * half)
        scale_ref[:, at] = scale
        item = (iota((poles, WIDE), 1) % width).astype(F32)
        times = iota((half, WIDE), 0).astype(F32)
        rate_row = rates_along(rates, width)
        power = jnp.exp(-rate_row * times)
        powers_ref[:, at] = (power * jnp.exp(-rate_row)).astype(BF16)
        power_hi, power_lo = split(power)
        lift_hi, lift_lo = split(scale * jnp.exp(rates * item))
        lift_hi, lift_lo = spread(lift_hi, mask), spread(lift_lo, mask)
        li_taps = dot(power_hi, lift_hi) + dot(power_hi, lift_lo) + dot(power_lo, lift_hi)
        causal = iota((half, WIDE), 0) >= iota((half, WIDE), 1) % width
        litab_ref[:, at] = jnp.where(causal, li_taps, 0.0).astype(BF16)

    pipelined(steps, tables, near_rows(ulate_ref, litab_ref, near_ref, mask_ref, width))
    copies[2].wait()


def rim_kernel(
    rim_ref, part_ref, q_ref, kli_ref, taptab_ref, ends_ref, decay_ref, late_ref, before_ref,
    mr_ref, u_ref, early_ref, total_ref,
    mask_ref, fold_ref, acc_ref,
):
    half, channels = rim_ref.shape
    width = taptab_ref.shape[0] - half
    poles = late_ref.shape[0]
    mask_ref[...] = same_group(width, BF16)
    fold_ref[...] = same_group(width, F32)

    def convolve(i, at):
        mask = mask_ref[...]
        rim = rim_ref[:, at]
        acc_ref[:, at] = part_ref[:, at]
        for first in range(0, half, width):
            acc_ref[: first + width, at] += dot(taptab_ref[half - first :, at], spread(rim[first : first + width], mask))

    def gate(i, at):
        decay = decay_ref[:, at]
        mr = (q_ref[:half, at].astype(F32) * acc_ref[:, at]).astype(BF16)
        mr_ref[:, at] = mr
        u = mr * kli_ref[:half, at]
        u_ref[:, at] = u
        state = pole_sums(ends_ref[at, :], u, fold_ref, poles)
        early_ref[:, at] = state
        entered = before_ref[:, at].astype(F32) * decay
        total_ref[:, at] = (late_ref[:, at] + (state + entered) * decay).astype(BF16)

    pipelined(channels // WIDE, convolve, gate)


def near_kernel(mr_early_ref, mr_late_ref, u_ref, litab_ref, mr_hbm, near_ref, mask_ref, sem):
    half, channels = u_ref.shape
    copies = (
        pltpu.make_async_copy(mr_early_ref, mr_hbm.at[:half], sem.at[0]),
        pltpu.make_async_copy(mr_late_ref, mr_hbm.at[half:], sem.at[1]),
    )
    for copy in copies:
        copy.start()
    mask_ref[...] = same_group(CHUNK, BF16)
    pipelined(channels // WIDE, near_rows(u_ref, litab_ref, near_ref, mask_ref, CHUNK))
    for copy in copies:
        copy.wait()


def far_kernel(one_before, *refs):
    (
        q_ref, near_early_ref, near_late_ref, early_ref, powers_ref, decay_ref, scale_ref,
        out_hbm, out_ref, mask_ref, out_sem,
    ) = refs[-11:]
    arrived = refs[one_before:-11]
    half, channels = powers_ref.shape
    steps = channels // WIDE

    def put(i, at):
        return pltpu.make_async_copy(out_ref.at[:, at], out_hbm.at[:, at], out_sem.at[i])

    mask_ref[...] = same_group(early_ref.shape[0], BF16)

    def work(i, at):
        mask = mask_ref[...]
        scale = scale_ref[:, at]
        decay = decay_ref[:, at]
        entering = arrived[-1][:, at].astype(F32)
        for ref in arrived[-2::-1]:
            entering = entering * (decay * decay) + ref[:, at].astype(F32)
        if one_before:
            entering = entering + refs[0][:, at].astype(F32)
        middle = entering * decay + early_ref[:, at]
        powers = powers_ref[:, at]
        for first, state, near_ref in ((0, entering, near_early_ref), (half, middle, near_late_ref)):
            far = dot(powers, spread((state * scale).astype(BF16), mask))
            gate = q_ref[first : first + half, at].astype(F32)
            out_ref[first : first + half, at] = (gate * (near_ref[:, at] + far)).astype(BF16)
        put(i, at).start()

    pipelined(steps, work)
    for i in range(steps):
        put(i, slice(i * WIDE, (i + 1) * WIDE)).wait()


def body(q_mr, k_mr, v_mr, q_li, k_li, mr_taps, li_rate, li_residue):
    rows, channels = q_mr.shape
    groups, tap_count = mr_taps.shape
    poles = li_rate.shape[1]
    width = channels // groups
    half = tap_count
    assert rows == 2 * half and poles == width == CHUNK
    steps = channels // WIDE
    params = pltpu.CompilerParams(vmem_limit_bytes=40 * 1024 * 1024)
    vmem, hbm = pl.BlockSpec(memory_space=pltpu.VMEM), pl.BlockSpec(memory_space=pl.ANY)
    in_hbm = lambda *arrays: [pltpu.with_memory_space_constraint(array, pltpu.HBM) for array in arrays]
    dma = pltpu.SemaphoreType.DMA
    mask, fold = pltpu.VMEM((WIDE, WIDE), BF16), pltpu.VMEM((WIDE, WIDE), F32)
    pole_sum, short, tall = (poles, channels), (half, channels), (rows, channels)

    def call(kernel, name, ins, outs, scratch, flops, *operands):
        return pl.pallas_call(
            kernel,
            in_specs=ins,
            out_specs=[hbm if isinstance(out, jax.ShapeDtypeStruct) else vmem for out in outs],
            out_shape=outs,
            scratch_shapes=scratch,
            cost_estimate=pl.CostEstimate(flops=flops, bytes_accessed=4 * 2**20, transcendentals=10**5),
            compiler_params=params,
            name=name,
        )(*operands)

    rim = shifted(k_mr[half:] * v_mr[half:], "ctx", 1)

    mr_late, part, u_late, late, first, taptab, ends, decay, q, kli = call(
        local_kernel,
        "local_rows",
        [hbm] * 6,
        [
            pltpu.VMEM(short, BF16),
            pltpu.VMEM(short, F32),
            pltpu.VMEM(short, BF16),
            pltpu.VMEM(pole_sum, F32),
            pltpu.VMEM(pole_sum, BF16),
            pltpu.VMEM((half + width, channels), BF16),
            pltpu.VMEM((channels, half), BF16),
            pltpu.VMEM(pole_sum, F32),
            pltpu.VMEM(tall, BF16),
            pltpu.VMEM(tall, BF16),
        ],
        [
            pltpu.VMEM(tall, BF16),
            pltpu.VMEM(tall, BF16),
            pltpu.VMEM((groups, tap_count), BF16),
            pltpu.VMEM((poles, groups), F32),
            mask,
            fold,
            pltpu.VMEM(tall, F32),
            dma((4, steps)),
            dma((2,)),
        ],
        4 * 10**9,
        *in_hbm(q_mr, k_mr, v_mr, k_li, mr_taps, li_rate.T),
    )

    peers = lax.axis_size("ctx")
    send = lambda array, pairs: lax.ppermute(array, "ctx", pairs)
    before = send(first, [(0, 1)]) if peers == 4 else jnp.zeros(pole_sum, BF16)

    near_late, litab, powers, decay, scale, qli = call(
        filter_kernel,
        "filter_tables",
        [hbm] * 3 + [vmem],
        [
            pltpu.VMEM(short, F32),
            pltpu.VMEM(short, BF16),
            pltpu.VMEM(short, BF16),
            pltpu.VMEM(pole_sum, F32),
            pltpu.VMEM(pole_sum, F32),
            pltpu.VMEM(tall, BF16),
        ],
        [pltpu.VMEM((poles, groups), F32), pltpu.VMEM((poles, groups), F32), mask, dma((3,))],
        2 * 10**9,
        *in_hbm(q_li, li_rate.T, li_residue.T),
        u_late,
    )

    mr_early, u_early, early, total = call(
        rim_kernel,
        "rim_rows",
        [vmem] * 9,
        [pltpu.VMEM(short, BF16), pltpu.VMEM(short, BF16), pltpu.VMEM(pole_sum, F32), pltpu.VMEM(pole_sum, BF16)],
        [mask, fold, pltpu.VMEM(short, F32)],
        2 * 10**9,
        rim, part, q, kli, taptab, ends, decay, late, before,
    )

    if peers == 4:
        next_but_one = send(total, [(1, 3)])
        arrived = [send(total, [(1, 2), (2, 3)]), next_but_one]
    else:
        reach = min(3, max(peers - 1, 1))
        arrived = [shifted(total, "ctx", by) for by in range(1, reach + 1)]
        rates = jnp.repeat(li_rate.T, width, axis=1)
        while reach < peers - 1:
            window = arrived[-1].astype(F32)
            for piece in arrived[-2::-1]:
                window = window * jnp.exp(-rates * rows) + piece.astype(F32)
            merged = window
            for times in (1, 2, 3):
                if times * reach < peers:
                    moved = shifted(window, "ctx", times * reach)
                    merged = merged + moved * jnp.exp(-rates * (rows * reach * times))
            arrived = [merged]
            reach *= 4

    mr_out, near_early = call(
        near_kernel,
        "near_part",
        [vmem] * 4,
        [jax.ShapeDtypeStruct(tall, BF16), pltpu.VMEM(short, F32)],
        [mask, dma((2,))],
        2 * 10**9,
        mr_early, mr_late, u_early, litab,
    )

    if peers == 4:
        arrived = [before] + arrived
    (li_out,) = call(
        functools.partial(far_kernel, peers == 4),
        "far_rows",
        [vmem] * (len(arrived) + 7),
        [jax.ShapeDtypeStruct(tall, BF16)],
        [pltpu.VMEM(tall, BF16), mask, dma((steps,))],
        10**9,
        *arrived, qli, near_early, near_late, early, powers, decay, scale,
    )
    return (mr_out, li_out)


def solution(mesh):
    seq = P(("rep", "ctx"), "tp")
    in_specs = (seq, seq, seq, seq, seq, P("tp", None), P("tp", None), P("tp", None))
    return jax.shard_map(body, mesh=mesh, in_specs=in_specs, out_specs=(seq, seq), check_vma=False)
```

time: 295 us -> 29.7 us (0.10)
  the two profiles are of different devices: /device:TPU:0 before, /device:TPU:18 now
where the time goes in v3:
time: 29.7 us; the launch traced here: 29.4 us
  Pallas kernels  17.2 us (58%)
  starting transfers between devices  8.16 us (27%)
  waiting for transfers between devices  2.15 us (7%)
  other arithmetic  1.26 us (4%)
  between operations  0.71 us (2%)
    pallas_call x5, Pallas kernels, call(): pl.pallas_call(kernel, in_specs=ins, out_specs=[hbm if isinstance(out, ja...  17.2 us
    ppermute x3, starting transfers between devices, body(): send = lambda array, pairs: lax.ppermute(array, 'ctx', pairs)  4.68 us
    ppermute x1, starting transfers between devices, shifted(): return lax.ppermute(array, axis, pairs)  3.48 us
    ppermute x3, waiting for transfers between devices, body(): send = lambda array, pairs: lax.ppermute(array, 'ctx', pairs)  2.14 us
    mul x1, other arithmetic, body(): rim = shifted(k_mr[half:] * v_mr[half:], 'ctx', 1)  1.26 us
  transfers between devices with their start and end apart: 4, of which 1 were waited for; matrix products, arithmetic and copies ran while one was open for 0% of the time, Pallas kernels for 46%

profile of v3, /device:TPU:18, one launch (start us, length us, event | category | flops | bytes accessed | tf_op | source)
XLA Modules:
  0.0 29.4 jit_solution(3570063875943596566)
XLA Ops:
  0.6 1.3 %slice_multiply_fusion = bf16[128,2048]{1,0:T(8,128)(2,1)S(1)} fusion(bf16[256,2048]{1,0:T(8,128)(2,1)} %v_hbm.1, bf16[256,2048]{1,0:T(8,128)(2,1)} %k_hbm.1), kind=kLoop, calls=%fused_computation | loop fusion | flops 262144 | bytes 1572864 | tf_op jit(solution)/shard_map/mul | solution.py:327
  1.9 3.5 %collective-permute-start = (bf16[128,2048]{1,0:T(8,128)(2,1)S(1)}, bf16[128,2048]{1,0:T(8,128)(2,1)S(1)}, u32[]{:S(2)}, u32[]{:S(2)}) collective-permute-start(bf16[128,2048]{1,0:T(8,128)(2,1)S(1)} %slice_multiply_fusion), channel_id=1, source_target_pairs={{0,4},{4,8},{8,12},{1,5},{5,9},{9,13},{2,6},{6,10},{10,14},{3,7},{... | collective-permute-start | bytes 1572872 | tf_op jit(solution)/shard_map/ppermute | solution.py:19
  5.4 7.9 %local_rows.1 = (bf16[128,2048]{1,0:T(8,128)(2,1)S(1)}, f32[128,2048]{1,0:T(8,128)S(1)}, bf16[128,2048]{1,0:T(8,128)(2,1)S(1)}, f32[16,2048]{1,0:T(8,128)S(1)}, ...) custom-call(bf16[256,2048]{1,0:T(8,128)(2,1)} %q_hbm.1, ...), custom_call_target="tpu_custom_call" | custom-call | flops 4000000000 | bytes 4194304 | tf_op jit(solution)/shard_map/local_rows/pallas_call | solution.py:316
  13.3 0.7 %collective-permute-start.1 = (bf16[16,2048]{1,0:T(8,128)(2,1)S(1)}, bf16[16,2048]{1,0:T(8,128)(2,1)S(1)}, u32[]{:S(2)}, u32[]{:S(2)}) collective-permute-start(bf16[16,2048]{1,0:T(8,128)(2,1)S(1)} %get-tuple-element.31), channel_id=1, source_target_pairs={{0,4},{1,5},{2,6},{3,7},{16,20},{17,21},{18,22},{19,23}} | collective-permute-start | bytes 196616 | tf_op jit(solution)/shard_map/ppermute | solution.py:361
  14.0 4.2 %filter_tables.1 = (f32[128,2048]{1,0:T(8,128)S(1)}, bf16[128,2048]{1,0:T(8,128)(2,1)S(1)}, bf16[128,2048]{1,0:T(8,128)(2,1)S(1)}, f32[16,2048]{1,0:T(8,128)S(1)...) custom-call(bf16[256,2048]{1,0:T(8,128)(2,1)} %qli_hbm.1, f32[16,128]{1,0:T(8,128)} %bitcast.3, ...), custom_call_target="tpu_custom_call" | custom-call | flops 2000000000 | bytes 4194304 | tf_op jit(solution)/shard_map/filter_tables/pallas_call | solution.py:316
  18.2 0.0 collective-permute-done.1.before_ref.refs_0_
  18.2 0.0 collective-permute-done.rim_ref
  18.2 2.2 %rim_rows.1 = (bf16[128,2048]{1,0:T(8,128)(2,1)S(1)}, bf16[128,2048]{1,0:T(8,128)(2,1)S(1)}, f32[16,2048]{1,0:T(8,128)S(1)}, bf16[16,2048]{1,0:T(8,128)(2,1)S(1)}) custom-call(bf16[128,2048]{1,0:T(8,128)(2,1)S(1)} %collective-permute-done.rim_ref, f32[128,2048]{1,0:T(8,128)S(1)} %get-tuple-element.23.part_ref, ...), custom_call_target="tpu_custom_call" | custom-call | flops 2000000000 | bytes 4194304 | tf_op jit(solution)/shard_map/rim_rows/pallas_call | solution.py:316
  20.5 0.7 %collective-permute-start.3 = (bf16[16,2048]{1,0:T(8,128)(2,1)S(1)}, bf16[16,2048]{1,0:T(8,128)(2,1)S(1)}, u32[]{:S(2)}, u32[]{:S(2)}) collective-permute-start(bf16[16,2048]{1,0:T(8,128)(2,1)S(1)} %get-tuple-element.37), channel_id=1, source_target_pairs={{4,12},{5,13},{6,14},{7,15},{20,28},{21,29},{22,30},{23,31}} | collective-permute-start | bytes 196616 | tf_op jit(solution)/shard_map/ppermute | solution.py:361
  21.1 3.3 %collective-permute-start.2 = (bf16[16,2048]{1,0:T(8,128)(2,1)S(1)}, bf16[16,2048]{1,0:T(8,128)(2,1)S(1)}, u32[]{:S(2)}, u32[]{:S(2)}) collective-permute-start(bf16[16,2048]{1,0:T(8,128)(2,1)S(1)} %get-tuple-element.37), channel_id=1, source_target_pairs={{4,8},{8,12},{5,9},{9,13},{6,10},{10,14},{7,11},{11,15},{20,24},{2... | collective-permute-start | bytes 196616 | tf_op jit(solution)/shard_map/ppermute | solution.py:361
  24.5 1.5 %near_part.1 = (bf16[256,2048]{1,0:T(8,128)(2,1)}, f32[128,2048]{1,0:T(8,128)S(1)}) custom-call(bf16[128,2048]{1,0:T(8,128)(2,1)S(1)} %get-tuple-element.32.mr_early_ref, bf16[128,2048]{1,0:T(8,128)(2,1)S(1)} %get-tuple-element.33.mr_late_ref, bf16[128,2048]{1,0:T(8,128)(2,1)S(1)} %get-tuple-element.34.u_ref, bf16[128,2048]{1,0:T(8,128)(2,1)S(1)} %get-tuple-element.35.litab_ref), custom_call_target="tpu_custom_call" | custom-call | flops 2000000000 | bytes 4194304 | tf_op jit(solution)/shard_map/near_part/pallas_call | solution.py:316
  26.0 0.0 collective-permute-done.3.refs_2_
  26.0 2.1 %collective-permute-done.2.refs_1_ = bf16[16,2048]{1,0:T(8,128)(2,1)S(1)} collective-permute-done((bf16[16,2048]{1,0:T(8,128)(2,1)S(1)}, bf16[16,2048]{1,0:T(8,128)(2,1)S(1)}, u32[]{:S(2)}, u32[]{:S(2)}) %collective-permute-start.2) | collective-permute-done | bytes 65568 | tf_op jit(solution)/shard_map/ppermute | solution.py:361
  28.2 1.3 %far_rows.1 = bf16[256,2048]{1,0:T(8,128)(2,1)} custom-call(bf16[16,2048]{1,0:T(8,128)(2,1)S(1)} %collective-permute-done.1.before_ref.refs_0_, bf16[16,2048]{1,0:T(8,128)(2,1)S(1)} %collective-permute-done.2.refs_1_, bf16[16,2048]{1,0:T(8,128)(2,1)S(1)} %collective-permute-done.3.refs_2_, bf16[256,2048]{1,0:T(8,128)(2,1)S(1)} %get-tuple-element.38.refs_3_, ...), custom_call_target="tpu_custom_call" | custom-call | flops 1000000000 | bytes 4194304 | tf_op jit(solution)/shard_map/far_rows/pallas_call | solution.py:316
Async XLA Ops:
  1.9 16.3 %collective-permute-start = (bf16[128,2048]{1,0:T(8,128)(2,1)S(1)}, bf16[128,2048]{1,0:T(8,128)(2,1)S(1)}, u32[]{:S(2)}, u32[]{:S(2)}) collective-permute-start(bf16[128,2048]{1,0:T(8,128)(2,1)S(1)} %slice_multiply_fusion), channel_id=1, source_target_pairs={{0,4},{4,8},{8,12},{1,5},{5,9},{9,13},{2,6},{6,10},{10,14},{3,7},{... | collective-permute-start | bytes 1572872 | tf_op jit(solution)/shard_map/ppermute | solution.py:19
  13.3 4.9 %collective-permute-start.1 = (bf16[16,2048]{1,0:T(8,128)(2,1)S(1)}, bf16[16,2048]{1,0:T(8,128)(2,1)S(1)}, u32[]{:S(2)}, u32[]{:S(2)}) collective-permute-start(bf16[16,2048]{1,0:T(8,128)(2,1)S(1)} %get-tuple-element.31), channel_id=1, source_target_pairs={{0,4},{1,5},{2,6},{3,7},{16,20},{17,21},{18,22},{19,23}} | collective-permute-start | bytes 196616 | tf_op jit(solution)/shard_map/ppermute | solution.py:361
  20.5 5.6 %collective-permute-start.3 = (bf16[16,2048]{1,0:T(8,128)(2,1)S(1)}, bf16[16,2048]{1,0:T(8,128)(2,1)S(1)}, u32[]{:S(2)}, u32[]{:S(2)}) collective-permute-start(bf16[16,2048]{1,0:T(8,128)(2,1)S(1)} %get-tuple-element.37), channel_id=1, source_target_pairs={{4,12},{5,13},{6,14},{7,15},{20,28},{21,29},{22,30},{23,31}} | collective-permute-start | bytes 196616 | tf_op jit(solution)/shard_map/ppermute | solution.py:361
  21.1 7.0 %collective-permute-start.2 = (bf16[16,2048]{1,0:T(8,128)(2,1)S(1)}, bf16[16,2048]{1,0:T(8,128)(2,1)S(1)}, u32[]{:S(2)}, u32[]{:S(2)}) collective-permute-start(bf16[16,2048]{1,0:T(8,128)(2,1)S(1)} %get-tuple-element.37), channel_id=1, source_target_pairs={{4,8},{8,12},{5,9},{9,13},{6,10},{10,14},{7,11},{11,15},{20,24},{2... | collective-permute-start | bytes 196616 | tf_op jit(solution)/shard_map/ppermute | solution.py:361

commit v4 on v3

--- a/solution.py
+++ b/solution.py
@@ -79,9 +79,10 @@
 
 
 def local_kernel(
-    q_hbm, k_hbm, v_hbm, kli_hbm, taps_hbm, rate_hbm,
+    tail_ref, q_hbm, k_hbm, v_hbm, kli_hbm, taps_hbm, rate_hbm,
     mr_ref, part_ref, ulate_ref, late_ref, first_ref, taptab_ref, ends_ref, decay_ref, q_ref, kli_ref,
-    k_ref, v_ref, taps_ref, rate_ref, mask_ref, fold_ref, acc_ref, in_sem, small_sem,
+    mr_early_ref, u_early_ref, early_ref,
+    k_ref, v_ref, taps_ref, rate_ref, mask_ref, fold_ref, acc_ref, in_sem,
 ):
     rows, channels = k_hbm.shape
     groups, tap_count = taps_hbm.shape
@@ -90,28 +91,18 @@
     wide_groups = WIDE // width
     poles = rate_hbm.shape[0]
     half = tap_count
-    block = 2 * WIDE
-
-    small = (
-        pltpu.make_async_copy(taps_hbm, taps_ref, small_sem.at[0]),
-        pltpu.make_async_copy(rate_hbm, rate_ref, small_sem.at[1]),
-    )
-    for copy in small:
+
+    pairs = (
+        (taps_hbm, taps_ref), (rate_hbm, rate_ref),
+        (k_hbm.at[:half], k_ref), (v_hbm.at[:half], v_ref), (q_hbm, q_ref), (kli_hbm, kli_ref),
+    )
+    copies = [pltpu.make_async_copy(a, b, in_sem.at[n]) for n, (a, b) in enumerate(pairs)]
+    for copy in copies:
         copy.start()
-
-    def fetch(n):
-        at = slice(n * block, (n + 1) * block)
-        pairs = ((k_hbm, k_ref), (v_hbm, v_ref), (q_hbm, q_ref), (kli_hbm, kli_ref))
-        return [pltpu.make_async_copy(a.at[:, at], b.at[:, at], in_sem.at[m, n]) for m, (a, b) in enumerate(pairs)]
-
-    blocks = [fetch(n) for n in range(channels // block)]
-    for copies in blocks:
-        for copy in copies:
-            copy.start()
 
     mask_ref[...] = same_group(width, BF16)
     fold_ref[...] = same_group(width, F32)
-    for copy in small:
+    for copy in copies[:2]:
         copy.wait()
 
     def tables(i, at):
@@ -130,16 +121,20 @@
         left = half - 1.0 - iota((half, WIDE), 0).astype(F32)
         ends_ref[at, :] = jnp.transpose(jnp.exp(-rates_along(rates, width) * left)).astype(BF16)
 
-    def convolve(i, at):
-        if i * WIDE % block == 0:
-            for copy in blocks[i * WIDE // block]:
-                copy.wait()
+    def convolve_late(i, at):
+        mask = mask_ref[...]
+        acc_ref[half:, at] = jnp.zeros((rows - half, WIDE), F32)
+        for first in range(half, rows, width):
+            u = tail_ref[first - half : first - half + width, at]
+            acc_ref[first:, at] += dot(taptab_ref[: rows - first, at], spread(u, mask))
+
+    def convolve_early(i, at):
         mask = mask_ref[...]
         u = k_ref[:, at] * v_ref[:, at]
-        acc_ref[:, at] = jnp.zeros((rows, WIDE), F32)
-        for first in range(0, rows, width):
-            count = min(tap_count + width, rows - first)
-            acc_ref[first : first + count, at] += dot(taptab_ref[:count, at], spread(u[first : first + width], mask))
+        acc_ref[:half, at] = jnp.zeros((half, WIDE), F32)
+        for first in range(0, half, width):
+            count = tap_count + width
+            acc_ref[first : first + count, at] += dot(taptab_ref[:, at], spread(u[first : first + width], mask))
 
     def gate(i, at):
         early, late = acc_ref[:half, at], acc_ref[half:, at]
@@ -148,14 +143,22 @@
         mr_ref[:, at] = mr
         u_late = mr * kli_ref[half:, at]
         ulate_ref[:, at] = u_late
-        u_early = (q_ref[:half, at].astype(F32) * early).astype(BF16) * kli_ref[:half, at]
+        mr_early = (q_ref[:half, at].astype(F32) * early).astype(BF16)
+        mr_early_ref[:, at] = mr_early
+        u_early = mr_early * kli_ref[:half, at]
+        u_early_ref[:, at] = u_early
         ends = ends_ref[at, :]
         late_state = pole_sums(ends, u_late, fold_ref, poles)
         early_state = pole_sums(ends, u_early, fold_ref, poles)
         late_ref[:, at] = late_state
+        early_ref[:, at] = early_state
         first_ref[:, at] = (late_state + early_state * decay_ref[:, at]).astype(BF16)
 
-    pipelined(steps, tables, convolve, gate)
+    pipelined(steps, tables)
+    pipelined(steps, convolve_late)
+    for copy in copies[2:]:
+        copy.wait()
+    pipelined(steps, convolve_early, gate)
 
 
 def near_rows(u_ref, litab_ref, near_ref, mask_ref, width):
@@ -172,11 +175,11 @@
 
 
 def filter_kernel(
-    qli_hbm, rate_hbm, residue_hbm, ulate_ref,
-    near_ref, litab_ref, powers_ref, decay_ref, scale_ref, qli_ref,
+    qli_hbm, rate_hbm, residue_hbm,
+    litab_ref, powers_ref, decay_ref, scale_ref, qli_ref,
     rate_ref, residue_ref, mask_ref, sem,
 ):
-    half, channels = ulate_ref.shape
+    half, channels = litab_ref.shape
     poles, groups = rate_hbm.shape
     steps = channels // WIDE
     width = channels // groups
@@ -211,18 +214,16 @@
         causal = iota((half, WIDE), 0) >= iota((half, WIDE), 1) % width
         litab_ref[:, at] = jnp.where(causal, li_taps, 0.0).astype(BF16)
 
-    pipelined(steps, tables, near_rows(ulate_ref, litab_ref, near_ref, mask_ref, width))
+    pipelined(steps, tables)
     copies[2].wait()
 
 
-def rim_kernel(
-    rim_ref, part_ref, q_ref, kli_ref, taptab_ref, ends_ref, decay_ref, late_ref, before_ref,
-    mr_ref, u_ref, early_ref, total_ref,
-    mask_ref, fold_ref, acc_ref,
+def rim_rows(
+    rim_ref, part_ref, q_ref, kli_ref, taptab_ref, ends_ref, mr_ref, u_ref, early_ref, mask_ref, fold_ref, acc_ref
 ):
     half, channels = rim_ref.shape
     width = taptab_ref.shape[0] - half
-    poles = late_ref.shape[0]
+    poles = early_ref.shape[0]
     mask_ref[...] = same_group(width, BF16)
     fold_ref[...] = same_group(width, F32)
 
@@ -234,29 +235,58 @@
             acc_ref[: first + width, at] += dot(taptab_ref[half - first :, at], spread(rim[first : first + width], mask))
 
     def gate(i, at):
-        decay = decay_ref[:, at]
         mr = (q_ref[:half, at].astype(F32) * acc_ref[:, at]).astype(BF16)
         mr_ref[:, at] = mr
         u = mr * kli_ref[:half, at]
         u_ref[:, at] = u
-        state = pole_sums(ends_ref[at, :], u, fold_ref, poles)
-        early_ref[:, at] = state
-        entered = before_ref[:, at].astype(F32) * decay
-        total_ref[:, at] = (late_ref[:, at] + (state + entered) * decay).astype(BF16)
+        early_ref[:, at] = pole_sums(ends_ref[at, :], u, fold_ref, poles)
 
     pipelined(channels // WIDE, convolve, gate)
 
 
-def near_kernel(mr_early_ref, mr_late_ref, u_ref, litab_ref, mr_hbm, near_ref, mask_ref, sem):
+def inner(name):
+    at = lax.axis_index(name)
+    return jnp.logical_and(at > 0, at < lax.axis_size(name) - 1)
+
+
+def rim_kernel(by_place, *refs):
+    if by_place:
+        pl.when(inner("ctx"))(lambda: rim_rows(*refs))
+    else:
+        rim_rows(*refs)
+
+
+def near_kernel(
+    by_place,
+    rim_ref, part_ref, q_ref, kli_ref, taptab_ref, ends_ref,
+    mr_first_ref, u_first_ref, early_first_ref, mr_rim_ref, u_rim_ref, early_rim_ref, mr_late_ref, ulate_ref, litab_ref,
+    early_ref, near_early_ref, near_late_ref, mr_hbm,
+    mr_ref, u_ref, mask_ref, fold_ref, acc_ref, sem,
+):
     half, channels = u_ref.shape
+    steps = channels // WIDE
     copies = (
-        pltpu.make_async_copy(mr_early_ref, mr_hbm.at[:half], sem.at[0]),
-        pltpu.make_async_copy(mr_late_ref, mr_hbm.at[half:], sem.at[1]),
-    )
-    for copy in copies:
-        copy.start()
+        pltpu.make_async_copy(mr_late_ref, mr_hbm.at[half:], sem.at[0]),
+        pltpu.make_async_copy(mr_ref, mr_hbm.at[:half], sem.at[1]),
+    )
+    copies[0].start()
+
+    def take(*sources):
+        for source, target in zip(sources, (mr_ref, u_ref, early_ref)):
+            target[...] = source[...]
+
+    if by_place:
+        own = (rim_ref, part_ref, q_ref, kli_ref, taptab_ref, ends_ref, mr_ref, u_ref, early_ref, mask_ref, fold_ref, acc_ref)
+        place = lax.axis_index("ctx")
+        pl.when(place == 0)(lambda: take(mr_first_ref, u_first_ref, early_first_ref))
+        pl.when(inner("ctx"))(lambda: take(mr_rim_ref, u_rim_ref, early_rim_ref))
+        pl.when(place == lax.axis_size("ctx") - 1)(lambda: rim_rows(*own))
+    else:
+        take(mr_rim_ref, u_rim_ref, early_rim_ref)
+    copies[1].start()
     mask_ref[...] = same_group(CHUNK, BF16)
-    pipelined(channels // WIDE, near_rows(u_ref, litab_ref, near_ref, mask_ref, CHUNK))
+    pipelined(steps, near_rows(ulate_ref, litab_ref, near_late_ref, mask_ref, CHUNK))
+    pipelined(steps, near_rows(u_ref, litab_ref, near_early_ref, mask_ref, CHUNK))
     for copy in copies:
         copy.wait()
 
@@ -324,12 +354,13 @@
             name=name,
         )(*operands)
 
-    rim = shifted(k_mr[half:] * v_mr[half:], "ctx", 1)
-
-    mr_late, part, u_late, late, first, taptab, ends, decay, q, kli = call(
+    tail = k_mr[half:] * v_mr[half:]
+    rim = shifted(tail, "ctx", 1)
+
+    mr_late, part, u_late, late, first, taptab, ends, decay, q, kli, *without_rim = call(
         local_kernel,
         "local_rows",
-        [hbm] * 6,
+        [vmem] + [hbm] * 6,
         [
             pltpu.VMEM(short, BF16),
             pltpu.VMEM(short, F32),
@@ -341,19 +372,22 @@
             pltpu.VMEM(pole_sum, F32),
             pltpu.VMEM(tall, BF16),
             pltpu.VMEM(tall, BF16),
+            pltpu.VMEM(short, BF16),
+            pltpu.VMEM(short, BF16),
+            pltpu.VMEM(pole_sum, F32),
         ],
         [
-            pltpu.VMEM(tall, BF16),
-            pltpu.VMEM(tall, BF16),
+            pltpu.VMEM(short, BF16),
+            pltpu.VMEM(short, BF16),
             pltpu.VMEM((groups, tap_count), BF16),
             pltpu.VMEM((poles, groups), F32),
             mask,
             fold,
             pltpu.VMEM(tall, F32),
-            dma((4, steps)),
-            dma((2,)),
+            dma((6,)),
         ],
         4 * 10**9,
+        tail,
         *in_hbm(q_mr, k_mr, v_mr, k_li, mr_taps, li_rate.T),
     )
 
@@ -361,12 +395,11 @@
     send = lambda array, pairs: lax.ppermute(array, "ctx", pairs)
     before = send(first, [(0, 1)]) if peers == 4 else jnp.zeros(pole_sum, BF16)
 
-    near_late, litab, powers, decay, scale, qli = call(
+    litab, powers, decay, scale, qli = call(
         filter_kernel,
         "filter_tables",
-        [hbm] * 3 + [vmem],
+        [hbm] * 3,
         [
-            pltpu.VMEM(short, F32),
             pltpu.VMEM(short, BF16),
             pltpu.VMEM(short, BF16),
             pltpu.VMEM(pole_sum, F32),
@@ -376,18 +409,20 @@
         [pltpu.VMEM((poles, groups), F32), pltpu.VMEM((poles, groups), F32), mask, dma((3,))],
         2 * 10**9,
         *in_hbm(q_li, li_rate.T, li_residue.T),
-        u_late,
-    )
-
-    mr_early, u_early, early, total = call(
-        rim_kernel,
+    )
+
+    by_place = peers == 4
+    rows_of_rim = (rim, part, q, kli, taptab, ends)
+    with_rim = call(
+        functools.partial(rim_kernel, by_place),
         "rim_rows",
-        [vmem] * 9,
-        [pltpu.VMEM(short, BF16), pltpu.VMEM(short, BF16), pltpu.VMEM(pole_sum, F32), pltpu.VMEM(pole_sum, BF16)],
+        [vmem] * 6,
+        [pltpu.VMEM(short, BF16), pltpu.VMEM(short, BF16), pltpu.VMEM(pole_sum, F32)],
         [mask, fold, pltpu.VMEM(short, F32)],
         2 * 10**9,
-        rim, part, q, kli, taptab, ends, decay, late, before,
-    )
+        *rows_of_rim,
+    )
+    total = (late + (with_rim[2] + before.astype(F32) * decay) * decay).astype(BF16)
 
     if peers == 4:
         next_but_one = send(total, [(1, 3)])
@@ -408,14 +443,14 @@
             arrived = [merged]
             reach *= 4
 
-    mr_out, near_early = call(
-        near_kernel,
+    early, near_early, near_late, mr_out = call(
+        functools.partial(near_kernel, by_place),
         "near_part",
-        [vmem] * 4,
-        [jax.ShapeDtypeStruct(tall, BF16), pltpu.VMEM(short, F32)],
-        [mask, dma((2,))],
+        [vmem] * 15,
+        [pltpu.VMEM(pole_sum, F32), pltpu.VMEM(short, F32), pltpu.VMEM(short, F32), jax.ShapeDtypeStruct(tall, BF16)],
+        [pltpu.VMEM(short, BF16), pltpu.VMEM(short, BF16), mask, fold, pltpu.VMEM(short, F32), dma((2,))],
         2 * 10**9,
-        mr_early, mr_late, u_early, litab,
+        *rows_of_rim, *without_rim, *with_rim, mr_late, u_late, litab,
     )
 
     if peers == 4:

time: 29.7 us -> 28.8 us (0.970)
  the two profiles are of different devices: /device:TPU:18 before, /device:TPU:14 now
where the time goes in v4:
time: 28.8 us; the launch traced here: 28.5 us
  Pallas kernels  15.7 us (55%)
  starting transfers between devices  8.23 us (29%)
  waiting for transfers between devices  2.39 us (8%)
  other arithmetic  1.29 us (4%)
  between operations  0.89 us (3%)
    pallas_call x5, Pallas kernels, call(): pl.pallas_call(kernel, in_specs=ins, out_specs=[hbm if isinstance(out, ja...  15.7 us
    ppermute x3, starting transfers between devices, body(): send = lambda array, pairs: lax.ppermute(array, 'ctx', pairs)  4.74 us
    ppermute x1, starting transfers between devices, shifted(): return lax.ppermute(array, axis, pairs)  3.48 us
    ppermute x1, waiting for transfers between devices, shifted(): return lax.ppermute(array, axis, pairs)  2.39 us
    mul x1, other arithmetic, body(): tail = k_mr[half:] * v_mr[half:]  1.26 us
  transfers between devices with their start and end apart: 4, of which 1 were waited for; matrix products, arithmetic and copies ran while one was open for 0% of the time, Pallas kernels for 51%

profile of v4, /device:TPU:14, one launch (start us, length us, event | category | flops | bytes accessed | tf_op | source)
XLA Modules:
  0.0 28.5 jit_solution(8298854406016138199)
XLA Ops:
  0.6 1.3 %slice_multiply_fusion.tail_ref = bf16[128,2048]{1,0:T(8,128)(2,1)S(1)} fusion(bf16[256,2048]{1,0:T(8,128)(2,1)} %v_hbm.1, bf16[256,2048]{1,0:T(8,128)(2,1)} %k_hbm.1), kind=kLoop, calls=%fused_computation | loop fusion | flops 262144 | bytes 1572864 | tf_op jit(solution)/shard_map/mul | solution.py:357
  1.9 3.5 %collective-permute-start = (bf16[128,2048]{1,0:T(8,128)(2,1)S(1)}, bf16[128,2048]{1,0:T(8,128)(2,1)S(1)}, u32[]{:S(2)}, u32[]{:S(2)}) collective-permute-start(bf16[128,2048]{1,0:T(8,128)(2,1)S(1)} %slice_multiply_fusion.tail_ref), channel_id=1, source_target_pairs={{0,4},{4,8},{8,12},{1,5},{5,9},{9,13},{2,6},{6,10},{10,14},{3,7},{... | collective-permute-start | bytes 1572872 | tf_op jit(solution)/shard_map/ppermute | solution.py:19
  5.4 6.0 %local_rows.1 = (bf16[128,2048]{1,0:T(8,128)(2,1)S(1)}, f32[128,2048]{1,0:T(8,128)S(1)}, bf16[128,2048]{1,0:T(8,128)(2,1)S(1)}, f32[16,2048]{1,0:T(8,128)S(1)}, ...) custom-call(bf16[128,2048]{1,0:T(8,128)(2,1)S(1)} %slice_multiply_fu, ...), custom_call_target="tpu_custom_call" | custom-call | flops 4000000000 | bytes 4194304 | tf_op jit(solution)/shard_map/local_rows/pallas_call | solution.py:346
  11.4 1.3 %collective-permute-start.1 = (bf16[16,2048]{1,0:T(8,128)(2,1)S(1)}, bf16[16,2048]{1,0:T(8,128)(2,1)S(1)}, u32[]{:S(2)}, u32[]{:S(2)}) collective-permute-start(bf16[16,2048]{1,0:T(8,128)(2,1)S(1)} %get-tuple-element.41), channel_id=1, source_target_pairs={{0,4},{1,5},{2,6},{3,7},{16,20},{17,21},{18,22},{19,23}} | collective-permute-start | bytes 196616 | tf_op jit(solution)/shard_map/ppermute | solution.py:395
  12.7 3.1 %filter_tables.1 = (bf16[128,2048]{1,0:T(8,128)(2,1)S(1)}, bf16[128,2048]{1,0:T(8,128)(2,1)S(1)}, f32[16,2048]{1,0:T(8,128)S(1)}, f32[16,2048]{1,0:T(8,128)S(1)}, bf16[256,2048]{1,0:T(8,128)(2,1)S(1)}) custom-call(bf16[256,2048]{1,0:T(8,128)(2,1)} %qli_hbm.1, f32[16,128]{1,0:T(8,128)} %bitcast.3, f32[16,128]{1,0:T(8,128)} %bitcast.4), custom_call_target="tpu_custom_call" | custom-call | flops 2000000000 | bytes 4194304 | tf_op jit(solution)/shard_map/filter_tables/pallas_call | solution.py:346
  15.8 2.4 %collective-permute-done.refs_0_.rim_ref = bf16[128,2048]{1,0:T(8,128)(2,1)S(1)} collective-permute-done((bf16[128,2048]{1,0:T(8,128)(2,1)S(1)}, bf16[128,2048]{1,0:T(8,128)(2,1)S(1)}, u32[]{:S(2)}, u32[]{:S(2)}) %collective-permute-start) | collective-permute-done | bytes 524320 | tf_op jit(solution)/shard_map/ppermute | solution.py:19
  18.1 2.2 %rim_rows.1 = (bf16[128,2048]{1,0:T(8,128)(2,1)S(1)}, bf16[128,2048]{1,0:T(8,128)(2,1)S(1)}, f32[16,2048]{1,0:T(8,128)S(1)}) custom-call(bf16[128,2048]{1,0:T(8,128)(2,1)S(1)} %collective-permute-done.refs_0_.rim_ref, f32[128,2048]{1,0:T(8,128)S(1)} %get-tuple-element.26.refs_1_.part_ref, bf16[256,2048]{1,0:T(8,128)(2,1)S(1)} %get-tuple-element.27.refs_2_.q_ref, ...), custom_call_target="tpu_custom_call" | custom-call | flops 2000000000 | bytes 4194304 | tf_op jit(solution)/shard_map/rim_rows/pallas_call | solution.py:346
  20.4 0.0 collective-permute-done.1.refs_0_
  20.4 1.6 %collective-permute-start.3 = (bf16[16,2048]{1,0:T(8,128)(2,1)S(1)}, bf16[16,2048]{1,0:T(8,128)(2,1)S(1)}, u32[]{:S(2)}, u32[]{:S(2)}) collective-permute-start(bf16[16,2048]{1,0:T(8,128)(2,1)S(1)} %add_convert_fusion), channel_id=1, source_target_pairs={{4,12},{5,13},{6,14},{7,15},{20,28},{21,29},{22,30},{23,31}} | collective-permute-start | bytes 196616 | tf_op jit(solution)/shard_map/ppermute | solution.py:395
  22.0 1.9 %collective-permute-start.2 = (bf16[16,2048]{1,0:T(8,128)(2,1)S(1)}, bf16[16,2048]{1,0:T(8,128)(2,1)S(1)}, u32[]{:S(2)}, u32[]{:S(2)}) collective-permute-start(bf16[16,2048]{1,0:T(8,128)(2,1)S(1)} %add_convert_fusion), channel_id=1, source_target_pairs={{4,8},{8,12},{5,9},{9,13},{6,10},{10,14},{7,11},{11,15},{20,24},{2... | collective-permute-start | bytes 196616 | tf_op jit(solution)/shard_map/ppermute | solution.py:395
  23.9 3.2 %near_part.1 = (f32[16,2048]{1,0:T(8,128)S(1)}, f32[128,2048]{1,0:T(8,128)S(1)}, f32[128,2048]{1,0:T(8,128)S(1)}, bf16[256,2048]{1,0:T(8,128)(2,1)}) custom-call(bf16[128,2048]{1,0:T(8,128)(2,1)S(1)} %collective-permute-done.refs_0_.rim_ref, f32[128,2048]{1,0:T(8,128)S(1)} %get-tuple-element.26.refs_1_.part_ref, ...), custom_call_target="tpu_custom_call" | custom-call | flops 2000000000 | bytes 4194304 | tf_op jit(solution)/shard_map/near_part/pallas_call | solution.py:346
  27.1 0.0 collective-permute-done.3.refs_2_
  27.1 0.0 collective-permute-done.2.refs_1_
  27.1 1.3 %far_rows.1 = bf16[256,2048]{1,0:T(8,128)(2,1)} custom-call(bf16[16,2048]{1,0:T(8,128)(2,1)S(1)} %collective-permute-done.1.refs_0_, bf16[16,2048]{1,0:T(8,128)(2,1)S(1)} %collective-permute-done.2.refs_1_, bf16[16,2048]{1,0:T(8,128)(2,1)S(1)} %collective-permute-done.3.refs_2_, bf16[256,2048]{1,0:T(8,128)(2,1)S(1)} %get-tuple-element.44.refs_3_, ...), custom_call_target="tpu_custom_call" | custom-call | flops 1000000000 | bytes 4194304 | tf_op jit(solution)/shard_map/far_rows/pallas_call | solution.py:346
  (1 shorter events, 0.0 us)
Async XLA Ops:
  1.9 16.3 %collective-permute-start = (bf16[128,2048]{1,0:T(8,128)(2,1)S(1)}, bf16[128,2048]{1,0:T(8,128)(2,1)S(1)}, u32[]{:S(2)}, u32[]{:S(2)}) collective-permute-start(bf16[128,2048]{1,0:T(8,128)(2,1)S(1)} %slice_multiply_fusion.tail_ref), channel_id=1, source_target_pairs={{0,4},{4,8},{8,12},{1,5},{5,9},{9,13},{2,6},{6,10},{10,14},{3,7},{... | collective-permute-start | bytes 1572872 | tf_op jit(solution)/shard_map/ppermute | solution.py:19
  11.4 9.0 %collective-permute-start.1 = (bf16[16,2048]{1,0:T(8,128)(2,1)S(1)}, bf16[16,2048]{1,0:T(8,128)(2,1)S(1)}, u32[]{:S(2)}, u32[]{:S(2)}) collective-permute-start(bf16[16,2048]{1,0:T(8,128)(2,1)S(1)} %get-tuple-element.41), channel_id=1, source_target_pairs={{0,4},{1,5},{2,6},{3,7},{16,20},{17,21},{18,22},{19,23}} | collective-permute-start | bytes 196616 | tf_op jit(solution)/shard_map/ppermute | solution.py:395
  20.4 6.6 %collective-permute-start.3 = (bf16[16,2048]{1,0:T(8,128)(2,1)S(1)}, bf16[16,2048]{1,0:T(8,128)(2,1)S(1)}, u32[]{:S(2)}, u32[]{:S(2)}) collective-permute-start(bf16[16,2048]{1,0:T(8,128)(2,1)S(1)} %add_convert_fusion), channel_id=1, source_target_pairs={{4,12},{5,13},{6,14},{7,15},{20,28},{21,29},{22,30},{23,31}} | collective-permute-start | bytes 196616 | tf_op jit(solution)/shard_map/ppermute | solution.py:395
  22.0 5.1 %collective-permute-start.2 = (bf16[16,2048]{1,0:T(8,128)(2,1)S(1)}, bf16[16,2048]{1,0:T(8,128)(2,1)S(1)}, u32[]{:S(2)}, u32[]{:S(2)}) collective-permute-start(bf16[16,2048]{1,0:T(8,128)(2,1)S(1)} %add_convert_fusion), channel_id=1, source_target_pairs={{4,8},{8,12},{5,9},{9,13},{6,10},{10,14},{7,11},{11,15},{20,24},{2... | collective-permute-start | bytes 196616 | tf_op jit(solution)/shard_map/ppermute | solution.py:395

commit v5 on v4

--- a/solution.py
+++ b/solution.py
@@ -79,21 +79,20 @@
 
 
 def local_kernel(
-    tail_ref, q_hbm, k_hbm, v_hbm, kli_hbm, taps_hbm, rate_hbm,
+    tail_ref, taps_ref, rate_ref, residue_ref, q_hbm, k_hbm, v_hbm, kli_hbm,
     mr_ref, part_ref, ulate_ref, late_ref, first_ref, taptab_ref, ends_ref, decay_ref, q_ref, kli_ref,
-    mr_early_ref, u_early_ref, early_ref,
-    k_ref, v_ref, taps_ref, rate_ref, mask_ref, fold_ref, acc_ref, in_sem,
+    mr_early_ref, u_early_ref, early_ref, rates_ref, residues_ref,
+    k_ref, v_ref, mask_ref, fold_ref, acc_ref, in_sem,
 ):
     rows, channels = k_hbm.shape
-    groups, tap_count = taps_hbm.shape
+    groups, tap_count = taps_ref.shape
     steps = channels // WIDE
     width = channels // groups
     wide_groups = WIDE // width
-    poles = rate_hbm.shape[0]
+    poles = rate_ref.shape[0]
     half = tap_count
 
     pairs = (
-        (taps_hbm, taps_ref), (rate_hbm, rate_ref),
         (k_hbm.at[:half], k_ref), (v_hbm.at[:half], v_ref), (q_hbm, q_ref), (kli_hbm, kli_ref),
     )
     copies = [pltpu.make_async_copy(a, b, in_sem.at[n]) for n, (a, b) in enumerate(pairs)]
@@ -102,8 +101,6 @@
 
     mask_ref[...] = same_group(width, BF16)
     fold_ref[...] = same_group(width, F32)
-    for copy in copies[:2]:
-        copy.wait()
 
     def tables(i, at):
         lane_item = iota((tap_count + width, WIDE), 1) % width
@@ -117,6 +114,8 @@
             step *= 2
         taptab_ref[:, at] = table.astype(BF16)
         rates = expand_groups(rate_ref[...], i * wide_groups, width, lax.Precision.HIGHEST)
+        rates_ref[:, at] = rates
+        residues_ref[:, at] = expand_groups(residue_ref[...], i * wide_groups, width, lax.Precision.HIGHEST)
         decay_ref[:, at] = jnp.exp(-rates * half)
         left = half - 1.0 - iota((half, WIDE), 0).astype(F32)
         ends_ref[at, :] = jnp.transpose(jnp.exp(-rates_along(rates, width) * left)).astype(BF16)
@@ -156,7 +155,7 @@
 
     pipelined(steps, tables)
     pipelined(steps, convolve_late)
-    for copy in copies[2:]:
+    for copy in copies:
         copy.wait()
     pipelined(steps, convolve_early, gate)
 
@@ -175,32 +174,20 @@
 
 
 def filter_kernel(
-    qli_hbm, rate_hbm, residue_hbm,
-    litab_ref, powers_ref, decay_ref, scale_ref, qli_ref,
-    rate_ref, residue_ref, mask_ref, sem,
+    rates_ref, residues_ref, u_ref, qli_hbm, litab_ref, powers_ref, scale_ref, near_ref, qli_ref, mask_ref, sem
 ):
     half, channels = litab_ref.shape
-    poles, groups = rate_hbm.shape
+    poles = rates_ref.shape[0]
+    width = CHUNK
     steps = channels // WIDE
-    width = channels // groups
-    wide_groups = WIDE // width
-    copies = (
-        pltpu.make_async_copy(rate_hbm, rate_ref, sem.at[0]),
-        pltpu.make_async_copy(residue_hbm, residue_ref, sem.at[1]),
-        pltpu.make_async_copy(qli_hbm, qli_ref, sem.at[2]),
-    )
-    for copy in copies:
-        copy.start()
+    copy = pltpu.make_async_copy(qli_hbm, qli_ref, sem)
+    copy.start()
     mask_ref[...] = same_group(width, BF16)
-    for copy in copies[:2]:
-        copy.wait()
 
     def tables(i, at):
         mask = mask_ref[...]
-        rates = expand_groups(rate_ref[...], i * wide_groups, width, lax.Precision.HIGHEST)
-        residue = expand_groups(residue_ref[...], i * wide_groups, width, lax.Precision.HIGHEST)
-        scale = residue * jnp.sqrt(one_minus_exp(2.0 * rates))
-        decay_ref[:, at] = jnp.exp(-rates * half)
+        rates = rates_ref[:, at]
+        scale = residues_ref[:, at] * jnp.sqrt(one_minus_exp(2.0 * rates))
         scale_ref[:, at] = scale
         item = (iota((poles, WIDE), 1) % width).astype(F32)
         times = iota((half, WIDE), 0).astype(F32)
@@ -214,8 +201,8 @@
         causal = iota((half, WIDE), 0) >= iota((half, WIDE), 1) % width
         litab_ref[:, at] = jnp.where(causal, li_taps, 0.0).astype(BF16)
 
-    pipelined(steps, tables)
-    copies[2].wait()
+    pipelined(steps, tables, near_rows(u_ref, litab_ref, near_ref, mask_ref, width))
+    copy.wait()
 
 
 def rim_rows(
@@ -244,59 +231,60 @@
     pipelined(channels // WIDE, convolve, gate)
 
 
-def inner(name):
-    at = lax.axis_index(name)
-    return jnp.logical_and(at > 0, at < lax.axis_size(name) - 1)
-
-
-def rim_kernel(by_place, *refs):
-    if by_place:
-        pl.when(inner("ctx"))(lambda: rim_rows(*refs))
+def rim_kernel(place, late_ref, decay_ref, before_ref, _after, *refs):
+    total_ref, mr_ref, u_ref, early_ref, *scratch = refs[6:]
+
+    def work():
+        rim_rows(*refs[:6], mr_ref, u_ref, early_ref, *scratch)
+        decay = decay_ref[...]
+        entered = before_ref[...].astype(F32)
+        total_ref[...] = (late_ref[...] + (early_ref[...] + entered * decay) * decay).astype(BF16)
+
+    if place is None:
+        work()
     else:
-        rim_rows(*refs)
-
-
-def near_kernel(
-    by_place,
-    rim_ref, part_ref, q_ref, kli_ref, taptab_ref, ends_ref,
-    mr_first_ref, u_first_ref, early_first_ref, mr_rim_ref, u_rim_ref, early_rim_ref, mr_late_ref, ulate_ref, litab_ref,
-    early_ref, near_early_ref, near_late_ref, mr_hbm,
-    mr_ref, u_ref, mask_ref, fold_ref, acc_ref, sem,
-):
+        pl.when(lax.axis_index("ctx") == place)(work)
+
+
+def near_kernel(places, *refs):
+    sets = [refs[3 * n : 3 * n + 3] for n in range(len(places))]
+    (
+        rim_ref, part_ref, q_ref, kli_ref, taptab_ref, ends_ref, mr_late_ref, litab_ref,
+        early_ref, near_ref, mr_hbm,
+        mr_ref, u_ref, mask_ref, fold_ref, acc_ref, sem,
+    ) = refs[3 * len(places) :]
     half, channels = u_ref.shape
-    steps = channels // WIDE
     copies = (
         pltpu.make_async_copy(mr_late_ref, mr_hbm.at[half:], sem.at[0]),
         pltpu.make_async_copy(mr_ref, mr_hbm.at[:half], sem.at[1]),
     )
     copies[0].start()
 
-    def take(*sources):
+    def take(sources):
         for source, target in zip(sources, (mr_ref, u_ref, early_ref)):
             target[...] = source[...]
 
-    if by_place:
+    if places == (None,):
+        take(sets[0])
+    else:
         own = (rim_ref, part_ref, q_ref, kli_ref, taptab_ref, ends_ref, mr_ref, u_ref, early_ref, mask_ref, fold_ref, acc_ref)
-        place = lax.axis_index("ctx")
-        pl.when(place == 0)(lambda: take(mr_first_ref, u_first_ref, early_first_ref))
-        pl.when(inner("ctx"))(lambda: take(mr_rim_ref, u_rim_ref, early_rim_ref))
-        pl.when(place == lax.axis_size("ctx") - 1)(lambda: rim_rows(*own))
-    else:
-        take(mr_rim_ref, u_rim_ref, early_rim_ref)
+        at = lax.axis_index("ctx")
+        for place, sources in zip(places, sets):
+            pl.when(at == place)(functools.partial(take, sources))
+        pl.when(at == len(places))(lambda: rim_rows(*own))
     copies[1].start()
     mask_ref[...] = same_group(CHUNK, BF16)
-    pipelined(steps, near_rows(ulate_ref, litab_ref, near_late_ref, mask_ref, CHUNK))
-    pipelined(steps, near_rows(u_ref, litab_ref, near_early_ref, mask_ref, CHUNK))
+    pipelined(channels // WIDE, near_rows(u_ref, litab_ref, near_ref, mask_ref, CHUNK))
     for copy in copies:
         copy.wait()
 
 
-def far_kernel(one_before, *refs):
+def far_kernel(adjacent, *refs):
     (
         q_ref, near_early_ref, near_late_ref, early_ref, powers_ref, decay_ref, scale_ref,
         out_hbm, out_ref, mask_ref, out_sem,
     ) = refs[-11:]
-    arrived = refs[one_before:-11]
+    arrived = refs[:-11]
     half, channels = powers_ref.shape
     steps = channels // WIDE
 
@@ -310,10 +298,10 @@
         scale = scale_ref[:, at]
         decay = decay_ref[:, at]
         entering = arrived[-1][:, at].astype(F32)
-        for ref in arrived[-2::-1]:
-            entering = entering * (decay * decay) + ref[:, at].astype(F32)
-        if one_before:
-            entering = entering + refs[0][:, at].astype(F32)
+        for n in range(len(arrived) - 2, -1, -1):
+            if n >= adjacent - 1:
+                entering = entering * (decay * decay)
+            entering = entering + arrived[n][:, at].astype(F32)
         middle = entering * decay + early_ref[:, at]
         powers = powers_ref[:, at]
         for first, state, near_ref in ((0, entering, near_early_ref), (half, middle, near_late_ref)):
@@ -349,18 +337,24 @@
             out_specs=[hbm if isinstance(out, jax.ShapeDtypeStruct) else vmem for out in outs],
             out_shape=outs,
             scratch_shapes=scratch,
-            cost_estimate=pl.CostEstimate(flops=flops, bytes_accessed=4 * 2**20, transcendentals=10**5),
+            cost_estimate=pl.CostEstimate(flops=flops, bytes_accessed=flops // 1000, transcendentals=0),
             compiler_params=params,
             name=name,
         )(*operands)
 
     tail = k_mr[half:] * v_mr[half:]
-    rim = shifted(tail, "ctx", 1)
-
-    mr_late, part, u_late, late, first, taptab, ends, decay, q, kli, *without_rim = call(
+    peers = lax.axis_size("ctx")
+    send = lambda array, *pairs: lax.ppermute(array, "ctx", pairs)
+    by_place = peers == 4
+    if by_place:
+        rims = [send(tail, (at, at + 1)) for at in range(3)]
+    else:
+        rims = [shifted(tail, "ctx", 1)]
+
+    mr_late, part, u_late, late, first, taptab, ends, decay, q, kli, *without_rim, rates, residues = call(
         local_kernel,
         "local_rows",
-        [vmem] + [hbm] * 6,
+        [vmem] * 4 + [hbm] * 4,
         [
             pltpu.VMEM(short, BF16),
             pltpu.VMEM(short, F32),
@@ -375,62 +369,72 @@
             pltpu.VMEM(short, BF16),
             pltpu.VMEM(short, BF16),
             pltpu.VMEM(pole_sum, F32),
+            pltpu.VMEM(pole_sum, F32),
+            pltpu.VMEM(pole_sum, F32),
         ],
         [
             pltpu.VMEM(short, BF16),
             pltpu.VMEM(short, BF16),
-            pltpu.VMEM((groups, tap_count), BF16),
-            pltpu.VMEM((poles, groups), F32),
             mask,
             fold,
             pltpu.VMEM(tall, F32),
-            dma((6,)),
+            dma((4,)),
         ],
         4 * 10**9,
-        tail,
-        *in_hbm(q_mr, k_mr, v_mr, k_li, mr_taps, li_rate.T),
-    )
-
-    peers = lax.axis_size("ctx")
-    send = lambda array, pairs: lax.ppermute(array, "ctx", pairs)
-    before = send(first, [(0, 1)]) if peers == 4 else jnp.zeros(pole_sum, BF16)
-
-    litab, powers, decay, scale, qli = call(
+        tail, mr_taps, li_rate.T, li_residue.T,
+        *in_hbm(q_mr, k_mr, v_mr, k_li),
+    )
+
+    zeros = jnp.zeros(pole_sum, BF16)
+    before = send(first, (0, 1)) if by_place else zeros
+
+    litab, powers, scale, near_late, qli = call(
         filter_kernel,
         "filter_tables",
-        [hbm] * 3,
+        [vmem] * 3 + [hbm],
         [
             pltpu.VMEM(short, BF16),
             pltpu.VMEM(short, BF16),
             pltpu.VMEM(pole_sum, F32),
-            pltpu.VMEM(pole_sum, F32),
+            pltpu.VMEM(short, F32),
             pltpu.VMEM(tall, BF16),
         ],
-        [pltpu.VMEM((poles, groups), F32), pltpu.VMEM((poles, groups), F32), mask, dma((3,))],
-        2 * 10**9,
-        *in_hbm(q_li, li_rate.T, li_residue.T),
-    )
-
-    by_place = peers == 4
-    rows_of_rim = (rim, part, q, kli, taptab, ends)
-    with_rim = call(
-        functools.partial(rim_kernel, by_place),
-        "rim_rows",
-        [vmem] * 6,
-        [pltpu.VMEM(short, BF16), pltpu.VMEM(short, BF16), pltpu.VMEM(pole_sum, F32)],
-        [mask, fold, pltpu.VMEM(short, F32)],
-        2 * 10**9,
-        *rows_of_rim,
-    )
-    total = (late + (with_rim[2] + before.astype(F32) * decay) * decay).astype(BF16)
-
-    if peers == 4:
-        next_but_one = send(total, [(1, 3)])
-        arrived = [send(total, [(1, 2), (2, 3)]), next_but_one]
+        [mask, dma(())],
+        10**7,
+        rates, residues, u_late, *in_hbm(q_li),
+    )
+
+    own = (part, q, kli, taptab, ends)
+
+    def with_rim(place, rim, entered, after):
+        return call(
+            functools.partial(rim_kernel, place),
+            "rim_rows",
+            [vmem] * 10,
+            [
+                pltpu.VMEM(pole_sum, BF16),
+                pltpu.VMEM(short, BF16),
+                pltpu.VMEM(short, BF16),
+                pltpu.VMEM(pole_sum, F32),
+            ],
+            [mask, fold, pltpu.VMEM(short, F32)],
+            10**7,
+            late, decay, entered, after, rim, *own,
+        )
+
+    if by_place:
+        total_1, *rim_1 = with_rim(1, rims[0], before, scale)
+        two_before = send(total_1, (1, 3))
+        one_before = send(total_1, (1, 2))
+        total_2, *rim_2 = with_rim(2, rims[1], zeros, total_1)
+        entered = before.astype(F32) + one_before.astype(F32) + two_before.astype(F32) * (decay * decay)
+        arrived = [entered, send(total_2, (2, 3))]
+        early_rows, places = (*without_rim, *rim_1, *rim_2), (0, 1, 2)
     else:
+        total, *early_rows = with_rim(None, rims[0], zeros, scale)
+        places = (None,)
         reach = min(3, max(peers - 1, 1))
         arrived = [shifted(total, "ctx", by) for by in range(1, reach + 1)]
-        rates = jnp.repeat(li_rate.T, width, axis=1)
         while reach < peers - 1:
             window = arrived[-1].astype(F32)
             for piece in arrived[-2::-1]:
@@ -443,20 +447,18 @@
             arrived = [merged]
             reach *= 4
 
-    early, near_early, near_late, mr_out = call(
-        functools.partial(near_kernel, by_place),
+    early, near_early, mr_out = call(
+        functools.partial(near_kernel, places),
         "near_part",
-        [vmem] * 15,
-        [pltpu.VMEM(pole_sum, F32), pltpu.VMEM(short, F32), pltpu.VMEM(short, F32), jax.ShapeDtypeStruct(tall, BF16)],
+        [vmem] * (len(early_rows) + 8),
+        [pltpu.VMEM(pole_sum, F32), pltpu.VMEM(short, F32), jax.ShapeDtypeStruct(tall, BF16)],
         [pltpu.VMEM(short, BF16), pltpu.VMEM(short, BF16), mask, fold, pltpu.VMEM(short, F32), dma((2,))],
-        2 * 10**9,
-        *rows_of_rim, *without_rim, *with_rim, mr_late, u_late, litab,
-    )
-
-    if peers == 4:
-        arrived = [before] + arrived
+        10**6,
+        *early_rows, rims[-1], *own, mr_late, litab,
+    )
+
     (li_out,) = call(
-        functools.partial(far_kernel, peers == 4),
+        functools.partial(far_kernel, 2 if by_place else 1),
         "far_rows",
         [vmem] * (len(arrived) + 7),
         [jax.ShapeDtypeStruct(tall, BF16)],

time: 28.8 us -> 28.2 us (0.979)
  the two profiles are of different devices: /device:TPU:14 before, /device:TPU:18 now
where the time goes in v5:
time: 28.2 us; the launch traced here: 27.9 us
  Pallas kernels  12.4 us (44%)
  starting transfers between devices  8.82 us (31%)
  waiting for transfers between devices  4.43 us (16%)
  other arithmetic  1.3 us (5%)
  between operations  0.98 us (3%)
    pallas_call x6, Pallas kernels, call(): pl.pallas_call(kernel, in_specs=ins, out_specs=[hbm if isinstance(out, ja...  12.4 us
    ppermute x7, starting transfers between devices, body(): send = lambda array, *pairs: lax.ppermute(array, 'ctx', pairs)  8.82 us
    ppermute x7, waiting for transfers between devices, body(): send = lambda array, *pairs: lax.ppermute(array, 'ctx', pairs)  4.43 us
    mul x1, other arithmetic, body(): tail = k_mr[half:] * v_mr[half:]  1.27 us
  transfers between devices with their start and end apart: 7, of which 2 were waited for; matrix products, arithmetic and copies ran while one was open for 0% of the time, Pallas kernels for 40%

profile of v5, /device:TPU:18, one launch (start us, length us, event | category | flops | bytes accessed | tf_op | source)
XLA Modules:
  0.0 27.9 jit_solution(4606090851915011932)
XLA Ops:
  0.6 0.0 copy-start.2
  0.6 0.0 copy-start.1
  0.7 0.0 copy-start
  0.7 1.3 %slice_multiply_fusion.tail_ref = bf16[128,2048]{1,0:T(8,128)(2,1)S(1)} fusion(bf16[256,2048]{1,0:T(8,128)(2,1)} %v_hbm.1, bf16[256,2048]{1,0:T(8,128)(2,1)} %k_hbm.1), kind=kLoop, calls=%fused_computation | loop fusion | flops 262144 | bytes 1572864 | tf_op jit(solution)/shard_map/mul | solution.py:345
  1.9 0.7 %collective-permute-start.1 = (bf16[128,2048]{1,0:T(8,128)(2,1)S(1)}, bf16[128,2048]{1,0:T(8,128)(2,1)S(1)}, u32[]{:S(2)}, u32[]{:S(2)}) collective-permute-start(bf16[128,2048]{1,0:T(8,128)(2,1)S(1)} %slice_multiply_fusion.tail_ref), channel_id=1, source_target_pairs={{0,4},{1,5},{2,6},{3,7},{16,20},{17,21},{18,22},{19,23}} | collective-permute-start | bytes 1572872 | tf_op jit(solution)/shard_map/ppermute | solution.py:347
  2.6 1.3 %collective-permute-start.2 = (bf16[128,2048]{1,0:T(8,128)(2,1)S(1)}, bf16[128,2048]{1,0:T(8,128)(2,1)S(1)}, u32[]{:S(2)}, u32[]{:S(2)}) collective-permute-start(bf16[128,2048]{1,0:T(8,128)(2,1)S(1)} %slice_multiply_fusion.tail_ref), channel_id=1, source_target_pairs={{4,8},{5,9},{6,10},{7,11},{20,24},{21,25},{22,26},{23,27}} | collective-permute-start | bytes 1572872 | tf_op jit(solution)/shard_map/ppermute | solution.py:347
  3.9 2.9 %collective-permute-start.3 = (bf16[128,2048]{1,0:T(8,128)(2,1)S(1)}, bf16[128,2048]{1,0:T(8,128)(2,1)S(1)}, u32[]{:S(2)}, u32[]{:S(2)}) collective-permute-start(bf16[128,2048]{1,0:T(8,128)(2,1)S(1)} %slice_multiply_fusion.tail_ref), channel_id=1, source_target_pairs={{8,12},{9,13},{10,14},{11,15},{24,28},{25,29},{26,30},{27,31}} | collective-permute-start | bytes 1572872 | tf_op jit(solution)/shard_map/ppermute | solution.py:347
  6.9 0.0 copy-done.2
  6.9 5.0 %local_rows.1 = (bf16[128,2048]{1,0:T(8,128)(2,1)S(1)}, f32[128,2048]{1,0:T(8,128)S(1)}, bf16[128,2048]{1,0:T(8,128)(2,1)S(1)}, f32[16,2048]{1,0:T(8,128)S(1)}, ...) custom-call(bf16[128,2048]{1,0:T(8,128)(2,1)S(1)} %slice_multiply_fu, ...), custom_call_target="tpu_custom_call" | custom-call | flops 4000000000 | bytes 4000000 | tf_op jit(solution)/shard_map/local_rows/pallas_call | solution.py:334
  11.9 0.7 %collective-permute-start = (bf16[16,2048]{1,0:T(8,128)(2,1)S(1)}, bf16[16,2048]{1,0:T(8,128)(2,1)S(1)}, u32[]{:S(2)}, u32[]{:S(2)}) collective-permute-start(bf16[16,2048]{1,0:T(8,128)(2,1)S(1)} %get-tuple-element.38), channel_id=1, source_target_pairs={{0,4},{1,5},{2,6},{3,7},{16,20},{17,21},{18,22},{19,23}} | collective-permute-start | bytes 196616 | tf_op jit(solution)/shard_map/ppermute | solution.py:347
  12.6 2.0 %filter_tables.1 = (bf16[128,2048]{1,0:T(8,128)(2,1)S(1)}, bf16[128,2048]{1,0:T(8,128)(2,1)S(1)}, f32[16,2048]{1,0:T(8,128)S(1)}, f32[128,2048]{1,0:T(8,128)S(1)}, bf16[256,2048]{1,0:T(8,128)(2,1)S(1)}) custom-call(f32[16,2048]{1,0:T(8,128)S(1)} %get-tuple-element.39.rates_ref, f32[16,2048]{1,0:T(8,128)S(1)} %get-tuple-element.40.residues_ref, ...), custom_call_target="tpu_custom_call" | custom-call | flops 10000000 | bytes 10000 | tf_op jit(solution)/shard_map/filter_tables/pallas_call | solution.py:334
  14.6 0.0 collective-permute-done.before_ref
  14.6 0.0 collective-permute-done.1.refs_0_
  14.6 0.7 %collective-permute-start.5 = (bf16[16,2048]{1,0:T(8,128)(2,1)S(1)}, bf16[16,2048]{1,0:T(8,128)(2,1)S(1)}, u32[]{:S(2)}, u32[]{:S(2)}) collective-permute-start(bf16[16,2048]{1,0:T(8,128)(2,1)S(1)} %get-tuple-element.51._after), channel_id=1, source_target_pairs={{4,12},{5,13},{6,14},{7,15},{20,28},{21,29},{22,30},{23,31}} | collective-permute-start | bytes 196616 | tf_op jit(solution)/shard_map/ppermute | solution.py:347
  15.3 1.3 %collective-permute-start.4 = (bf16[16,2048]{1,0:T(8,128)(2,1)S(1)}, bf16[16,2048]{1,0:T(8,128)(2,1)S(1)}, u32[]{:S(2)}, u32[]{:S(2)}) collective-permute-start(bf16[16,2048]{1,0:T(8,128)(2,1)S(1)} %get-tuple-element.51._after), channel_id=1, source_target_pairs={{4,8},{5,9},{6,10},{7,11},{20,24},{21,25},{22,26},{23,27}} | collective-permute-start | bytes 196616 | tf_op jit(solution)/shard_map/ppermute | solution.py:347
  16.6 1.6 %collective-permute-done.2.refs_0_ = bf16[128,2048]{1,0:T(8,128)(2,1)S(1)} collective-permute-done((bf16[128,2048]{1,0:T(8,128)(2,1)S(1)}, bf16[128,2048]{1,0:T(8,128)(2,1)S(1)}, u32[]{:S(2)}, u32[]{:S(2)}) %collective-permute-start.2) | collective-permute-done | bytes 524320 | tf_op jit(solution)/shard_map/ppermute | solution.py:347
  18.2 2.2 %rim_rows.3 = (bf16[16,2048]{1,0:T(8,128)(2,1)S(1)}, bf16[128,2048]{1,0:T(8,128)(2,1)S(1)}, bf16[128,2048]{1,0:T(8,128)(2,1)S(1)}, f32[16,2048]{1,0:T(8,128)S(1)}) custom-call(f32[16,2048]{1,0:T(8,128)S(1)} %get-tuple-element.36.late_ref, f32[16,2048]{1,0:T(8,128)S(1)} %get-tuple-element.37.decay_ref.refs_7_, ...), custom_call_target="tpu_custom_call" | custom-call | flops 10000000 | bytes 10000 | tf_op jit(solution)/shard_map/rim_rows/pallas_call | solution.py:334
  20.4 1.3 %collective-permute-start.6 = (bf16[16,2048]{1,0:T(8,128)(2,1)S(1)}, bf16[16,2048]{1,0:T(8,128)(2,1)S(1)}, u32[]{:S(2)}, u32[]{:S(2)}) collective-permute-start(bf16[16,2048]{1,0:T(8,128)(2,1)S(1)} %get-tuple-element.58), channel_id=1, source_target_pairs={{8,12},{9,13},{10,14},{11,15},{24,28},{25,29},{26,30},{27,31}} | collective-permute-start | bytes 196616 | tf_op jit(solution)/shard_map/ppermute | solution.py:347
  21.7 0.0 collective-permute-done.3.refs_9_
  21.8 1.8 %near_part.1 = (f32[16,2048]{1,0:T(8,128)S(1)}, f32[128,2048]{1,0:T(8,128)S(1)}, bf16[256,2048]{1,0:T(8,128)(2,1)}) custom-call(bf16[128,2048]{1,0:T(8,128)(2,1)S(1)} %get-tuple-element.33.refs_0_, bf16[128,2048]{1,0:T(8,128)(2,1)S(1)} %get-tuple-element.34.refs_1_, f32[16,2048]{1,0:T(8,128)S(1)} %get-tuple-element.35.refs_2_, ...), custom_call_target="tpu_custom_call" | custom-call | flops 1000000 | bytes 1000 | tf_op jit(solution)/shard_map/near_part/pallas_call | solution.py:334
  23.6 0.0 collective-permute-done.5
  23.6 2.8 %collective-permute-done.4 = bf16[16,2048]{1,0:T(8,128)(2,1)S(1)} collective-permute-done((bf16[16,2048]{1,0:T(8,128)(2,1)S(1)}, bf16[16,2048]{1,0:T(8,128)(2,1)S(1)}, u32[]{:S(2)}, u32[]{:S(2)}) %collective-permute-start.4) | collective-permute-done | bytes 65568 | tf_op jit(solution)/shard_map/ppermute | solution.py:347
  26.5 0.0 collective-permute-done.6.refs_1_
  26.5 1.3 %far_rows.1 = bf16[256,2048]{1,0:T(8,128)(2,1)} custom-call(f32[16,2048]{1,0:T(8,128)S(1)} %multiply_add_fusion.refs_0_, bf16[16,2048]{1,0:T(8,128)(2,1)S(1)} %collective-permute-done.6.refs_1_, bf16[256,2048]{1,0:T(8,128)(2,1)S(1)} %get-tuple-element.59.refs_2_, f32[128,2048]{1,0:T(8,128)S(1)} %get-tuple-element.60.refs_3_, ...), custom_call_target="tpu_custom_call" | custom-call | flops 1000000000 | bytes 1000000 | tf_op jit(solution)/shard_map/far_rows/pallas_call | solution.py:334
  (5 shorter events, 0.1 us)
Async XLA Ops:
  0.6 6.2 %copy-start.2 = (f32[128,16]{0,1:T(8,128)S(1)}, f32[128,16]{0,1:T(8,128)}, u32[]{:S(2)}) copy-start(f32[128,16]{0,1:T(8,128)} %param.15) | copy-start | bytes 24580
  0.6 6.2 %copy-start.1 = (f32[128,16]{0,1:T(8,128)S(1)}, f32[128,16]{0,1:T(8,128)}, u32[]{:S(2)}) copy-start(f32[128,16]{0,1:T(8,128)} %param.14) | copy-start | bytes 24580
  0.7 6.2 %copy-start = (bf16[128,128]{1,0:T(8,128)(2,1)S(1)}, bf16[128,128]{1,0:T(8,128)(2,1)}, u32[]{:S(2)}) copy-start(bf16[128,128]{1,0:T(8,128)(2,1)} %taps_ref.1) | copy-start | bytes 98308
  1.9 12.7 %collective-permute-start.1 = (bf16[128,2048]{1,0:T(8,128)(2,1)S(1)}, bf16[128,2048]{1,0:T(8,128)(2,1)S(1)}, u32[]{:S(2)}, u32[]{:S(2)}) collective-permute-start(bf16[128,2048]{1,0:T(8,128)(2,1)S(1)} %slice_multiply_fusion.tail_ref), channel_id=1, source_target_pairs={{0,4},{1,5},{2,6},{3,7},{16,20},{17,21},{18,22},{19,23}} | collective-permute-start | bytes 1572872 | tf_op jit(solution)/shard_map/ppermute | solution.py:347
  2.6 15.6 %collective-permute-start.2 = (bf16[128,2048]{1,0:T(8,128)(2,1)S(1)}, bf16[128,2048]{1,0:T(8,128)(2,1)S(1)}, u32[]{:S(2)}, u32[]{:S(2)}) collective-permute-start(bf16[128,2048]{1,0:T(8,128)(2,1)S(1)} %slice_multiply_fusion.tail_ref), channel_id=1, source_target_pairs={{4,8},{5,9},{6,10},{7,11},{20,24},{21,25},{22,26},{23,27}} | collective-permute-start | bytes 1572872 | tf_op jit(solution)/shard_map/ppermute | solution.py:347
  3.9 17.8 %collective-permute-start.3 = (bf16[128,2048]{1,0:T(8,128)(2,1)S(1)}, bf16[128,2048]{1,0:T(8,128)(2,1)S(1)}, u32[]{:S(2)}, u32[]{:S(2)}) collective-permute-start(bf16[128,2048]{1,0:T(8,128)(2,1)S(1)} %slice_multiply_fusion.tail_ref), channel_id=1, source_target_pairs={{8,12},{9,13},{10,14},{11,15},{24,28},{25,29},{26,30},{27,31}} | collective-permute-start | bytes 1572872 | tf_op jit(solution)/shard_map/ppermute | solution.py:347
  11.9 2.7 %collective-permute-start = (bf16[16,2048]{1,0:T(8,128)(2,1)S(1)}, bf16[16,2048]{1,0:T(8,128)(2,1)S(1)}, u32[]{:S(2)}, u32[]{:S(2)}) collective-permute-start(bf16[16,2048]{1,0:T(8,128)(2,1)S(1)} %get-tuple-element.38), channel_id=1, source_target_pairs={{0,4},{1,5},{2,6},{3,7},{16,20},{17,21},{18,22},{19,23}} | collective-permute-start | bytes 196616 | tf_op jit(solution)/shard_map/ppermute | solution.py:347
  14.6 8.9 %collective-permute-start.5 = (bf16[16,2048]{1,0:T(8,128)(2,1)S(1)}, bf16[16,2048]{1,0:T(8,128)(2,1)S(1)}, u32[]{:S(2)}, u32[]{:S(2)}) collective-permute-start(bf16[16,2048]{1,0:T(8,128)(2,1)S(1)} %get-tuple-element.51._after), channel_id=1, source_target_pairs={{4,12},{5,13},{6,14},{7,15},{20,28},{21,29},{22,30},{23,31}} | collective-permute-start | bytes 196616 | tf_op jit(solution)/shard_map/ppermute | solution.py:347
  15.3 11.1 %collective-permute-start.4 = (bf16[16,2048]{1,0:T(8,128)(2,1)S(1)}, bf16[16,2048]{1,0:T(8,128)(2,1)S(1)}, u32[]{:S(2)}, u32[]{:S(2)}) collective-permute-start(bf16[16,2048]{1,0:T(8,128)(2,1)S(1)} %get-tuple-element.51._after), channel_id=1, source_target_pairs={{4,8},{5,9},{6,10},{7,11},{20,24},{21,25},{22,26},{23,27}} | collective-permute-start | bytes 196616 | tf_op jit(solution)/shard_map/ppermute | solution.py:347
  20.4 6.0 %collective-permute-start.6 = (bf16[16,2048]{1,0:T(8,128)(2,1)S(1)}, bf16[16,2048]{1,0:T(8,128)(2,1)S(1)}, u32[]{:S(2)}, u32[]{:S(2)}) collective-permute-start(bf16[16,2048]{1,0:T(8,128)(2,1)S(1)} %get-tuple-element.58), channel_id=1, source_target_pairs={{8,12},{9,13},{10,14},{11,15},{24,28},{25,29},{26,30},{27,31}} | collective-permute-start | bytes 196616 | tf_op jit(solution)/shard_map/ppermute | solution.py:347

commit v6 on v5

--- a/solution.py
+++ b/solution.py
@@ -231,19 +231,22 @@
     pipelined(channels // WIDE, convolve, gate)
 
 
-def rim_kernel(place, late_ref, decay_ref, before_ref, _after, *refs):
+def rim_kernel(place, late_ref, decay_ref, _after, *refs):
     total_ref, mr_ref, u_ref, early_ref, *scratch = refs[6:]
 
     def work():
         rim_rows(*refs[:6], mr_ref, u_ref, early_ref, *scratch)
-        decay = decay_ref[...]
-        entered = before_ref[...].astype(F32)
-        total_ref[...] = (late_ref[...] + (early_ref[...] + entered * decay) * decay).astype(BF16)
+        total_ref[...] = (late_ref[...] + early_ref[...] * decay_ref[...]).astype(total_ref.dtype)
 
     if place is None:
         work()
     else:
         pl.when(lax.axis_index("ctx") == place)(work)
+
+
+def joined_kernel(own_ref, before_ref, decay_ref, total_ref):
+    decay = decay_ref[...]
+    total_ref[...] = (own_ref[...] + before_ref[...].astype(F32) * (decay * decay)).astype(BF16)
 
 
 def near_kernel(places, *refs):
@@ -385,8 +388,7 @@
         *in_hbm(q_mr, k_mr, v_mr, k_li),
     )
 
-    zeros = jnp.zeros(pole_sum, BF16)
-    before = send(first, (0, 1)) if by_place else zeros
+    before = send(first, (0, 1)) if by_place else None
 
     litab, powers, scale, near_late, qli = call(
         filter_kernel,
@@ -400,38 +402,47 @@
             pltpu.VMEM(tall, BF16),
         ],
         [mask, dma(())],
-        10**7,
+        10**6,
         rates, residues, u_late, *in_hbm(q_li),
     )
 
     own = (part, q, kli, taptab, ends)
 
-    def with_rim(place, rim, entered, after):
+    def with_rim(place, rim, after, dtype):
         return call(
             functools.partial(rim_kernel, place),
             "rim_rows",
-            [vmem] * 10,
+            [vmem] * 9,
             [
-                pltpu.VMEM(pole_sum, BF16),
+                pltpu.VMEM(pole_sum, dtype),
                 pltpu.VMEM(short, BF16),
                 pltpu.VMEM(short, BF16),
                 pltpu.VMEM(pole_sum, F32),
             ],
             [mask, fold, pltpu.VMEM(short, F32)],
-            10**7,
-            late, decay, entered, after, rim, *own,
+            10**6,
+            late, decay, after, rim, *own,
         )
 
     if by_place:
-        total_1, *rim_1 = with_rim(1, rims[0], before, scale)
+        total_1, *rim_1 = with_rim(1, rims[0], scale, F32)
+        (total_1,) = call(
+            joined_kernel,
+            "joined_sums",
+            [vmem] * 3,
+            [pltpu.VMEM(pole_sum, BF16)],
+            [],
+            10**6,
+            total_1, before, decay,
+        )
         two_before = send(total_1, (1, 3))
         one_before = send(total_1, (1, 2))
-        total_2, *rim_2 = with_rim(2, rims[1], zeros, total_1)
+        total_2, *rim_2 = with_rim(2, rims[1], total_1, BF16)
         entered = before.astype(F32) + one_before.astype(F32) + two_before.astype(F32) * (decay * decay)
         arrived = [entered, send(total_2, (2, 3))]
         early_rows, places = (*without_rim, *rim_1, *rim_2), (0, 1, 2)
     else:
-        total, *early_rows = with_rim(None, rims[0], zeros, scale)
+        total, *early_rows = with_rim(None, rims[0], scale, BF16)
         places = (None,)
         reach = min(3, max(peers - 1, 1))
         arrived = [shifted(total, "ctx", by) for by in range(1, reach + 1)]

time: 28.2 us -> 27.5 us (0.975)
  waiting for transfers between devices: 4.43 us -> 3.74 us
    ppermute x7, waiting for transfers between devices: 4.43 us -> 3.74 us  [body(): send = lambda array, *pairs: lax.ppermute(array, 'ctx', pairs)]
    pallas_call x6 -> x7, Pallas kernels: 12.4 us -> 12.4 us  [call(): pl.pallas_call(kernel, in_specs=ins, out_specs=[hbm if isinstance(out, ja...]
  transfers between devices with their start and end apart: 7 -> 7, of which waited for: 2 -> 2; matrix products, arithmetic and copies ran while one was open for 0% -> 0% of each run, Pallas kernels for 40% -> 41%
where the time goes in v6:
time: 27.5 us; the launch traced here: 27.2 us
  Pallas kernels  12.4 us (45%)
  starting transfers between devices  8.82 us (32%)
  waiting for transfers between devices  3.74 us (14%)
  other arithmetic  1.3 us (5%)
  between operations  0.98 us (4%)
    pallas_call x7, Pallas kernels, call(): pl.pallas_call(kernel, in_specs=ins, out_specs=[hbm if isinstance(out, ja...  12.4 us
    ppermute x7, starting transfers between devices, body(): send = lambda array, *pairs: lax.ppermute(array, 'ctx', pairs)  8.82 us
    ppermute x7, waiting for transfers between devices, body(): send = lambda array, *pairs: lax.ppermute(array, 'ctx', pairs)  3.74 us
    mul x1, other arithmetic, body(): tail = k_mr[half:] * v_mr[half:]  1.27 us
  transfers between devices with their start and end apart: 7, of which 2 were waited for; matrix products, arithmetic and copies ran while one was open for 0% of the time, Pallas kernels for 41%

profile of v6, /device:TPU:18, one launch (start us, length us, event | category | flops | bytes accessed | tf_op | source)
XLA Modules:
  0.0 27.2 jit_solution(3303983522223450877)
XLA Ops:
  0.6 0.0 copy-start.2
  0.6 0.0 copy-start.1
  0.7 0.0 copy-start
  0.7 1.3 %slice_multiply_fusion.tail_ref = bf16[128,2048]{1,0:T(8,128)(2,1)S(1)} fusion(bf16[256,2048]{1,0:T(8,128)(2,1)} %v_hbm.1, bf16[256,2048]{1,0:T(8,128)(2,1)} %k_hbm.1), kind=kLoop, calls=%fused_computation | loop fusion | flops 262144 | bytes 1572864 | tf_op jit(solution)/shard_map/mul | solution.py:348
  1.9 0.7 %collective-permute-start = (bf16[128,2048]{1,0:T(8,128)(2,1)S(1)}, bf16[128,2048]{1,0:T(8,128)(2,1)S(1)}, u32[]{:S(2)}, u32[]{:S(2)}) collective-permute-start(bf16[128,2048]{1,0:T(8,128)(2,1)S(1)} %slice_multiply_fusion.tail_ref), channel_id=1, source_target_pairs={{0,4},{1,5},{2,6},{3,7},{16,20},{17,21},{18,22},{19,23}} | collective-permute-start | bytes 1572872 | tf_op jit(solution)/shard_map/ppermute | solution.py:350
  2.6 1.3 %collective-permute-start.2 = (bf16[128,2048]{1,0:T(8,128)(2,1)S(1)}, bf16[128,2048]{1,0:T(8,128)(2,1)S(1)}, u32[]{:S(2)}, u32[]{:S(2)}) collective-permute-start(bf16[128,2048]{1,0:T(8,128)(2,1)S(1)} %slice_multiply_fusion.tail_ref), channel_id=1, source_target_pairs={{4,8},{5,9},{6,10},{7,11},{20,24},{21,25},{22,26},{23,27}} | collective-permute-start | bytes 1572872 | tf_op jit(solution)/shard_map/ppermute | solution.py:350
  3.9 2.9 %collective-permute-start.3 = (bf16[128,2048]{1,0:T(8,128)(2,1)S(1)}, bf16[128,2048]{1,0:T(8,128)(2,1)S(1)}, u32[]{:S(2)}, u32[]{:S(2)}) collective-permute-start(bf16[128,2048]{1,0:T(8,128)(2,1)S(1)} %slice_multiply_fusion.tail_ref), channel_id=1, source_target_pairs={{8,12},{9,13},{10,14},{11,15},{24,28},{25,29},{26,30},{27,31}} | collective-permute-start | bytes 1572872 | tf_op jit(solution)/shard_map/ppermute | solution.py:350
  6.9 0.0 copy-done.2
  6.9 5.0 %local_rows.1 = (bf16[128,2048]{1,0:T(8,128)(2,1)S(1)}, f32[128,2048]{1,0:T(8,128)S(1)}, bf16[128,2048]{1,0:T(8,128)(2,1)S(1)}, f32[16,2048]{1,0:T(8,128)S(1)}, ...) custom-call(bf16[128,2048]{1,0:T(8,128)(2,1)S(1)} %slice_multiply_fu, ...), custom_call_target="tpu_custom_call" | custom-call | flops 4000000000 | bytes 4000000 | tf_op jit(solution)/shard_map/local_rows/pallas_call | solution.py:337
  11.9 0.7 %collective-permute-start.1 = (bf16[16,2048]{1,0:T(8,128)(2,1)S(1)}, bf16[16,2048]{1,0:T(8,128)(2,1)S(1)}, u32[]{:S(2)}, u32[]{:S(2)}) collective-permute-start(bf16[16,2048]{1,0:T(8,128)(2,1)S(1)} %get-tuple-element.51), channel_id=1, source_target_pairs={{0,4},{1,5},{2,6},{3,7},{16,20},{17,21},{18,22},{19,23}} | collective-permute-start | bytes 196616 | tf_op jit(solution)/shard_map/ppermute | solution.py:350
  12.6 2.0 %filter_tables.1 = (bf16[128,2048]{1,0:T(8,128)(2,1)S(1)}, bf16[128,2048]{1,0:T(8,128)(2,1)S(1)}, f32[16,2048]{1,0:T(8,128)S(1)}, f32[128,2048]{1,0:T(8,128)S(1)}, bf16[256,2048]{1,0:T(8,128)(2,1)S(1)}) custom-call(f32[16,2048]{1,0:T(8,128)S(1)} %get-tuple-element.38.rates_ref, f32[16,2048]{1,0:T(8,128)S(1)} %get-tuple-element.39.residues_ref, ...), custom_call_target="tpu_custom_call" | custom-call | flops 1000000 | bytes 1000 | tf_op jit(solution)/shard_map/filter_tables/pallas_call | solution.py:337
  14.6 0.0 collective-permute-done.refs_0_
  14.6 0.0 collective-permute-done.1.before_ref
  14.7 0.7 %collective-permute-start.5 = (bf16[16,2048]{1,0:T(8,128)(2,1)S(1)}, bf16[16,2048]{1,0:T(8,128)(2,1)S(1)}, u32[]{:S(2)}, u32[]{:S(2)}) collective-permute-start(bf16[16,2048]{1,0:T(8,128)(2,1)S(1)} %joined_sums.1._after), channel_id=1, source_target_pairs={{4,12},{5,13},{6,14},{7,15},{20,28},{21,29},{22,30},{23,31}} | collective-permute-start | bytes 196616 | tf_op jit(solution)/shard_map/ppermute | solution.py:350
  15.3 1.3 %collective-permute-start.4 = (bf16[16,2048]{1,0:T(8,128)(2,1)S(1)}, bf16[16,2048]{1,0:T(8,128)(2,1)S(1)}, u32[]{:S(2)}, u32[]{:S(2)}) collective-permute-start(bf16[16,2048]{1,0:T(8,128)(2,1)S(1)} %joined_sums.1._after), channel_id=1, source_target_pairs={{4,8},{5,9},{6,10},{7,11},{20,24},{21,25},{22,26},{23,27}} | collective-permute-start | bytes 196616 | tf_op jit(solution)/shard_map/ppermute | solution.py:350
  16.6 1.6 %collective-permute-done.2.refs_0_ = bf16[128,2048]{1,0:T(8,128)(2,1)S(1)} collective-permute-done((bf16[128,2048]{1,0:T(8,128)(2,1)S(1)}, bf16[128,2048]{1,0:T(8,128)(2,1)S(1)}, u32[]{:S(2)}, u32[]{:S(2)}) %collective-permute-start.2) | collective-permute-done | bytes 524320 | tf_op jit(solution)/shard_map/ppermute | solution.py:350
  18.2 2.2 %rim_rows.3 = (bf16[16,2048]{1,0:T(8,128)(2,1)S(1)}, bf16[128,2048]{1,0:T(8,128)(2,1)S(1)}, bf16[128,2048]{1,0:T(8,128)(2,1)S(1)}, f32[16,2048]{1,0:T(8,128)S(1)}) custom-call(f32[16,2048]{1,0:T(8,128)S(1)} %get-tuple-element.36.late_ref, f32[16,2048]{1,0:T(8,128)S(1)} %get-tuple-element.37.decay_ref.refs_7_, bf16[16,2048]{1,0:T(8,128)(2,1)S(1)} %joined_sums.1._after, ...), custom_call_target="tpu_custom_call" | custom-call | flops 1000000 | bytes 1000 | tf_op jit(solution)/shard_map/rim_rows/pallas_call | solution.py:337
  20.4 1.3 %collective-permute-start.6 = (bf16[16,2048]{1,0:T(8,128)(2,1)S(1)}, bf16[16,2048]{1,0:T(8,128)(2,1)S(1)}, u32[]{:S(2)}, u32[]{:S(2)}) collective-permute-start(bf16[16,2048]{1,0:T(8,128)(2,1)S(1)} %get-tuple-element.58), channel_id=1, source_target_pairs={{8,12},{9,13},{10,14},{11,15},{24,28},{25,29},{26,30},{27,31}} | collective-permute-start | bytes 196616 | tf_op jit(solution)/shard_map/ppermute | solution.py:350
  21.7 0.0 collective-permute-done.3.refs_9_
  21.7 1.8 %near_part.1 = (f32[16,2048]{1,0:T(8,128)S(1)}, f32[128,2048]{1,0:T(8,128)S(1)}, bf16[256,2048]{1,0:T(8,128)(2,1)}) custom-call(bf16[128,2048]{1,0:T(8,128)(2,1)S(1)} %get-tuple-element.33.refs_0_, bf16[128,2048]{1,0:T(8,128)(2,1)S(1)} %get-tuple-element.34.refs_1_, f32[16,2048]{1,0:T(8,128)S(1)} %get-tuple-element.35.refs_2_, ...), custom_call_target="tpu_custom_call" | custom-call | flops 1000000 | bytes 1000 | tf_op jit(solution)/shard_map/near_part/pallas_call | solution.py:337
  23.6 0.0 collective-permute-done.5
  23.6 2.2 %collective-permute-done.4 = bf16[16,2048]{1,0:T(8,128)(2,1)S(1)} collective-permute-done((bf16[16,2048]{1,0:T(8,128)(2,1)S(1)}, bf16[16,2048]{1,0:T(8,128)(2,1)S(1)}, u32[]{:S(2)}, u32[]{:S(2)}) %collective-permute-start.4) | collective-permute-done | bytes 65568 | tf_op jit(solution)/shard_map/ppermute | solution.py:350
  25.8 0.0 collective-permute-done.6.refs_1_
  25.8 1.3 %far_rows.1 = bf16[256,2048]{1,0:T(8,128)(2,1)} custom-call(f32[16,2048]{1,0:T(8,128)S(1)} %multiply_add_fusion.refs_0_, bf16[16,2048]{1,0:T(8,128)(2,1)S(1)} %collective-permute-done.6.refs_1_, bf16[256,2048]{1,0:T(8,128)(2,1)S(1)} %get-tuple-element.59.refs_2_, f32[128,2048]{1,0:T(8,128)S(1)} %get-tuple-element.60.refs_3_, ...), custom_call_target="tpu_custom_call" | custom-call | flops 1000000000 | bytes 1000000 | tf_op jit(solution)/shard_map/far_rows/pallas_call | solution.py:337
  (5 shorter events, 0.1 us)
Async XLA Ops:
  0.6 6.2 %copy-start.2 = (f32[128,16]{0,1:T(8,128)S(1)}, f32[128,16]{0,1:T(8,128)}, u32[]{:S(2)}) copy-start(f32[128,16]{0,1:T(8,128)} %param.15) | copy-start | bytes 24580
  0.6 6.2 %copy-start.1 = (f32[128,16]{0,1:T(8,128)S(1)}, f32[128,16]{0,1:T(8,128)}, u32[]{:S(2)}) copy-start(f32[128,16]{0,1:T(8,128)} %param.14) | copy-start | bytes 24580
  0.7 6.2 %copy-start = (bf16[128,128]{1,0:T(8,128)(2,1)S(1)}, bf16[128,128]{1,0:T(8,128)(2,1)}, u32[]{:S(2)}) copy-start(bf16[128,128]{1,0:T(8,128)(2,1)} %taps_ref.1) | copy-start | bytes 98308
  1.9 12.7 %collective-permute-start = (bf16[128,2048]{1,0:T(8,128)(2,1)S(1)}, bf16[128,2048]{1,0:T(8,128)(2,1)S(1)}, u32[]{:S(2)}, u32[]{:S(2)}) collective-permute-start(bf16[128,2048]{1,0:T(8,128)(2,1)S(1)} %slice_multiply_fusion.tail_ref), channel_id=1, source_target_pairs={{0,4},{1,5},{2,6},{3,7},{16,20},{17,21},{18,22},{19,23}} | collective-permute-start | bytes 1572872 | tf_op jit(solution)/shard_map/ppermute | solution.py:350
  2.6 15.6 %collective-permute-start.2 = (bf16[128,2048]{1,0:T(8,128)(2,1)S(1)}, bf16[128,2048]{1,0:T(8,128)(2,1)S(1)}, u32[]{:S(2)}, u32[]{:S(2)}) collective-permute-start(bf16[128,2048]{1,0:T(8,128)(2,1)S(1)} %slice_multiply_fusion.tail_ref), channel_id=1, source_target_pairs={{4,8},{5,9},{6,10},{7,11},{20,24},{21,25},{22,26},{23,27}} | collective-permute-start | bytes 1572872 | tf_op jit(solution)/shard_map/ppermute | solution.py:350
  3.9 17.8 %collective-permute-start.3 = (bf16[128,2048]{1,0:T(8,128)(2,1)S(1)}, bf16[128,2048]{1,0:T(8,128)(2,1)S(1)}, u32[]{:S(2)}, u32[]{:S(2)}) collective-permute-start(bf16[128,2048]{1,0:T(8,128)(2,1)S(1)} %slice_multiply_fusion.tail_ref), channel_id=1, source_target_pairs={{8,12},{9,13},{10,14},{11,15},{24,28},{25,29},{26,30},{27,31}} | collective-permute-start | bytes 1572872 | tf_op jit(solution)/shard_map/ppermute | solution.py:350
  11.9 2.7 %collective-permute-start.1 = (bf16[16,2048]{1,0:T(8,128)(2,1)S(1)}, bf16[16,2048]{1,0:T(8,128)(2,1)S(1)}, u32[]{:S(2)}, u32[]{:S(2)}) collective-permute-start(bf16[16,2048]{1,0:T(8,128)(2,1)S(1)} %get-tuple-element.51), channel_id=1, source_target_pairs={{0,4},{1,5},{2,6},{3,7},{16,20},{17,21},{18,22},{19,23}} | collective-permute-start | bytes 196616 | tf_op jit(solution)/shard_map/ppermute | solution.py:350
  14.7 8.9 %collective-permute-start.5 = (bf16[16,2048]{1,0:T(8,128)(2,1)S(1)}, bf16[16,2048]{1,0:T(8,128)(2,1)S(1)}, u32[]{:S(2)}, u32[]{:S(2)}) collective-permute-start(bf16[16,2048]{1,0:T(8,128)(2,1)S(1)} %joined_sums.1._after), channel_id=1, source_target_pairs={{4,12},{5,13},{6,14},{7,15},{20,28},{21,29},{22,30},{23,31}} | collective-permute-start | bytes 196616 | tf_op jit(solution)/shard_map/ppermute | solution.py:350
  15.3 10.4 %collective-permute-start.4 = (bf16[16,2048]{1,0:T(8,128)(2,1)S(1)}, bf16[16,2048]{1,0:T(8,128)(2,1)S(1)}, u32[]{:S(2)}, u32[]{:S(2)}) collective-permute-start(bf16[16,2048]{1,0:T(8,128)(2,1)S(1)} %joined_sums.1._after), channel_id=1, source_target_pairs={{4,8},{5,9},{6,10},{7,11},{20,24},{21,25},{22,26},{23,27}} | collective-permute-start | bytes 196616 | tf_op jit(solution)/shard_map/ppermute | solution.py:350
  20.4 5.4 %collective-permute-start.6 = (bf16[16,2048]{1,0:T(8,128)(2,1)S(1)}, bf16[16,2048]{1,0:T(8,128)(2,1)S(1)}, u32[]{:S(2)}, u32[]{:S(2)}) collective-permute-start(bf16[16,2048]{1,0:T(8,128)(2,1)S(1)} %get-tuple-element.58), channel_id=1, source_target_pairs={{8,12},{9,13},{10,14},{11,15},{24,28},{25,29},{26,30},{27,31}} | collective-permute-start | bytes 196616 | tf_op jit(solution)/shard_map/ppermute | solution.py:350

commit v7 on v6

--- a/solution.py
+++ b/solution.py
@@ -55,11 +55,11 @@
     return jnp.dot(per_group, pick.astype(F32).astype(per_group.dtype), precision=precision, preferred_element_type=F32)
 
 
-def pipelined(steps, *stages):
-    for turn in range(steps + len(stages) - 1):
-        for lag, stage in enumerate(stages):
-            if 0 <= turn - lag < steps:
-                i = turn - lag
+def pipelined(steps, *stages, lag=1):
+    for turn in range(steps + lag * (len(stages) - 1)):
+        for n, stage in enumerate(stages):
+            i = turn - lag * n
+            if 0 <= i < steps:
                 stage(i, slice(i * WIDE, (i + 1) * WIDE))
 
 
@@ -157,7 +157,7 @@
     pipelined(steps, convolve_late)
     for copy in copies:
         copy.wait()
-    pipelined(steps, convolve_early, gate)
+    pipelined(steps, convolve_early, gate, lag=3)
 
 
 def near_rows(u_ref, litab_ref, near_ref, mask_ref, width):
@@ -218,7 +218,7 @@
         mask = mask_ref[...]
         rim = rim_ref[:, at]
         acc_ref[:, at] = part_ref[:, at]
-        for first in range(0, half, width):
+        for first in range(half - width, -1, -width):
             acc_ref[: first + width, at] += dot(taptab_ref[half - first :, at], spread(rim[first : first + width], mask))
 
     def gate(i, at):
@@ -228,7 +228,7 @@
         u_ref[:, at] = u
         early_ref[:, at] = pole_sums(ends_ref[at, :], u, fold_ref, poles)
 
-    pipelined(channels // WIDE, convolve, gate)
+    pipelined(channels // WIDE, convolve, gate, lag=4)
 
 
 def rim_kernel(place, late_ref, decay_ref, _after, *refs):

time: 27.5 us -> 26.8 us (0.975)
  Pallas kernels: 12.4 us -> 11.2 us
  waiting for transfers between devices: 3.74 us -> 4.37 us
    pallas_call x7, Pallas kernels: 12.4 us -> 11.2 us  [call(): pl.pallas_call(kernel, in_specs=ins, out_specs=[hbm if isinstance(out, ja...]
    ppermute x7, waiting for transfers between devices: 3.74 us -> 4.37 us  [body(): send = lambda array, *pairs: lax.ppermute(array, 'ctx', pairs)]
  transfers between devices with their start and end apart: 7 -> 7, of which waited for: 2 -> 2; matrix products, arithmetic and copies ran while one was open for 0% -> 0% of each run, Pallas kernels for 41% -> 37%
where the time goes in v7:
time: 26.8 us; the launch traced here: 26.5 us
  Pallas kernels  11.2 us (42%)
  starting transfers between devices  8.82 us (33%)
  waiting for transfers between devices  4.37 us (16%)
  other arithmetic  1.3 us (5%)
  between operations  0.82 us (3%)
    pallas_call x7, Pallas kernels, call(): pl.pallas_call(kernel, in_specs=ins, out_specs=[hbm if isinstance(out, ja...  11.2 us
    ppermute x7, starting transfers between devices, body(): send = lambda array, *pairs: lax.ppermute(array, 'ctx', pairs)  8.82 us
    ppermute x7, waiting for transfers between devices, body(): send = lambda array, *pairs: lax.ppermute(array, 'ctx', pairs)  4.37 us
    mul x1, other arithmetic, body(): tail = k_mr[half:] * v_mr[half:]  1.27 us
  transfers between devices with their start and end apart: 7, of which 2 were waited for; matrix products, arithmetic and copies ran while one was open for 0% of the time, Pallas kernels for 37%

profile of v7, /device:TPU:18, one launch (start us, length us, event | category | flops | bytes accessed | tf_op | source)
XLA Modules:
  0.0 26.5 jit_solution(14393446400915834427)
XLA Ops:
  0.6 0.0 copy-start.2
  0.7 1.3 %slice_multiply_fusion.tail_ref = bf16[128,2048]{1,0:T(8,128)(2,1)S(1)} fusion(bf16[256,2048]{1,0:T(8,128)(2,1)} %v_hbm.1, bf16[256,2048]{1,0:T(8,128)(2,1)} %k_hbm.1), kind=kLoop, calls=%fused_computation | loop fusion | flops 262144 | bytes 1572864 | tf_op jit(solution)/shard_map/mul | solution.py:348
  1.9 0.7 %collective-permute-start = (bf16[128,2048]{1,0:T(8,128)(2,1)S(1)}, bf16[128,2048]{1,0:T(8,128)(2,1)S(1)}, u32[]{:S(2)}, u32[]{:S(2)}) collective-permute-start(bf16[128,2048]{1,0:T(8,128)(2,1)S(1)} %slice_multiply_fusion.tail_ref), channel_id=1, source_target_pairs={{0,4},{1,5},{2,6},{3,7},{16,20},{17,21},{18,22},{19,23}} | collective-permute-start | bytes 1572872 | tf_op jit(solution)/shard_map/ppermute | solution.py:350
  2.6 1.3 %collective-permute-start.2 = (bf16[128,2048]{1,0:T(8,128)(2,1)S(1)}, bf16[128,2048]{1,0:T(8,128)(2,1)S(1)}, u32[]{:S(2)}, u32[]{:S(2)}) collective-permute-start(bf16[128,2048]{1,0:T(8,128)(2,1)S(1)} %slice_multiply_fusion.tail_ref), channel_id=1, source_target_pairs={{4,8},{5,9},{6,10},{7,11},{20,24},{21,25},{22,26},{23,27}} | collective-permute-start | bytes 1572872 | tf_op jit(solution)/shard_map/ppermute | solution.py:350
  3.9 2.9 %collective-permute-start.3 = (bf16[128,2048]{1,0:T(8,128)(2,1)S(1)}, bf16[128,2048]{1,0:T(8,128)(2,1)S(1)}, u32[]{:S(2)}, u32[]{:S(2)}) collective-permute-start(bf16[128,2048]{1,0:T(8,128)(2,1)S(1)} %slice_multiply_fusion.tail_ref), channel_id=1, source_target_pairs={{8,12},{9,13},{10,14},{11,15},{24,28},{25,29},{26,30},{27,31}} | collective-permute-start | bytes 1572872 | tf_op jit(solution)/shard_map/ppermute | solution.py:350
  6.9 0.0 copy-done.2
  6.9 0.0 copy-done.1
  6.9 0.0 copy-done
  6.9 4.6 %local_rows.1 = (bf16[128,2048]{1,0:T(8,128)(2,1)S(1)}, f32[128,2048]{1,0:T(8,128)S(1)}, bf16[128,2048]{1,0:T(8,128)(2,1)S(1)}, f32[16,2048]{1,0:T(8,128)S(1)}, ...) custom-call(bf16[128,2048]{1,0:T(8,128)(2,1)S(1)} %slice_multiply_fu, ...), custom_call_target="tpu_custom_call" | custom-call | flops 4000000000 | bytes 4000000 | tf_op jit(solution)/shard_map/local_rows/pallas_call | solution.py:337
  11.5 0.7 %collective-permute-start.1 = (bf16[16,2048]{1,0:T(8,128)(2,1)S(1)}, bf16[16,2048]{1,0:T(8,128)(2,1)S(1)}, u32[]{:S(2)}, u32[]{:S(2)}) collective-permute-start(bf16[16,2048]{1,0:T(8,128)(2,1)S(1)} %get-tuple-element.51), channel_id=1, source_target_pairs={{0,4},{1,5},{2,6},{3,7},{16,20},{17,21},{18,22},{19,23}} | collective-permute-start | bytes 196616 | tf_op jit(solution)/shard_map/ppermute | solution.py:350
  12.2 2.0 %filter_tables.1 = (bf16[128,2048]{1,0:T(8,128)(2,1)S(1)}, bf16[128,2048]{1,0:T(8,128)(2,1)S(1)}, f32[16,2048]{1,0:T(8,128)S(1)}, f32[128,2048]{1,0:T(8,128)S(1)}, bf16[256,2048]{1,0:T(8,128)(2,1)S(1)}) custom-call(f32[16,2048]{1,0:T(8,128)S(1)} %get-tuple-element.38.rates_ref, f32[16,2048]{1,0:T(8,128)S(1)} %get-tuple-element.39.residues_ref, ...), custom_call_target="tpu_custom_call" | custom-call | flops 1000000 | bytes 1000 | tf_op jit(solution)/shard_map/filter_tables/pallas_call | solution.py:337
  14.1 0.0 collective-permute-done.refs_0_
  14.2 0.0 collective-permute-done.1.before_ref
  14.2 0.7 %collective-permute-start.5 = (bf16[16,2048]{1,0:T(8,128)(2,1)S(1)}, bf16[16,2048]{1,0:T(8,128)(2,1)S(1)}, u32[]{:S(2)}, u32[]{:S(2)}) collective-permute-start(bf16[16,2048]{1,0:T(8,128)(2,1)S(1)} %joined_sums.1._after), channel_id=1, source_target_pairs={{4,12},{5,13},{6,14},{7,15},{20,28},{21,29},{22,30},{23,31}} | collective-permute-start | bytes 196616 | tf_op jit(solution)/shard_map/ppermute | solution.py:350
  14.9 1.3 %collective-permute-start.4 = (bf16[16,2048]{1,0:T(8,128)(2,1)S(1)}, bf16[16,2048]{1,0:T(8,128)(2,1)S(1)}, u32[]{:S(2)}, u32[]{:S(2)}) collective-permute-start(bf16[16,2048]{1,0:T(8,128)(2,1)S(1)} %joined_sums.1._after), channel_id=1, source_target_pairs={{4,8},{5,9},{6,10},{7,11},{20,24},{21,25},{22,26},{23,27}} | collective-permute-start | bytes 196616 | tf_op jit(solution)/shard_map/ppermute | solution.py:350
  16.2 2.0 %collective-permute-done.2.refs_0_ = bf16[128,2048]{1,0:T(8,128)(2,1)S(1)} collective-permute-done((bf16[128,2048]{1,0:T(8,128)(2,1)S(1)}, bf16[128,2048]{1,0:T(8,128)(2,1)S(1)}, u32[]{:S(2)}, u32[]{:S(2)}) %collective-permute-start.2) | collective-permute-done | bytes 524320 | tf_op jit(solution)/shard_map/ppermute | solution.py:350
  18.2 1.7 %rim_rows.3 = (bf16[16,2048]{1,0:T(8,128)(2,1)S(1)}, bf16[128,2048]{1,0:T(8,128)(2,1)S(1)}, bf16[128,2048]{1,0:T(8,128)(2,1)S(1)}, f32[16,2048]{1,0:T(8,128)S(1)}) custom-call(f32[16,2048]{1,0:T(8,128)S(1)} %get-tuple-element.36.late_ref, f32[16,2048]{1,0:T(8,128)S(1)} %get-tuple-element.37.decay_ref.refs_7_, bf16[16,2048]{1,0:T(8,128)(2,1)S(1)} %joined_sums.1._after, ...), custom_call_target="tpu_custom_call" | custom-call | flops 1000000 | bytes 1000 | tf_op jit(solution)/shard_map/rim_rows/pallas_call | solution.py:337
  19.9 1.3 %collective-permute-start.6 = (bf16[16,2048]{1,0:T(8,128)(2,1)S(1)}, bf16[16,2048]{1,0:T(8,128)(2,1)S(1)}, u32[]{:S(2)}, u32[]{:S(2)}) collective-permute-start(bf16[16,2048]{1,0:T(8,128)(2,1)S(1)} %get-tuple-element.58), channel_id=1, source_target_pairs={{8,12},{9,13},{10,14},{11,15},{24,28},{25,29},{26,30},{27,31}} | collective-permute-start | bytes 196616 | tf_op jit(solution)/shard_map/ppermute | solution.py:350
  21.2 0.0 collective-permute-done.3.refs_9_
  21.2 1.6 %near_part.1 = (f32[16,2048]{1,0:T(8,128)S(1)}, f32[128,2048]{1,0:T(8,128)S(1)}, bf16[256,2048]{1,0:T(8,128)(2,1)}) custom-call(bf16[128,2048]{1,0:T(8,128)(2,1)S(1)} %get-tuple-element.33.refs_0_, bf16[128,2048]{1,0:T(8,128)(2,1)S(1)} %get-tuple-element.34.refs_1_, f32[16,2048]{1,0:T(8,128)S(1)} %get-tuple-element.35.refs_2_, ...), custom_call_target="tpu_custom_call" | custom-call | flops 1000000 | bytes 1000 | tf_op jit(solution)/shard_map/near_part/pallas_call | solution.py:337
  22.8 0.0 collective-permute-done.5
  22.9 2.3 %collective-permute-done.4 = bf16[16,2048]{1,0:T(8,128)(2,1)S(1)} collective-permute-done((bf16[16,2048]{1,0:T(8,128)(2,1)S(1)}, bf16[16,2048]{1,0:T(8,128)(2,1)S(1)}, u32[]{:S(2)}, u32[]{:S(2)}) %collective-permute-start.4) | collective-permute-done | bytes 65568 | tf_op jit(solution)/shard_map/ppermute | solution.py:350
  25.2 0.0 collective-permute-done.6.refs_1_
  25.2 1.3 %far_rows.1 = bf16[256,2048]{1,0:T(8,128)(2,1)} custom-call(f32[16,2048]{1,0:T(8,128)S(1)} %multiply_add_fusion.refs_0_, bf16[16,2048]{1,0:T(8,128)(2,1)S(1)} %collective-permute-done.6.refs_1_, bf16[256,2048]{1,0:T(8,128)(2,1)S(1)} %get-tuple-element.59.refs_2_, f32[128,2048]{1,0:T(8,128)S(1)} %get-tuple-element.60.refs_3_, ...), custom_call_target="tpu_custom_call" | custom-call | flops 1000000000 | bytes 1000000 | tf_op jit(solution)/shard_map/far_rows/pallas_call | solution.py:337
  (5 shorter events, 0.1 us)
Async XLA Ops:
  0.6 6.2 %copy-start.2 = (f32[128,16]{0,1:T(8,128)S(1)}, f32[128,16]{0,1:T(8,128)}, u32[]{:S(2)}) copy-start(f32[128,16]{0,1:T(8,128)} %param.15) | copy-start | bytes 24580
  0.6 6.2 %copy-start.1 = (f32[128,16]{0,1:T(8,128)S(1)}, f32[128,16]{0,1:T(8,128)}, u32[]{:S(2)}) copy-start(f32[128,16]{0,1:T(8,128)} %param.14) | copy-start | bytes 24580
  0.7 6.2 %copy-start = (bf16[128,128]{1,0:T(8,128)(2,1)S(1)}, bf16[128,128]{1,0:T(8,128)(2,1)}, u32[]{:S(2)}) copy-start(bf16[128,128]{1,0:T(8,128)(2,1)} %taps_ref.1) | copy-start | bytes 98308
  1.9 12.2 %collective-permute-start = (bf16[128,2048]{1,0:T(8,128)(2,1)S(1)}, bf16[128,2048]{1,0:T(8,128)(2,1)S(1)}, u32[]{:S(2)}, u32[]{:S(2)}) collective-permute-start(bf16[128,2048]{1,0:T(8,128)(2,1)S(1)} %slice_multiply_fusion.tail_ref), channel_id=1, source_target_pairs={{0,4},{1,5},{2,6},{3,7},{16,20},{17,21},{18,22},{19,23}} | collective-permute-start | bytes 1572872 | tf_op jit(solution)/shard_map/ppermute | solution.py:350
  2.6 15.6 %collective-permute-start.2 = (bf16[128,2048]{1,0:T(8,128)(2,1)S(1)}, bf16[128,2048]{1,0:T(8,128)(2,1)S(1)}, u32[]{:S(2)}, u32[]{:S(2)}) collective-permute-start(bf16[128,2048]{1,0:T(8,128)(2,1)S(1)} %slice_multiply_fusion.tail_ref), channel_id=1, source_target_pairs={{4,8},{5,9},{6,10},{7,11},{20,24},{21,25},{22,26},{23,27}} | collective-permute-start | bytes 1572872 | tf_op jit(solution)/shard_map/ppermute | solution.py:350
  3.9 17.3 %collective-permute-start.3 = (bf16[128,2048]{1,0:T(8,128)(2,1)S(1)}, bf16[128,2048]{1,0:T(8,128)(2,1)S(1)}, u32[]{:S(2)}, u32[]{:S(2)}) collective-permute-start(bf16[128,2048]{1,0:T(8,128)(2,1)S(1)} %slice_multiply_fusion.tail_ref), channel_id=1, source_target_pairs={{8,12},{9,13},{10,14},{11,15},{24,28},{25,29},{26,30},{27,31}} | collective-permute-start | bytes 1572872 | tf_op jit(solution)/shard_map/ppermute | solution.py:350
  11.5 2.7 %collective-permute-start.1 = (bf16[16,2048]{1,0:T(8,128)(2,1)S(1)}, bf16[16,2048]{1,0:T(8,128)(2,1)S(1)}, u32[]{:S(2)}, u32[]{:S(2)}) collective-permute-start(bf16[16,2048]{1,0:T(8,128)(2,1)S(1)} %get-tuple-element.51), channel_id=1, source_target_pairs={{0,4},{1,5},{2,6},{3,7},{16,20},{17,21},{18,22},{19,23}} | collective-permute-start | bytes 196616 | tf_op jit(solution)/shard_map/ppermute | solution.py:350
  14.2 8.6 %collective-permute-start.5 = (bf16[16,2048]{1,0:T(8,128)(2,1)S(1)}, bf16[16,2048]{1,0:T(8,128)(2,1)S(1)}, u32[]{:S(2)}, u32[]{:S(2)}) collective-permute-start(bf16[16,2048]{1,0:T(8,128)(2,1)S(1)} %joined_sums.1._after), channel_id=1, source_target_pairs={{4,12},{5,13},{6,14},{7,15},{20,28},{21,29},{22,30},{23,31}} | collective-permute-start | bytes 196616 | tf_op jit(solution)/shard_map/ppermute | solution.py:350
  14.9 10.3 %collective-permute-start.4 = (bf16[16,2048]{1,0:T(8,128)(2,1)S(1)}, bf16[16,2048]{1,0:T(8,128)(2,1)S(1)}, u32[]{:S(2)}, u32[]{:S(2)}) collective-permute-start(bf16[16,2048]{1,0:T(8,128)(2,1)S(1)} %joined_sums.1._after), channel_id=1, source_target_pairs={{4,8},{5,9},{6,10},{7,11},{20,24},{21,25},{22,26},{23,27}} | collective-permute-start | bytes 196616 | tf_op jit(solution)/shard_map/ppermute | solution.py:350
  19.9 5.3 %collective-permute-start.6 = (bf16[16,2048]{1,0:T(8,128)(2,1)S(1)}, bf16[16,2048]{1,0:T(8,128)(2,1)S(1)}, u32[]{:S(2)}, u32[]{:S(2)}) collective-permute-start(bf16[16,2048]{1,0:T(8,128)(2,1)S(1)} %get-tuple-element.58), channel_id=1, source_target_pairs={{8,12},{9,13},{10,14},{11,15},{24,28},{25,29},{26,30},{27,31}} | collective-permute-start | bytes 196616 | tf_op jit(solution)/shard_map/ppermute | solution.py:350

commit v8 on v7

--- a/solution.py
+++ b/solution.py
@@ -80,7 +80,7 @@
 
 def local_kernel(
     tail_ref, taps_ref, rate_ref, residue_ref, q_hbm, k_hbm, v_hbm, kli_hbm,
-    mr_ref, part_ref, ulate_ref, late_ref, first_ref, taptab_ref, ends_ref, decay_ref, q_ref, kli_ref,
+    mr_ref, part_ref, ulate_ref, late_ref, taptab_ref, ends_ref, decay_ref, q_ref, kli_ref,
     mr_early_ref, u_early_ref, early_ref, rates_ref, residues_ref,
     k_ref, v_ref, mask_ref, fold_ref, acc_ref, in_sem,
 ):
@@ -122,10 +122,10 @@
 
     def convolve_late(i, at):
         mask = mask_ref[...]
-        acc_ref[half:, at] = jnp.zeros((rows - half, WIDE), F32)
         for first in range(half, rows, width):
             u = tail_ref[first - half : first - half + width, at]
-            acc_ref[first:, at] += dot(taptab_ref[: rows - first, at], spread(u, mask))
+            reached = dot(taptab_ref[: rows - first, at], spread(u, mask))
+            acc_ref[first:, at] = acc_ref[first:, at] + reached if first > half else reached
 
     def convolve_early(i, at):
         mask = mask_ref[...]
@@ -147,11 +147,8 @@
         u_early = mr_early * kli_ref[:half, at]
         u_early_ref[:, at] = u_early
         ends = ends_ref[at, :]
-        late_state = pole_sums(ends, u_late, fold_ref, poles)
-        early_state = pole_sums(ends, u_early, fold_ref, poles)
-        late_ref[:, at] = late_state
-        early_ref[:, at] = early_state
-        first_ref[:, at] = (late_state + early_state * decay_ref[:, at]).astype(BF16)
+        late_ref[:, at] = pole_sums(ends, u_late, fold_ref, poles)
+        early_ref[:, at] = pole_sums(ends, u_early, fold_ref, poles)
 
     pipelined(steps, tables)
     pipelined(steps, convolve_late)
@@ -165,16 +162,18 @@
 
     def work(i, at):
         mask = mask_ref[...]
-        near_ref[:, at] = jnp.zeros((half, WIDE), F32)
         u = u_ref[:, at]
         for first in range(0, half, width):
-            near_ref[first:half, at] += dot(litab_ref[: half - first, at], spread(u[first : first + width], mask))
+            reached = dot(litab_ref[: half - first, at], spread(u[first : first + width], mask))
+            near_ref[first:half, at] = near_ref[first:half, at] + reached if first else reached
 
     return work
 
 
 def filter_kernel(
-    rates_ref, residues_ref, u_ref, qli_hbm, litab_ref, powers_ref, scale_ref, near_ref, qli_ref, mask_ref, sem
+    rates_ref, residues_ref, late_ref, early_ref, decay_ref, qli_hbm,
+    first_ref, litab_ref, powers_ref, scale_ref, qli_ref,
+    mask_ref, sem,
 ):
     half, channels = litab_ref.shape
     poles = rates_ref.shape[0]
@@ -182,6 +181,7 @@
     steps = channels // WIDE
     copy = pltpu.make_async_copy(qli_hbm, qli_ref, sem)
     copy.start()
+    first_ref[...] = (late_ref[...] + early_ref[...] * decay_ref[...]).astype(BF16)
     mask_ref[...] = same_group(width, BF16)
 
     def tables(i, at):
@@ -201,8 +201,13 @@
         causal = iota((half, WIDE), 0) >= iota((half, WIDE), 1) % width
         litab_ref[:, at] = jnp.where(causal, li_taps, 0.0).astype(BF16)
 
-    pipelined(steps, tables, near_rows(u_ref, litab_ref, near_ref, mask_ref, width))
+    pipelined(steps, tables)
     copy.wait()
+
+
+def near_late_kernel(u_ref, litab_ref, near_ref, mask_ref):
+    mask_ref[...] = same_group(CHUNK, BF16)
+    pipelined(u_ref.shape[1] // WIDE, near_rows(u_ref, litab_ref, near_ref, mask_ref, CHUNK))
 
 
 def rim_rows(
@@ -217,9 +222,10 @@
     def convolve(i, at):
         mask = mask_ref[...]
         rim = rim_ref[:, at]
-        acc_ref[:, at] = part_ref[:, at]
         for first in range(half - width, -1, -width):
-            acc_ref[: first + width, at] += dot(taptab_ref[half - first :, at], spread(rim[first : first + width], mask))
+            reached = dot(taptab_ref[half - first :, at], spread(rim[first : first + width], mask))
+            before_ref = part_ref if first == half - width else acc_ref
+            acc_ref[: first + width, at] = before_ref[: first + width, at] + reached
 
     def gate(i, at):
         mr = (q_ref[:half, at].astype(F32) * acc_ref[:, at]).astype(BF16)
@@ -354,7 +360,7 @@
     else:
         rims = [shifted(tail, "ctx", 1)]
 
-    mr_late, part, u_late, late, first, taptab, ends, decay, q, kli, *without_rim, rates, residues = call(
+    mr_late, part, u_late, late, taptab, ends, decay, q, kli, *without_rim, rates, residues = call(
         local_kernel,
         "local_rows",
         [vmem] * 4 + [hbm] * 4,
@@ -363,7 +369,6 @@
             pltpu.VMEM(short, F32),
             pltpu.VMEM(short, BF16),
             pltpu.VMEM(pole_sum, F32),
-            pltpu.VMEM(pole_sum, BF16),
             pltpu.VMEM((half + width, channels), BF16),
             pltpu.VMEM((channels, half), BF16),
             pltpu.VMEM(pole_sum, F32),
@@ -388,23 +393,26 @@
         *in_hbm(q_mr, k_mr, v_mr, k_li),
     )
 
-    before = send(first, (0, 1)) if by_place else None
-
-    litab, powers, scale, near_late, qli = call(
+    first, litab, powers, scale, qli = call(
         filter_kernel,
         "filter_tables",
-        [vmem] * 3 + [hbm],
+        [vmem] * 5 + [hbm],
         [
-            pltpu.VMEM(short, BF16),
-            pltpu.VMEM(short, BF16),
-            pltpu.VMEM(pole_sum, F32),
-            pltpu.VMEM(short, F32),
+            pltpu.VMEM(pole_sum, BF16),
+            pltpu.VMEM(short, BF16),
+            pltpu.VMEM(short, BF16),
+            pltpu.VMEM(pole_sum, F32),
             pltpu.VMEM(tall, BF16),
         ],
         [mask, dma(())],
         10**6,
-        rates, residues, u_late, *in_hbm(q_li),
-    )
+        rates, residues, late, without_rim[2], decay, *in_hbm(q_li),
+    )
+    (near_late,) = call(
+        near_late_kernel, "near_late", [vmem] * 2, [pltpu.VMEM(short, F32)], [mask], 10**6, u_late, litab
+    )
+
+    before = send(first, (0, 1)) if by_place else None
 
     own = (part, q, kli, taptab, ends)
 
@@ -425,7 +433,7 @@
         )
 
     if by_place:
-        total_1, *rim_1 = with_rim(1, rims[0], scale, F32)
+        total_1, *rim_1 = with_rim(1, rims[0], near_late, F32)
         (total_1,) = call(
             joined_kernel,
             "joined_sums",
@@ -442,7 +450,7 @@
         arrived = [entered, send(total_2, (2, 3))]
         early_rows, places = (*without_rim, *rim_1, *rim_2), (0, 1, 2)
     else:
-        total, *early_rows = with_rim(None, rims[0], scale, BF16)
+        total, *early_rows = with_rim(None, rims[0], near_late, BF16)
         places = (None,)
         reach = min(3, max(peers - 1, 1))
         arrived = [shifted(total, "ctx", by) for by in range(1, reach + 1)]

time: 26.8 us -> 26.3 us (0.981)
  waiting for transfers between devices: 4.37 us -> 2.72 us
  Pallas kernels: 11.2 us -> 12.4 us
    ppermute x7, waiting for transfers between devices: 4.37 us -> 2.72 us  [body(): send = lambda array, *pairs: lax.ppermute(array, 'ctx', pairs)]
    pallas_call x7 -> x8, Pallas kernels: 11.2 us -> 12.4 us  [call(): pl.pallas_call(kernel, in_specs=ins, out_specs=[hbm if isinstance(out, ja...]
  transfers between devices with their start and end apart: 7 -> 7, of which waited for: 2 -> 2; matrix products, arithmetic and copies ran while one was open for 0% -> 0% of each run, Pallas kernels for 37% -> 43%
where the time goes in v8:
time: 26.3 us; the launch traced here: 26 us
  Pallas kernels  12.4 us (47%)
  starting transfers between devices  8.82 us (34%)
  waiting for transfers between devices  2.72 us (10%)
  other arithmetic  1.3 us (5%)
  between operations  0.81 us (3%)
    pallas_call x8, Pallas kernels, call(): pl.pallas_call(kernel, in_specs=ins, out_specs=[hbm if isinstance(out, ja...  12.4 us
    ppermute x7, starting transfers between devices, body(): send = lambda array, *pairs: lax.ppermute(array, 'ctx', pairs)  8.82 us
    ppermute x7, waiting for transfers between devices, body(): send = lambda array, *pairs: lax.ppermute(array, 'ctx', pairs)  2.72 us
    mul x1, other arithmetic, body(): tail = k_mr[half:] * v_mr[half:]  1.27 us
  transfers between devices with their start and end apart: 7, of which 2 were waited for; matrix products, arithmetic and copies ran while one was open for 0% of the time, Pallas kernels for 43%

profile of v8, /device:TPU:18, one launch (start us, length us, event | category | flops | bytes accessed | tf_op | source)
XLA Modules:
  0.0 26.0 jit_solution(11404210305813536380)
XLA Ops:
  0.7 1.3 %slice_multiply_fusion.tail_ref = bf16[128,2048]{1,0:T(8,128)(2,1)S(1)} fusion(bf16[256,2048]{1,0:T(8,128)(2,1)} %v_hbm.1, bf16[256,2048]{1,0:T(8,128)(2,1)} %k_hbm.1), kind=kLoop, calls=%fused_computation | loop fusion | flops 262144 | bytes 1572864 | tf_op jit(solution)/shard_map/mul | solution.py:354
  1.9 0.7 %collective-permute-start = (bf16[128,2048]{1,0:T(8,128)(2,1)S(1)}, bf16[128,2048]{1,0:T(8,128)(2,1)S(1)}, u32[]{:S(2)}, u32[]{:S(2)}) collective-permute-start(bf16[128,2048]{1,0:T(8,128)(2,1)S(1)} %slice_multiply_fusion.tail_ref), channel_id=1, source_target_pairs={{0,4},{1,5},{2,6},{3,7},{16,20},{17,21},{18,22},{19,23}} | collective-permute-start | bytes 1572872 | tf_op jit(solution)/shard_map/ppermute | solution.py:356
  2.6 1.3 %collective-permute-start.2 = (bf16[128,2048]{1,0:T(8,128)(2,1)S(1)}, bf16[128,2048]{1,0:T(8,128)(2,1)S(1)}, u32[]{:S(2)}, u32[]{:S(2)}) collective-permute-start(bf16[128,2048]{1,0:T(8,128)(2,1)S(1)} %slice_multiply_fusion.tail_ref), channel_id=1, source_target_pairs={{4,8},{5,9},{6,10},{7,11},{20,24},{21,25},{22,26},{23,27}} | collective-permute-start | bytes 1572872 | tf_op jit(solution)/shard_map/ppermute | solution.py:356
  3.9 2.9 %collective-permute-start.3 = (bf16[128,2048]{1,0:T(8,128)(2,1)S(1)}, bf16[128,2048]{1,0:T(8,128)(2,1)S(1)}, u32[]{:S(2)}, u32[]{:S(2)}) collective-permute-start(bf16[128,2048]{1,0:T(8,128)(2,1)S(1)} %slice_multiply_fusion.tail_ref), channel_id=1, source_target_pairs={{8,12},{9,13},{10,14},{11,15},{24,28},{25,29},{26,30},{27,31}} | collective-permute-start | bytes 1572872 | tf_op jit(solution)/shard_map/ppermute | solution.py:356
  6.9 0.0 copy-done.2
  6.9 0.0 copy-done.1
  6.9 0.0 copy-done
  6.9 5.0 %local_rows.1 = (bf16[128,2048]{1,0:T(8,128)(2,1)S(1)}, f32[128,2048]{1,0:T(8,128)S(1)}, bf16[128,2048]{1,0:T(8,128)(2,1)S(1)}, f32[16,2048]{1,0:T(8,128)S(1)}, ...) custom-call(bf16[128,2048]{1,0:T(8,128)(2,1)S(1)} %slice_multiply_fu, ...), custom_call_target="tpu_custom_call" | custom-call | flops 4000000000 | bytes 4000000 | tf_op jit(solution)/shard_map/local_rows/pallas_call | solution.py:343
  11.9 1.2 %filter_tables.1 = (bf16[16,2048]{1,0:T(8,128)(2,1)S(1)}, bf16[128,2048]{1,0:T(8,128)(2,1)S(1)}, bf16[128,2048]{1,0:T(8,128)(2,1)S(1)}, f32[16,2048]{1,0:T(8,128)S(1)}, bf16[256,2048]{1,0:T(8,128)(2,1)S(1)}) custom-call(f32[16,2048]{1,0:T(8,128)S(1)} %get-tuple-element.38.rates_ref, f32[16,2048]{1,0:T(8,128)S(1)} %get-tuple-element.39.residues_ref, ...), custom_call_target="tpu_custom_call" | custom-call | flops 1000000 | bytes 1000 | tf_op jit(solution)/shard_map/filter_tables/pallas_call | solution.py:343
  13.2 0.7 %collective-permute-start.1 = (bf16[16,2048]{1,0:T(8,128)(2,1)S(1)}, bf16[16,2048]{1,0:T(8,128)(2,1)S(1)}, u32[]{:S(2)}, u32[]{:S(2)}) collective-permute-start(bf16[16,2048]{1,0:T(8,128)(2,1)S(1)} %get-tuple-element.50), channel_id=1, source_target_pairs={{0,4},{1,5},{2,6},{3,7},{16,20},{17,21},{18,22},{19,23}} | collective-permute-start | bytes 196616 | tf_op jit(solution)/shard_map/ppermute | solution.py:356
  13.8 1.5 %near_late.1._after.refs_4_ = f32[128,2048]{1,0:T(8,128)S(1)} custom-call(bf16[128,2048]{1,0:T(8,128)(2,1)S(1)} %get-tuple-element.37.u_ref, bf16[128,2048]{1,0:T(8,128)(2,1)S(1)} %get-tuple-element.40.litab_ref.refs_16_), custom_call_target="tpu_custom_call" | custom-call | flops 1000000 | bytes 1000 | tf_op jit(solution)/shard_map/near_late/pallas_call | solution.py:343
  15.3 0.0 collective-permute-done.refs_0_
  15.3 0.0 collective-permute-done.1.before_ref
  15.4 0.7 %collective-permute-start.5 = (bf16[16,2048]{1,0:T(8,128)(2,1)S(1)}, bf16[16,2048]{1,0:T(8,128)(2,1)S(1)}, u32[]{:S(2)}, u32[]{:S(2)}) collective-permute-start(bf16[16,2048]{1,0:T(8,128)(2,1)S(1)} %joined_sums.1._after), channel_id=1, source_target_pairs={{4,12},{5,13},{6,14},{7,15},{20,28},{21,29},{22,30},{23,31}} | collective-permute-start | bytes 196616 | tf_op jit(solution)/shard_map/ppermute | solution.py:356
  16.1 1.3 %collective-permute-start.4 = (bf16[16,2048]{1,0:T(8,128)(2,1)S(1)}, bf16[16,2048]{1,0:T(8,128)(2,1)S(1)}, u32[]{:S(2)}, u32[]{:S(2)}) collective-permute-start(bf16[16,2048]{1,0:T(8,128)(2,1)S(1)} %joined_sums.1._after), channel_id=1, source_target_pairs={{4,8},{5,9},{6,10},{7,11},{20,24},{21,25},{22,26},{23,27}} | collective-permute-start | bytes 196616 | tf_op jit(solution)/shard_map/ppermute | solution.py:356
  17.4 0.8 %collective-permute-done.2.refs_0_ = bf16[128,2048]{1,0:T(8,128)(2,1)S(1)} collective-permute-done((bf16[128,2048]{1,0:T(8,128)(2,1)S(1)}, bf16[128,2048]{1,0:T(8,128)(2,1)S(1)}, u32[]{:S(2)}, u32[]{:S(2)}) %collective-permute-start.2) | collective-permute-done | bytes 524320 | tf_op jit(solution)/shard_map/ppermute | solution.py:356
  18.2 1.7 %rim_rows.3 = (bf16[16,2048]{1,0:T(8,128)(2,1)S(1)}, bf16[128,2048]{1,0:T(8,128)(2,1)S(1)}, bf16[128,2048]{1,0:T(8,128)(2,1)S(1)}, f32[16,2048]{1,0:T(8,128)S(1)}) custom-call(f32[16,2048]{1,0:T(8,128)S(1)} %get-tuple-element.35.late_ref, f32[16,2048]{1,0:T(8,128)S(1)} %get-tuple-element.36.decay_ref.refs_7_, bf16[16,2048]{1,0:T(8,128)(2,1)S(1)} %joined_sums.1._after, ...), custom_call_target="tpu_custom_call" | custom-call | flops 1000000 | bytes 1000 | tf_op jit(solution)/shard_map/rim_rows/pallas_call | solution.py:343
  19.9 1.3 %collective-permute-start.6 = (bf16[16,2048]{1,0:T(8,128)(2,1)S(1)}, bf16[16,2048]{1,0:T(8,128)(2,1)S(1)}, u32[]{:S(2)}, u32[]{:S(2)}) collective-permute-start(bf16[16,2048]{1,0:T(8,128)(2,1)S(1)} %get-tuple-element.56), channel_id=1, source_target_pairs={{8,12},{9,13},{10,14},{11,15},{24,28},{25,29},{26,30},{27,31}} | collective-permute-start | bytes 196616 | tf_op jit(solution)/shard_map/ppermute | solution.py:356
  21.2 0.0 collective-permute-done.3.refs_9_
  21.2 1.6 %near_part.1 = (f32[16,2048]{1,0:T(8,128)S(1)}, f32[128,2048]{1,0:T(8,128)S(1)}, bf16[256,2048]{1,0:T(8,128)(2,1)}) custom-call(bf16[128,2048]{1,0:T(8,128)(2,1)S(1)} %get-tuple-element.32.refs_0_, bf16[128,2048]{1,0:T(8,128)(2,1)S(1)} %get-tuple-element.33.refs_1_, f32[16,2048]{1,0:T(8,128)S(1)} %get-tuple-element.34.early_ref.refs_2_, ...), custom_call_target="tpu_custom_call" | custom-call | flops 1000000 | bytes 1000 | tf_op jit(solution)/shard_map/near_part/pallas_call | solution.py:343
  22.8 0.0 collective-permute-done.5
  22.9 1.9 %collective-permute-done.4 = bf16[16,2048]{1,0:T(8,128)(2,1)S(1)} collective-permute-done((bf16[16,2048]{1,0:T(8,128)(2,1)S(1)}, bf16[16,2048]{1,0:T(8,128)(2,1)S(1)}, u32[]{:S(2)}, u32[]{:S(2)}) %collective-permute-start.4) | collective-permute-done | bytes 65568 | tf_op jit(solution)/shard_map/ppermute | solution.py:356
  24.8 0.0 collective-permute-done.6.refs_1_
  24.8 1.3 %far_rows.1 = bf16[256,2048]{1,0:T(8,128)(2,1)} custom-call(f32[16,2048]{1,0:T(8,128)S(1)} %multiply_add_fusion.refs_0_, bf16[16,2048]{1,0:T(8,128)(2,1)S(1)} %collective-permute-done.6.refs_1_, bf16[256,2048]{1,0:T(8,128)(2,1)S(1)} %get-tuple-element.57.refs_2_, f32[128,2048]{1,0:T(8,128)S(1)} %get-tuple-element.58.refs_3_, ...), custom_call_target="tpu_custom_call" | custom-call | flops 1000000000 | bytes 1000000 | tf_op jit(solution)/shard_map/far_rows/pallas_call | solution.py:343
  (6 shorter events, 0.1 us)
Async XLA Ops:
  0.6 6.2 %copy-start.2 = (f32[128,16]{0,1:T(8,128)S(1)}, f32[128,16]{0,1:T(8,128)}, u32[]{:S(2)}) copy-start(f32[128,16]{0,1:T(8,128)} %param.15) | copy-start | bytes 24580
  0.6 6.2 %copy-start.1 = (f32[128,16]{0,1:T(8,128)S(1)}, f32[128,16]{0,1:T(8,128)}, u32[]{:S(2)}) copy-start(f32[128,16]{0,1:T(8,128)} %param.14) | copy-start | bytes 24580
  0.7 6.2 %copy-start = (bf16[128,128]{1,0:T(8,128)(2,1)S(1)}, bf16[128,128]{1,0:T(8,128)(2,1)}, u32[]{:S(2)}) copy-start(bf16[128,128]{1,0:T(8,128)(2,1)} %taps_ref.1) | copy-start | bytes 98308
  1.9 13.4 %collective-permute-start = (bf16[128,2048]{1,0:T(8,128)(2,1)S(1)}, bf16[128,2048]{1,0:T(8,128)(2,1)S(1)}, u32[]{:S(2)}, u32[]{:S(2)}) collective-permute-start(bf16[128,2048]{1,0:T(8,128)(2,1)S(1)} %slice_multiply_fusion.tail_ref), channel_id=1, source_target_pairs={{0,4},{1,5},{2,6},{3,7},{16,20},{17,21},{18,22},{19,23}} | collective-permute-start | bytes 1572872 | tf_op jit(solution)/shard_map/ppermute | solution.py:356
  2.6 15.6 %collective-permute-start.2 = (bf16[128,2048]{1,0:T(8,128)(2,1)S(1)}, bf16[128,2048]{1,0:T(8,128)(2,1)S(1)}, u32[]{:S(2)}, u32[]{:S(2)}) collective-permute-start(bf16[128,2048]{1,0:T(8,128)(2,1)S(1)} %slice_multiply_fusion.tail_ref), channel_id=1, source_target_pairs={{4,8},{5,9},{6,10},{7,11},{20,24},{21,25},{22,26},{23,27}} | collective-permute-start | bytes 1572872 | tf_op jit(solution)/shard_map/ppermute | solution.py:356
  3.9 17.3 %collective-permute-start.3 = (bf16[128,2048]{1,0:T(8,128)(2,1)S(1)}, bf16[128,2048]{1,0:T(8,128)(2,1)S(1)}, u32[]{:S(2)}, u32[]{:S(2)}) collective-permute-start(bf16[128,2048]{1,0:T(8,128)(2,1)S(1)} %slice_multiply_fusion.tail_ref), channel_id=1, source_target_pairs={{8,12},{9,13},{10,14},{11,15},{24,28},{25,29},{26,30},{27,31}} | collective-permute-start | bytes 1572872 | tf_op jit(solution)/shard_map/ppermute | solution.py:356
  13.2 2.2 %collective-permute-start.1 = (bf16[16,2048]{1,0:T(8,128)(2,1)S(1)}, bf16[16,2048]{1,0:T(8,128)(2,1)S(1)}, u32[]{:S(2)}, u32[]{:S(2)}) collective-permute-start(bf16[16,2048]{1,0:T(8,128)(2,1)S(1)} %get-tuple-element.50), channel_id=1, source_target_pairs={{0,4},{1,5},{2,6},{3,7},{16,20},{17,21},{18,22},{19,23}} | collective-permute-start | bytes 196616 | tf_op jit(solution)/shard_map/ppermute | solution.py:356
  15.4 7.5 %collective-permute-start.5 = (bf16[16,2048]{1,0:T(8,128)(2,1)S(1)}, bf16[16,2048]{1,0:T(8,128)(2,1)S(1)}, u32[]{:S(2)}, u32[]{:S(2)}) collective-permute-start(bf16[16,2048]{1,0:T(8,128)(2,1)S(1)} %joined_sums.1._after), channel_id=1, source_target_pairs={{4,12},{5,13},{6,14},{7,15},{20,28},{21,29},{22,30},{23,31}} | collective-permute-start | bytes 196616 | tf_op jit(solution)/shard_map/ppermute | solution.py:356
  16.1 8.7 %collective-permute-start.4 = (bf16[16,2048]{1,0:T(8,128)(2,1)S(1)}, bf16[16,2048]{1,0:T(8,128)(2,1)S(1)}, u32[]{:S(2)}, u32[]{:S(2)}) collective-permute-start(bf16[16,2048]{1,0:T(8,128)(2,1)S(1)} %joined_sums.1._after), channel_id=1, source_target_pairs={{4,8},{5,9},{6,10},{7,11},{20,24},{21,25},{22,26},{23,27}} | collective-permute-start | bytes 196616 | tf_op jit(solution)/shard_map/ppermute | solution.py:356
  19.9 4.9 %collective-permute-start.6 = (bf16[16,2048]{1,0:T(8,128)(2,1)S(1)}, bf16[16,2048]{1,0:T(8,128)(2,1)S(1)}, u32[]{:S(2)}, u32[]{:S(2)}) collective-permute-start(bf16[16,2048]{1,0:T(8,128)(2,1)S(1)} %get-tuple-element.56), channel_id=1, source_target_pairs={{8,12},{9,13},{10,14},{11,15},{24,28},{25,29},{26,30},{27,31}} | collective-permute-start | bytes 196616 | tf_op jit(solution)/shard_map/ppermute | solution.py:356

commit v9 on v8

--- a/solution.py
+++ b/solution.py
@@ -78,7 +78,50 @@
     return jnp.concatenate(parts, axis=1)
 
 
-def local_kernel(
+def last_products(k_hbm, v_hbm, tail_ref, k_ref, v_ref, sem):
+    half, channels = tail_ref.shape
+    last = pl.ds(k_hbm.shape[0] - half, half)
+    pieces = (slice(0, channels // 2), slice(channels // 2, channels))
+    copies = [
+        (
+            pltpu.make_async_copy(k_hbm.at[last, at], k_ref.at[:, at], sem.at[0, n]),
+            pltpu.make_async_copy(v_hbm.at[last, at], v_ref.at[:, at], sem.at[1, n]),
+        )
+        for n, at in enumerate(pieces)
+    ]
+    for pair in copies:
+        for copy in pair:
+            copy.start()
+    for pair, at in zip(copies, pieces):
+        for copy in pair:
+            copy.wait()
+        tail_ref[:, at] = k_ref[:, at] * v_ref[:, at]
+
+
+def tail_kernel(place, _after, *refs):
+    pl.when(lax.axis_index("ctx") == place)(lambda: last_products(*refs))
+
+
+def local_kernel(count, *refs):
+    tails, refs = refs[:count], refs[count:]
+    if count > 1:
+        *refs, tail_ref, tail_sem = refs
+        k_hbm, v_hbm = refs[4:6]
+        k_ref, v_ref = refs[-6:-4]
+        at = lax.axis_index("ctx")
+        for place, ref in enumerate(tails):
+
+            @pl.when(at == place)
+            def _():
+                tail_ref[...] = ref[...]
+
+        pl.when(at == count)(lambda: last_products(k_hbm, v_hbm, tail_ref, k_ref, v_ref, tail_sem))
+    else:
+        (tail_ref,) = tails
+    local_rows(tail_ref, *refs)
+
+
+def local_rows(
     tail_ref, taps_ref, rate_ref, residue_ref, q_hbm, k_hbm, v_hbm, kli_hbm,
     mr_ref, part_ref, ulate_ref, late_ref, taptab_ref, ends_ref, decay_ref, q_ref, kli_ref,
     mr_early_ref, u_early_ref, early_ref, rates_ref, residues_ref,
@@ -351,19 +394,31 @@
             name=name,
         )(*operands)
 
-    tail = k_mr[half:] * v_mr[half:]
     peers = lax.axis_size("ctx")
     send = lambda array, *pairs: lax.ppermute(array, "ctx", pairs)
     by_place = peers == 4
     if by_place:
-        rims = [send(tail, (at, at + 1)) for at in range(3)]
+        tails = []
+        for place in range(3):
+            tails += call(
+                functools.partial(tail_kernel, place),
+                "tail_rows",
+                [vmem if tails else hbm] + [hbm] * 2,
+                [pltpu.VMEM(short, BF16)],
+                [pltpu.VMEM(short, BF16), pltpu.VMEM(short, BF16), dma((2, 2))],
+                10**6,
+                tails[-1] if tails else in_hbm(k_mr)[0], *in_hbm(k_mr, v_mr),
+            )
+        rims = [send(tail, (at, at + 1)) for at, tail in enumerate(tails)]
     else:
+        tail = k_mr[half:] * v_mr[half:]
+        tails = [tail]
         rims = [shifted(tail, "ctx", 1)]
 
     mr_late, part, u_late, late, taptab, ends, decay, q, kli, *without_rim, rates, residues = call(
-        local_kernel,
+        functools.partial(local_kernel, len(tails)),
         "local_rows",
-        [vmem] * 4 + [hbm] * 4,
+        [vmem] * (len(tails) + 3) + [hbm] * 4,
         [
             pltpu.VMEM(short, BF16),
             pltpu.VMEM(short, F32),
@@ -387,9 +442,10 @@
             fold,
             pltpu.VMEM(tall, F32),
             dma((4,)),
+            *[pltpu.VMEM(short, BF16), dma((2, 2))] * (len(tails) > 1),
         ],
         4 * 10**9,
-        tail, mr_taps, li_rate.T, li_residue.T,
+        *tails, mr_taps, li_rate.T, li_residue.T,
         *in_hbm(q_mr, k_mr, v_mr, k_li),
     )
 

time: 26.3 us -> 25.3 us (0.962)
  other arithmetic: 1.3 us -> 0.03 us
  starting transfers between devices: 8.82 us -> 7.74 us
  Pallas kernels: 12.4 us -> 13.2 us
  waiting for transfers between devices: 2.72 us -> 3.15 us
    mul x1 -> x0, other arithmetic: 1.27 us -> none  [body(): tail = k_mr[half:] * v_mr[half:]]
    ppermute x7, starting transfers between devices: 8.82 us -> 7.74 us  [body(): send = lambda array, *pairs: lax.ppermute(array, 'ctx', pairs)]
    pallas_call x8 -> x11, Pallas kernels: 12.4 us -> 13.2 us  [call(): pl.pallas_call(kernel, in_specs=ins, out_specs=[hbm if isinstance(out, ja...]
    ppermute x7, waiting for transfers between devices: 2.72 us -> 3.15 us  [body(): send = lambda array, *pairs: lax.ppermute(array, 'ctx', pairs)]
  transfers between devices with their start and end apart: 7 -> 7, of which waited for: 2 -> 2; matrix products, arithmetic and copies ran while one was open for 0% -> 0% of each run, Pallas kernels for 43% -> 48%
where the time goes in v9:
time: 25.3 us; the launch traced here: 25 us
  Pallas kernels  13.2 us (52%)
  starting transfers between devices  7.74 us (31%)
  waiting for transfers between devices  3.15 us (12%)
  between operations  0.83 us (3%)
    pallas_call x11, Pallas kernels, call(): pl.pallas_call(kernel, in_specs=ins, out_specs=[hbm if isinstance(out, ja...  13.2 us
    ppermute x7, starting transfers between devices, body(): send = lambda array, *pairs: lax.ppermute(array, 'ctx', pairs)  7.74 us
    ppermute x7, waiting for transfers between devices, body(): send = lambda array, *pairs: lax.ppermute(array, 'ctx', pairs)  3.15 us
  transfers between devices with their start and end apart: 7, of which 2 were waited for; matrix products, arithmetic and copies ran while one was open for 0% of the time, Pallas kernels for 48%

profile of v9, /device:TPU:18, one launch (start us, length us, event | category | flops | bytes accessed | tf_op | source)
XLA Modules:
  0.0 25.0 jit_solution(2038192762664795649)
XLA Ops:
  0.6 0.1 tail_rows.3._after.refs_0_
  0.7 0.7 %collective-permute-start = (bf16[128,2048]{1,0:T(8,128)(2,1)S(1)}, bf16[128,2048]{1,0:T(8,128)(2,1)S(1)}, u32[]{:S(2)}, u32[]{:S(2)}) collective-permute-start(bf16[128,2048]{1,0:T(8,128)(2,1)S(1)} %tail_rows.3._after.refs_0_), channel_id=1, source_target_pairs={{0,4},{1,5},{2,6},{3,7},{16,20},{17,21},{18,22},{19,23}} | collective-permute-start | bytes 1572872 | tf_op jit(solution)/shard_map/ppermute | solution.py:398
  1.4 0.1 tail_rows.4._after.refs_1_
  1.5 0.0 copy-start
  1.5 0.0 copy-start.1
  1.5 0.0 copy-start.2
  1.5 1.4 %collective-permute-start.2 = (bf16[128,2048]{1,0:T(8,128)(2,1)S(1)}, bf16[128,2048]{1,0:T(8,128)(2,1)S(1)}, u32[]{:S(2)}, u32[]{:S(2)}) collective-permute-start(bf16[128,2048]{1,0:T(8,128)(2,1)S(1)} %tail_rows.4._after.refs_1_), channel_id=1, source_target_pairs={{4,8},{5,9},{6,10},{7,11},{20,24},{21,25},{22,26},{23,27}} | collective-permute-start | bytes 1572872 | tf_op jit(solution)/shard_map/ppermute | solution.py:398
  2.9 1.3 %tail_rows.5.refs_2_ = bf16[128,2048]{1,0:T(8,128)(2,1)S(1)} custom-call(bf16[128,2048]{1,0:T(8,128)(2,1)S(1)} %tail_rows.4._after.refs_1_, bf16[256,2048]{1,0:T(8,128)(2,1)} %refs_7_.1, bf16[256,2048]{1,0:T(8,128)(2,1)} %refs_8_.1), custom_call_target="tpu_custom_call" | custom-call | flops 1000000 | bytes 1000 | tf_op jit(solution)/shard_map/tail_rows/pallas_call | solution.py:386
  4.2 1.7 %collective-permute-start.3 = (bf16[128,2048]{1,0:T(8,128)(2,1)S(1)}, bf16[128,2048]{1,0:T(8,128)(2,1)S(1)}, u32[]{:S(2)}, u32[]{:S(2)}) collective-permute-start(bf16[128,2048]{1,0:T(8,128)(2,1)S(1)} %tail_rows.5.refs_2_), channel_id=1, source_target_pairs={{8,12},{9,13},{10,14},{11,15},{24,28},{25,29},{26,30},{27,31}} | collective-permute-start | bytes 1572872 | tf_op jit(solution)/shard_map/ppermute | solution.py:398
  5.9 4.5 %local_rows.1 = (bf16[128,2048]{1,0:T(8,128)(2,1)S(1)}, f32[128,2048]{1,0:T(8,128)S(1)}, bf16[128,2048]{1,0:T(8,128)(2,1)S(1)}, f32[16,2048]{1,0:T(8,128)S(1)}, ...) custom-call(bf16[128,2048]{1,0:T(8,128)(2,1)S(1)} %tail_rows.3._afte, ...), custom_call_target="tpu_custom_call" | custom-call | flops 4000000000 | bytes 4000000 | tf_op jit(solution)/shard_map/local_rows/pallas_call | solution.py:386
  10.5 1.2 %filter_tables.1 = (bf16[16,2048]{1,0:T(8,128)(2,1)S(1)}, bf16[128,2048]{1,0:T(8,128)(2,1)S(1)}, bf16[128,2048]{1,0:T(8,128)(2,1)S(1)}, f32[16,2048]{1,0:T(8,128)S(1)}, bf16[256,2048]{1,0:T(8,128)(2,1)S(1)}) custom-call(f32[16,2048]{1,0:T(8,128)S(1)} %get-tuple-element.38.rates_ref, f32[16,2048]{1,0:T(8,128)S(1)} %get-tuple-element.39.residues_ref, ...), custom_call_target="tpu_custom_call" | custom-call | flops 1000000 | bytes 1000 | tf_op jit(solution)/shard_map/filter_tables/pallas_call | solution.py:386
  11.7 0.7 %collective-permute-start.1 = (bf16[16,2048]{1,0:T(8,128)(2,1)S(1)}, bf16[16,2048]{1,0:T(8,128)(2,1)S(1)}, u32[]{:S(2)}, u32[]{:S(2)}) collective-permute-start(bf16[16,2048]{1,0:T(8,128)(2,1)S(1)} %get-tuple-element.50), channel_id=1, source_target_pairs={{0,4},{1,5},{2,6},{3,7},{16,20},{17,21},{18,22},{19,23}} | collective-permute-start | bytes 196616 | tf_op jit(solution)/shard_map/ppermute | solution.py:398
  12.4 1.5 %near_late.1._after.refs_4_ = f32[128,2048]{1,0:T(8,128)S(1)} custom-call(bf16[128,2048]{1,0:T(8,128)(2,1)S(1)} %get-tuple-element.37.u_ref, bf16[128,2048]{1,0:T(8,128)(2,1)S(1)} %get-tuple-element.40.litab_ref.refs_16_), custom_call_target="tpu_custom_call" | custom-call | flops 1000000 | bytes 1000 | tf_op jit(solution)/shard_map/near_late/pallas_call | solution.py:386
  13.9 0.0 collective-permute-done.refs_0_
  13.9 0.0 collective-permute-done.1.before_ref
  13.9 0.7 %collective-permute-start.5 = (bf16[16,2048]{1,0:T(8,128)(2,1)S(1)}, bf16[16,2048]{1,0:T(8,128)(2,1)S(1)}, u32[]{:S(2)}, u32[]{:S(2)}) collective-permute-start(bf16[16,2048]{1,0:T(8,128)(2,1)S(1)} %joined_sums.1._after), channel_id=1, source_target_pairs={{4,12},{5,13},{6,14},{7,15},{20,28},{21,29},{22,30},{23,31}} | collective-permute-start | bytes 196616 | tf_op jit(solution)/shard_map/ppermute | solution.py:398
  14.6 1.3 %collective-permute-start.4 = (bf16[16,2048]{1,0:T(8,128)(2,1)S(1)}, bf16[16,2048]{1,0:T(8,128)(2,1)S(1)}, u32[]{:S(2)}, u32[]{:S(2)}) collective-permute-start(bf16[16,2048]{1,0:T(8,128)(2,1)S(1)} %joined_sums.1._after), channel_id=1, source_target_pairs={{4,8},{5,9},{6,10},{7,11},{20,24},{21,25},{22,26},{23,27}} | collective-permute-start | bytes 196616 | tf_op jit(solution)/shard_map/ppermute | solution.py:398
  15.9 1.3 %collective-permute-done.2.refs_0_ = bf16[128,2048]{1,0:T(8,128)(2,1)S(1)} collective-permute-done((bf16[128,2048]{1,0:T(8,128)(2,1)S(1)}, bf16[128,2048]{1,0:T(8,128)(2,1)S(1)}, u32[]{:S(2)}, u32[]{:S(2)}) %collective-permute-start.2) | collective-permute-done | bytes 524320 | tf_op jit(solution)/shard_map/ppermute | solution.py:398
  17.2 1.7 %rim_rows.3 = (bf16[16,2048]{1,0:T(8,128)(2,1)S(1)}, bf16[128,2048]{1,0:T(8,128)(2,1)S(1)}, bf16[128,2048]{1,0:T(8,128)(2,1)S(1)}, f32[16,2048]{1,0:T(8,128)S(1)}) custom-call(f32[16,2048]{1,0:T(8,128)S(1)} %get-tuple-element.35.late_ref, f32[16,2048]{1,0:T(8,128)S(1)} %get-tuple-element.36.decay_ref.refs_7_, bf16[16,2048]{1,0:T(8,128)(2,1)S(1)} %joined_sums.1._after, ...), custom_call_target="tpu_custom_call" | custom-call | flops 1000000 | bytes 1000 | tf_op jit(solution)/shard_map/rim_rows/pallas_call | solution.py:386
  18.9 1.3 %collective-permute-start.6 = (bf16[16,2048]{1,0:T(8,128)(2,1)S(1)}, bf16[16,2048]{1,0:T(8,128)(2,1)S(1)}, u32[]{:S(2)}, u32[]{:S(2)}) collective-permute-start(bf16[16,2048]{1,0:T(8,128)(2,1)S(1)} %get-tuple-element.56), channel_id=1, source_target_pairs={{8,12},{9,13},{10,14},{11,15},{24,28},{25,29},{26,30},{27,31}} | collective-permute-start | bytes 196616 | tf_op jit(solution)/shard_map/ppermute | solution.py:398
  20.2 0.0 collective-permute-done.3.refs_9_
  20.2 1.6 %near_part.1 = (f32[16,2048]{1,0:T(8,128)S(1)}, f32[128,2048]{1,0:T(8,128)S(1)}, bf16[256,2048]{1,0:T(8,128)(2,1)}) custom-call(bf16[128,2048]{1,0:T(8,128)(2,1)S(1)} %get-tuple-element.32.refs_0_, bf16[128,2048]{1,0:T(8,128)(2,1)S(1)} %get-tuple-element.33.refs_1_, f32[16,2048]{1,0:T(8,128)S(1)} %get-tuple-element.34.early_ref.refs_2_, ...), custom_call_target="tpu_custom_call" | custom-call | flops 1000000 | bytes 1000 | tf_op jit(solution)/shard_map/near_part/pallas_call | solution.py:386
  21.8 1.8 %collective-permute-done.4 = bf16[16,2048]{1,0:T(8,128)(2,1)S(1)} collective-permute-done((bf16[16,2048]{1,0:T(8,128)(2,1)S(1)}, bf16[16,2048]{1,0:T(8,128)(2,1)S(1)}, u32[]{:S(2)}, u32[]{:S(2)}) %collective-permute-start.4) | collective-permute-done | bytes 65568 | tf_op jit(solution)/shard_map/ppermute | solution.py:398
  23.7 1.3 %far_rows.1 = bf16[256,2048]{1,0:T(8,128)(2,1)} custom-call(f32[16,2048]{1,0:T(8,128)S(1)} %multiply_add_fusion.refs_0_, bf16[16,2048]{1,0:T(8,128)(2,1)S(1)} %collective-permute-done.6.refs_1_, bf16[256,2048]{1,0:T(8,128)(2,1)S(1)} %get-tuple-element.57.refs_2_, f32[128,2048]{1,0:T(8,128)S(1)} %get-tuple-element.58.refs_3_, ...), custom_call_target="tpu_custom_call" | custom-call | flops 1000000000 | bytes 1000000 | tf_op jit(solution)/shard_map/far_rows/pallas_call | solution.py:386
  (8 shorter events, 0.1 us)
Async XLA Ops:
  0.7 13.2 %collective-permute-start = (bf16[128,2048]{1,0:T(8,128)(2,1)S(1)}, bf16[128,2048]{1,0:T(8,128)(2,1)S(1)}, u32[]{:S(2)}, u32[]{:S(2)}) collective-permute-start(bf16[128,2048]{1,0:T(8,128)(2,1)S(1)} %tail_rows.3._after.refs_0_), channel_id=1, source_target_pairs={{0,4},{1,5},{2,6},{3,7},{16,20},{17,21},{18,22},{19,23}} | collective-permute-start | bytes 1572872 | tf_op jit(solution)/shard_map/ppermute | solution.py:398
  1.5 4.5 %copy-start = (bf16[128,128]{1,0:T(8,128)(2,1)S(1)}, bf16[128,128]{1,0:T(8,128)(2,1)}, u32[]{:S(2)}) copy-start(bf16[128,128]{1,0:T(8,128)(2,1)} %refs_3_.1) | copy-start | bytes 98308
  1.5 4.5 %copy-start.1 = (f32[128,16]{0,1:T(8,128)S(1)}, f32[128,16]{0,1:T(8,128)}, u32[]{:S(2)}) copy-start(f32[128,16]{0,1:T(8,128)} %param.14) | copy-start | bytes 24580
  1.5 4.4 %copy-start.2 = (f32[128,16]{0,1:T(8,128)S(1)}, f32[128,16]{0,1:T(8,128)}, u32[]{:S(2)}) copy-start(f32[128,16]{0,1:T(8,128)} %param.15) | copy-start | bytes 24580
  1.5 15.7 %collective-permute-start.2 = (bf16[128,2048]{1,0:T(8,128)(2,1)S(1)}, bf16[128,2048]{1,0:T(8,128)(2,1)S(1)}, u32[]{:S(2)}, u32[]{:S(2)}) collective-permute-start(bf16[128,2048]{1,0:T(8,128)(2,1)S(1)} %tail_rows.4._after.refs_1_), channel_id=1, source_target_pairs={{4,8},{5,9},{6,10},{7,11},{20,24},{21,25},{22,26},{23,27}} | collective-permute-start | bytes 1572872 | tf_op jit(solution)/shard_map/ppermute | solution.py:398
  4.2 16.0 %collective-permute-start.3 = (bf16[128,2048]{1,0:T(8,128)(2,1)S(1)}, bf16[128,2048]{1,0:T(8,128)(2,1)S(1)}, u32[]{:S(2)}, u32[]{:S(2)}) collective-permute-start(bf16[128,2048]{1,0:T(8,128)(2,1)S(1)} %tail_rows.5.refs_2_), channel_id=1, source_target_pairs={{8,12},{9,13},{10,14},{11,15},{24,28},{25,29},{26,30},{27,31}} | collective-permute-start | bytes 1572872 | tf_op jit(solution)/shard_map/ppermute | solution.py:398
  11.7 2.2 %collective-permute-start.1 = (bf16[16,2048]{1,0:T(8,128)(2,1)S(1)}, bf16[16,2048]{1,0:T(8,128)(2,1)S(1)}, u32[]{:S(2)}, u32[]{:S(2)}) collective-permute-start(bf16[16,2048]{1,0:T(8,128)(2,1)S(1)} %get-tuple-element.50), channel_id=1, source_target_pairs={{0,4},{1,5},{2,6},{3,7},{16,20},{17,21},{18,22},{19,23}} | collective-permute-start | bytes 196616 | tf_op jit(solution)/shard_map/ppermute | solution.py:398
  13.9 7.9 %collective-permute-start.5 = (bf16[16,2048]{1,0:T(8,128)(2,1)S(1)}, bf16[16,2048]{1,0:T(8,128)(2,1)S(1)}, u32[]{:S(2)}, u32[]{:S(2)}) collective-permute-start(bf16[16,2048]{1,0:T(8,128)(2,1)S(1)} %joined_sums.1._after), channel_id=1, source_target_pairs={{4,12},{5,13},{6,14},{7,15},{20,28},{21,29},{22,30},{23,31}} | collective-permute-start | bytes 196616 | tf_op jit(solution)/shard_map/ppermute | solution.py:398
  14.6 9.1 %collective-permute-start.4 = (bf16[16,2048]{1,0:T(8,128)(2,1)S(1)}, bf16[16,2048]{1,0:T(8,128)(2,1)S(1)}, u32[]{:S(2)}, u32[]{:S(2)}) collective-permute-start(bf16[16,2048]{1,0:T(8,128)(2,1)S(1)} %joined_sums.1._after), channel_id=1, source_target_pairs={{4,8},{5,9},{6,10},{7,11},{20,24},{21,25},{22,26},{23,27}} | collective-permute-start | bytes 196616 | tf_op jit(solution)/shard_map/ppermute | solution.py:398
  18.9 4.9 %collective-permute-start.6 = (bf16[16,2048]{1,0:T(8,128)(2,1)S(1)}, bf16[16,2048]{1,0:T(8,128)(2,1)S(1)}, u32[]{:S(2)}, u32[]{:S(2)}) collective-permute-start(bf16[16,2048]{1,0:T(8,128)(2,1)S(1)} %get-tuple-element.56), channel_id=1, source_target_pairs={{8,12},{9,13},{10,14},{11,15},{24,28},{25,29},{26,30},{27,31}} | collective-permute-start | bytes 196616 | tf_op jit(solution)/shard_map/ppermute | solution.py:398

commit v10 on v9

--- a/solution.py
+++ b/solution.py
@@ -265,10 +265,12 @@
     def convolve(i, at):
         mask = mask_ref[...]
         rim = rim_ref[:, at]
-        for first in range(half - width, -1, -width):
-            reached = dot(taptab_ref[half - first :, at], spread(rim[first : first + width], mask))
-            before_ref = part_ref if first == half - width else acc_ref
-            acc_ref[: first + width, at] = before_ref[: first + width, at] + reached
+        tables, chunks = [], []
+        for first in range(0, half, width):
+            table = taptab_ref[half - first :, at]
+            tables.append(jnp.concatenate([table, jnp.zeros((half - table.shape[0], WIDE), BF16)], axis=0) if table.shape[0] < half else table)
+            chunks.append(spread(rim[first : first + width], mask))
+        acc_ref[:, at] = part_ref[:, at] + dot(jnp.concatenate(tables, axis=1), jnp.concatenate(chunks, axis=0))
 
     def gate(i, at):
         mr = (q_ref[:half, at].astype(F32) * acc_ref[:, at]).astype(BF16)
@@ -277,7 +279,7 @@
         u_ref[:, at] = u
         early_ref[:, at] = pole_sums(ends_ref[at, :], u, fold_ref, poles)
 
-    pipelined(channels // WIDE, convolve, gate, lag=4)
+    pipelined(channels // WIDE, convolve, gate, lag=6)
 
 
 def rim_kernel(place, late_ref, decay_ref, _after, *refs):
@@ -499,10 +501,10 @@
             10**6,
             total_1, before, decay,
         )
+        one_before = send(total_1, (1, 2))
         two_before = send(total_1, (1, 3))
-        one_before = send(total_1, (1, 2))
         total_2, *rim_2 = with_rim(2, rims[1], total_1, BF16)
-        entered = before.astype(F32) + one_before.astype(F32) + two_before.astype(F32) * (decay * decay)
+        entered = two_before.astype(F32) * (decay * decay) + one_before.astype(F32) + before.astype(F32)
         arrived = [entered, send(total_2, (2, 3))]
         early_rows, places = (*without_rim, *rim_1, *rim_2), (0, 1, 2)
     else:

time: 25.3 us -> 25.3 us (level)
  the two profiles are of different devices: /device:TPU:18 before, /device:TPU:12 now
where the time goes in v10:
time: 25.3 us; the launch traced here: 25 us
  Pallas kernels  13.4 us (53%)
  starting transfers between devices  8.37 us (33%)
  waiting for transfers between devices  2.19 us (9%)
  between operations  1.02 us (4%)
    pallas_call x11, Pallas kernels, call(): pl.pallas_call(kernel, in_specs=ins, out_specs=[hbm if isinstance(out, ja...  13.4 us
    ppermute x7, starting transfers between devices, body(): send = lambda array, *pairs: lax.ppermute(array, 'ctx', pairs)  8.37 us
    ppermute x7, waiting for transfers between devices, body(): send = lambda array, *pairs: lax.ppermute(array, 'ctx', pairs)  2.19 us
  transfers between devices with their start and end apart: 7, of which 1 were waited for; matrix products, arithmetic and copies ran while one was open for 0% of the time, Pallas kernels for 48%

profile of v10, /device:TPU:12, one launch (start us, length us, event | category | flops | bytes accessed | tf_op | source)
XLA Modules:
  0.0 25.0 jit_solution(10300126715795799086)
XLA Ops:
  0.6 0.1 tail_rows.3._after.refs_0_
  0.7 1.3 %collective-permute-start = (bf16[128,2048]{1,0:T(8,128)(2,1)S(1)}, bf16[128,2048]{1,0:T(8,128)(2,1)S(1)}, u32[]{:S(2)}, u32[]{:S(2)}) collective-permute-start(bf16[128,2048]{1,0:T(8,128)(2,1)S(1)} %tail_rows.3._after.refs_0_), channel_id=1, source_target_pairs={{0,4},{1,5},{2,6},{3,7},{16,20},{17,21},{18,22},{19,23}} | collective-permute-start | bytes 1572872 | tf_op jit(solution)/shard_map/ppermute | solution.py:400
  2.0 1.3 %tail_rows.4._after.refs_1_ = bf16[128,2048]{1,0:T(8,128)(2,1)S(1)} custom-call(bf16[128,2048]{1,0:T(8,128)(2,1)S(1)} %tail_rows.3._after.refs_0_, bf16[256,2048]{1,0:T(8,128)(2,1)} %refs_7_.1, bf16[256,2048]{1,0:T(8,128)(2,1)} %refs_8_.1), custom_call_target="tpu_custom_call" | custom-call | flops 1000000 | bytes 1000 | tf_op jit(solution)/shard_map/tail_rows/pallas_call | solution.py:388
  3.3 0.0 copy-start
  3.3 0.0 copy-start.1
  3.3 0.0 copy-start.2
  3.3 1.8 %collective-permute-start.2 = (bf16[128,2048]{1,0:T(8,128)(2,1)S(1)}, bf16[128,2048]{1,0:T(8,128)(2,1)S(1)}, u32[]{:S(2)}, u32[]{:S(2)}) collective-permute-start(bf16[128,2048]{1,0:T(8,128)(2,1)S(1)} %tail_rows.4._after.refs_1_), channel_id=1, source_target_pairs={{4,8},{5,9},{6,10},{7,11},{20,24},{21,25},{22,26},{23,27}} | collective-permute-start | bytes 1572872 | tf_op jit(solution)/shard_map/ppermute | solution.py:400
  5.1 0.1 tail_rows.5.refs_2_
  5.2 0.7 %collective-permute-start.3 = (bf16[128,2048]{1,0:T(8,128)(2,1)S(1)}, bf16[128,2048]{1,0:T(8,128)(2,1)S(1)}, u32[]{:S(2)}, u32[]{:S(2)}) collective-permute-start(bf16[128,2048]{1,0:T(8,128)(2,1)S(1)} %tail_rows.5.refs_2_), channel_id=1, source_target_pairs={{8,12},{9,13},{10,14},{11,15},{24,28},{25,29},{26,30},{27,31}} | collective-permute-start | bytes 1572872 | tf_op jit(solution)/shard_map/ppermute | solution.py:400
  5.9 4.5 %local_rows.1 = (bf16[128,2048]{1,0:T(8,128)(2,1)S(1)}, f32[128,2048]{1,0:T(8,128)S(1)}, bf16[128,2048]{1,0:T(8,128)(2,1)S(1)}, f32[16,2048]{1,0:T(8,128)S(1)}, ...) custom-call(bf16[128,2048]{1,0:T(8,128)(2,1)S(1)} %tail_rows.3._afte, ...), custom_call_target="tpu_custom_call" | custom-call | flops 4000000000 | bytes 4000000 | tf_op jit(solution)/shard_map/local_rows/pallas_call | solution.py:388
  10.5 1.2 %filter_tables.1 = (bf16[16,2048]{1,0:T(8,128)(2,1)S(1)}, bf16[128,2048]{1,0:T(8,128)(2,1)S(1)}, bf16[128,2048]{1,0:T(8,128)(2,1)S(1)}, f32[16,2048]{1,0:T(8,128)S(1)}, bf16[256,2048]{1,0:T(8,128)(2,1)S(1)}) custom-call(f32[16,2048]{1,0:T(8,128)S(1)} %get-tuple-element.38.rates_ref, f32[16,2048]{1,0:T(8,128)S(1)} %get-tuple-element.39.residues_ref, ...), custom_call_target="tpu_custom_call" | custom-call | flops 1000000 | bytes 1000 | tf_op jit(solution)/shard_map/filter_tables/pallas_call | solution.py:388
  11.7 1.3 %collective-permute-start.1 = (bf16[16,2048]{1,0:T(8,128)(2,1)S(1)}, bf16[16,2048]{1,0:T(8,128)(2,1)S(1)}, u32[]{:S(2)}, u32[]{:S(2)}) collective-permute-start(bf16[16,2048]{1,0:T(8,128)(2,1)S(1)} %get-tuple-element.50), channel_id=1, source_target_pairs={{0,4},{1,5},{2,6},{3,7},{16,20},{17,21},{18,22},{19,23}} | collective-permute-start | bytes 196616 | tf_op jit(solution)/shard_map/ppermute | solution.py:400
  13.0 1.5 %near_late.1._after.refs_4_ = f32[128,2048]{1,0:T(8,128)S(1)} custom-call(bf16[128,2048]{1,0:T(8,128)(2,1)S(1)} %get-tuple-element.37.u_ref, bf16[128,2048]{1,0:T(8,128)(2,1)S(1)} %get-tuple-element.40.litab_ref.refs_16_), custom_call_target="tpu_custom_call" | custom-call | flops 1000000 | bytes 1000 | tf_op jit(solution)/shard_map/near_late/pallas_call | solution.py:388
  14.5 2.2 %collective-permute-done.refs_0_ = bf16[128,2048]{1,0:T(8,128)(2,1)S(1)} collective-permute-done((bf16[128,2048]{1,0:T(8,128)(2,1)S(1)}, bf16[128,2048]{1,0:T(8,128)(2,1)S(1)}, u32[]{:S(2)}, u32[]{:S(2)}) %collective-permute-start) | collective-permute-done | bytes 524320 | tf_op jit(solution)/shard_map/ppermute | solution.py:400
  16.7 1.6 %rim_rows.2 = (f32[16,2048]{1,0:T(8,128)S(1)}, bf16[128,2048]{1,0:T(8,128)(2,1)S(1)}, bf16[128,2048]{1,0:T(8,128)(2,1)S(1)}, f32[16,2048]{1,0:T(8,128)S(1)}) custom-call(f32[16,2048]{1,0:T(8,128)S(1)} %get-tuple-element.35.late_ref, f32[16,2048]{1,0:T(8,128)S(1)} %get-tuple-element.36.decay_ref.refs_7_, f32[128,2048]{1,0:T(8,128)S(1)} %near_late.1._after.refs_4_, ...), custom_call_target="tpu_custom_call" | custom-call | flops 1000000 | bytes 1000 | tf_op jit(solution)/shard_map/rim_rows/pallas_call | solution.py:388
  18.3 1.3 %collective-permute-start.5 = (bf16[16,2048]{1,0:T(8,128)(2,1)S(1)}, bf16[16,2048]{1,0:T(8,128)(2,1)S(1)}, u32[]{:S(2)}, u32[]{:S(2)}) collective-permute-start(bf16[16,2048]{1,0:T(8,128)(2,1)S(1)} %joined_sums.1._after), channel_id=1, source_target_pairs={{4,8},{5,9},{6,10},{7,11},{20,24},{21,25},{22,26},{23,27}} | collective-permute-start | bytes 196616 | tf_op jit(solution)/shard_map/ppermute | solution.py:400
  19.6 1.3 %collective-permute-start.4 = (bf16[16,2048]{1,0:T(8,128)(2,1)S(1)}, bf16[16,2048]{1,0:T(8,128)(2,1)S(1)}, u32[]{:S(2)}, u32[]{:S(2)}) collective-permute-start(bf16[16,2048]{1,0:T(8,128)(2,1)S(1)} %joined_sums.1._after), channel_id=1, source_target_pairs={{4,12},{5,13},{6,14},{7,15},{20,28},{21,29},{22,30},{23,31}} | collective-permute-start | bytes 196616 | tf_op jit(solution)/shard_map/ppermute | solution.py:400
  20.9 0.0 collective-permute-done.2.refs_0_
  21.0 0.7 %collective-permute-start.6 = (bf16[16,2048]{1,0:T(8,128)(2,1)S(1)}, bf16[16,2048]{1,0:T(8,128)(2,1)S(1)}, u32[]{:S(2)}, u32[]{:S(2)}) collective-permute-start(bf16[16,2048]{1,0:T(8,128)(2,1)S(1)} %get-tuple-element.56), channel_id=1, source_target_pairs={{8,12},{9,13},{10,14},{11,15},{24,28},{25,29},{26,30},{27,31}} | collective-permute-start | bytes 196616 | tf_op jit(solution)/shard_map/ppermute | solution.py:400
  21.7 0.0 collective-permute-done.3.refs_9_
  21.7 1.8 %near_part.1 = (f32[16,2048]{1,0:T(8,128)S(1)}, f32[128,2048]{1,0:T(8,128)S(1)}, bf16[256,2048]{1,0:T(8,128)(2,1)}) custom-call(bf16[128,2048]{1,0:T(8,128)(2,1)S(1)} %get-tuple-element.32.refs_0_, bf16[128,2048]{1,0:T(8,128)(2,1)S(1)} %get-tuple-element.33.refs_1_, f32[16,2048]{1,0:T(8,128)S(1)} %get-tuple-element.34.early_ref.refs_2_, ...), custom_call_target="tpu_custom_call" | custom-call | flops 1000000 | bytes 1000 | tf_op jit(solution)/shard_map/near_part/pallas_call | solution.py:388
  23.5 0.0 collective-permute-done.5
  23.6 0.0 collective-permute-done.6.refs_1_
  23.6 1.3 %far_rows.1 = bf16[256,2048]{1,0:T(8,128)(2,1)} custom-call(f32[16,2048]{1,0:T(8,128)S(1)} %convert_add_fusion.refs_0_, bf16[16,2048]{1,0:T(8,128)(2,1)S(1)} %collective-permute-done.6.refs_1_, bf16[256,2048]{1,0:T(8,128)(2,1)S(1)} %get-tuple-element.57.refs_2_, f32[128,2048]{1,0:T(8,128)S(1)} %get-tuple-element.58.refs_3_, ...), custom_call_target="tpu_custom_call" | custom-call | flops 1000000000 | bytes 1000000 | tf_op jit(solution)/shard_map/far_rows/pallas_call | solution.py:388
  (8 shorter events, 0.1 us)
Async XLA Ops:
  0.7 16.0 %collective-permute-start = (bf16[128,2048]{1,0:T(8,128)(2,1)S(1)}, bf16[128,2048]{1,0:T(8,128)(2,1)S(1)}, u32[]{:S(2)}, u32[]{:S(2)}) collective-permute-start(bf16[128,2048]{1,0:T(8,128)(2,1)S(1)} %tail_rows.3._after.refs_0_), channel_id=1, source_target_pairs={{0,4},{1,5},{2,6},{3,7},{16,20},{17,21},{18,22},{19,23}} | collective-permute-start | bytes 1572872 | tf_op jit(solution)/shard_map/ppermute | solution.py:400
  3.3 2.6 %copy-start = (bf16[128,128]{1,0:T(8,128)(2,1)S(1)}, bf16[128,128]{1,0:T(8,128)(2,1)}, u32[]{:S(2)}) copy-start(bf16[128,128]{1,0:T(8,128)(2,1)} %refs_3_.1) | copy-start | bytes 98308
  3.3 2.6 %copy-start.1 = (f32[128,16]{0,1:T(8,128)S(1)}, f32[128,16]{0,1:T(8,128)}, u32[]{:S(2)}) copy-start(f32[128,16]{0,1:T(8,128)} %param.14) | copy-start | bytes 24580
  3.3 2.6 %copy-start.2 = (f32[128,16]{0,1:T(8,128)S(1)}, f32[128,16]{0,1:T(8,128)}, u32[]{:S(2)}) copy-start(f32[128,16]{0,1:T(8,128)} %param.15) | copy-start | bytes 24580
  3.3 17.7 %collective-permute-start.2 = (bf16[128,2048]{1,0:T(8,128)(2,1)S(1)}, bf16[128,2048]{1,0:T(8,128)(2,1)S(1)}, u32[]{:S(2)}, u32[]{:S(2)}) collective-permute-start(bf16[128,2048]{1,0:T(8,128)(2,1)S(1)} %tail_rows.4._after.refs_1_), channel_id=1, source_target_pairs={{4,8},{5,9},{6,10},{7,11},{20,24},{21,25},{22,26},{23,27}} | collective-permute-start | bytes 1572872 | tf_op jit(solution)/shard_map/ppermute | solution.py:400
  5.2 16.5 %collective-permute-start.3 = (bf16[128,2048]{1,0:T(8,128)(2,1)S(1)}, bf16[128,2048]{1,0:T(8,128)(2,1)S(1)}, u32[]{:S(2)}, u32[]{:S(2)}) collective-permute-start(bf16[128,2048]{1,0:T(8,128)(2,1)S(1)} %tail_rows.5.refs_2_), channel_id=1, source_target_pairs={{8,12},{9,13},{10,14},{11,15},{24,28},{25,29},{26,30},{27,31}} | collective-permute-start | bytes 1572872 | tf_op jit(solution)/shard_map/ppermute | solution.py:400
  11.7 6.6 %collective-permute-start.1 = (bf16[16,2048]{1,0:T(8,128)(2,1)S(1)}, bf16[16,2048]{1,0:T(8,128)(2,1)S(1)}, u32[]{:S(2)}, u32[]{:S(2)}) collective-permute-start(bf16[16,2048]{1,0:T(8,128)(2,1)S(1)} %get-tuple-element.50), channel_id=1, source_target_pairs={{0,4},{1,5},{2,6},{3,7},{16,20},{17,21},{18,22},{19,23}} | collective-permute-start | bytes 196616 | tf_op jit(solution)/shard_map/ppermute | solution.py:400
  18.3 5.2 %collective-permute-start.5 = (bf16[16,2048]{1,0:T(8,128)(2,1)S(1)}, bf16[16,2048]{1,0:T(8,128)(2,1)S(1)}, u32[]{:S(2)}, u32[]{:S(2)}) collective-permute-start(bf16[16,2048]{1,0:T(8,128)(2,1)S(1)} %joined_sums.1._after), channel_id=1, source_target_pairs={{4,8},{5,9},{6,10},{7,11},{20,24},{21,25},{22,26},{23,27}} | collective-permute-start | bytes 196616 | tf_op jit(solution)/shard_map/ppermute | solution.py:400
  19.6 3.9 %collective-permute-start.4 = (bf16[16,2048]{1,0:T(8,128)(2,1)S(1)}, bf16[16,2048]{1,0:T(8,128)(2,1)S(1)}, u32[]{:S(2)}, u32[]{:S(2)}) collective-permute-start(bf16[16,2048]{1,0:T(8,128)(2,1)S(1)} %joined_sums.1._after), channel_id=1, source_target_pairs={{4,12},{5,13},{6,14},{7,15},{20,28},{21,29},{22,30},{23,31}} | collective-permute-start | bytes 196616 | tf_op jit(solution)/shard_map/ppermute | solution.py:400
  21.0 2.6 %collective-permute-start.6 = (bf16[16,2048]{1,0:T(8,128)(2,1)S(1)}, bf16[16,2048]{1,0:T(8,128)(2,1)S(1)}, u32[]{:S(2)}, u32[]{:S(2)}) collective-permute-start(bf16[16,2048]{1,0:T(8,128)(2,1)S(1)} %get-tuple-element.56), channel_id=1, source_target_pairs={{8,12},{9,13},{10,14},{11,15},{24,28},{25,29},{26,30},{27,31}} | collective-permute-start | bytes 196616 | tf_op jit(solution)/shard_map/ppermute | solution.py:400

commit v11 on v9

--- a/solution.py
+++ b/solution.py
@@ -197,7 +197,7 @@
     pipelined(steps, convolve_late)
     for copy in copies:
         copy.wait()
-    pipelined(steps, convolve_early, gate, lag=3)
+    pipelined(steps, convolve_early, gate, lag=6)
 
 
 def near_rows(u_ref, litab_ref, near_ref, mask_ref, width):
@@ -277,7 +277,7 @@
         u_ref[:, at] = u
         early_ref[:, at] = pole_sums(ends_ref[at, :], u, fold_ref, poles)
 
-    pipelined(channels // WIDE, convolve, gate, lag=4)
+    pipelined(channels // WIDE, convolve, gate, lag=6)
 
 
 def rim_kernel(place, late_ref, decay_ref, _after, *refs):

time: 25.3 us -> 25.3 us (level)
  no operation moved by 1% of the time
where the time goes in v11:
time: 25.3 us; the launch traced here: 25 us
  Pallas kernels  13.3 us (53%)
  starting transfers between devices  7.74 us (31%)
  waiting for transfers between devices  3.1 us (12%)
  between operations  0.83 us (3%)
    pallas_call x11, Pallas kernels, call(): pl.pallas_call(kernel, in_specs=ins, out_specs=[hbm if isinstance(out, ja...  13.3 us
    ppermute x7, starting transfers between devices, body(): send = lambda array, *pairs: lax.ppermute(array, 'ctx', pairs)  7.74 us
    ppermute x7, waiting for transfers between devices, body(): send = lambda array, *pairs: lax.ppermute(array, 'ctx', pairs)  3.1 us
  transfers between devices with their start and end apart: 7, of which 2 were waited for; matrix products, arithmetic and copies ran while one was open for 0% of the time, Pallas kernels for 48%

profile of v11, /device:TPU:18, one launch (start us, length us, event | category | flops | bytes accessed | tf_op | source)
XLA Modules:
  0.0 25.0 jit_solution(16355096434530684934)
XLA Ops:
  0.6 0.1 tail_rows.3._after.refs_0_
  0.7 0.7 %collective-permute-start = (bf16[128,2048]{1,0:T(8,128)(2,1)S(1)}, bf16[128,2048]{1,0:T(8,128)(2,1)S(1)}, u32[]{:S(2)}, u32[]{:S(2)}) collective-permute-start(bf16[128,2048]{1,0:T(8,128)(2,1)S(1)} %tail_rows.3._after.refs_0_), channel_id=1, source_target_pairs={{0,4},{1,5},{2,6},{3,7},{16,20},{17,21},{18,22},{19,23}} | collective-permute-start | bytes 1572872 | tf_op jit(solution)/shard_map/ppermute | solution.py:398
  1.4 0.1 tail_rows.4._after.refs_1_
  1.5 0.0 copy-start
  1.5 0.0 copy-start.1
  1.5 0.0 copy-start.2
  1.5 1.4 %collective-permute-start.2 = (bf16[128,2048]{1,0:T(8,128)(2,1)S(1)}, bf16[128,2048]{1,0:T(8,128)(2,1)S(1)}, u32[]{:S(2)}, u32[]{:S(2)}) collective-permute-start(bf16[128,2048]{1,0:T(8,128)(2,1)S(1)} %tail_rows.4._after.refs_1_), channel_id=1, source_target_pairs={{4,8},{5,9},{6,10},{7,11},{20,24},{21,25},{22,26},{23,27}} | collective-permute-start | bytes 1572872 | tf_op jit(solution)/shard_map/ppermute | solution.py:398
  2.9 1.3 %tail_rows.5.refs_2_ = bf16[128,2048]{1,0:T(8,128)(2,1)S(1)} custom-call(bf16[128,2048]{1,0:T(8,128)(2,1)S(1)} %tail_rows.4._after.refs_1_, bf16[256,2048]{1,0:T(8,128)(2,1)} %refs_7_.1, bf16[256,2048]{1,0:T(8,128)(2,1)} %refs_8_.1), custom_call_target="tpu_custom_call" | custom-call | flops 1000000 | bytes 1000 | tf_op jit(solution)/shard_map/tail_rows/pallas_call | solution.py:386
  4.2 1.7 %collective-permute-start.3 = (bf16[128,2048]{1,0:T(8,128)(2,1)S(1)}, bf16[128,2048]{1,0:T(8,128)(2,1)S(1)}, u32[]{:S(2)}, u32[]{:S(2)}) collective-permute-start(bf16[128,2048]{1,0:T(8,128)(2,1)S(1)} %tail_rows.5.refs_2_), channel_id=1, source_target_pairs={{8,12},{9,13},{10,14},{11,15},{24,28},{25,29},{26,30},{27,31}} | collective-permute-start | bytes 1572872 | tf_op jit(solution)/shard_map/ppermute | solution.py:398
  5.9 4.5 %local_rows.1 = (bf16[128,2048]{1,0:T(8,128)(2,1)S(1)}, f32[128,2048]{1,0:T(8,128)S(1)}, bf16[128,2048]{1,0:T(8,128)(2,1)S(1)}, f32[16,2048]{1,0:T(8,128)S(1)}, ...) custom-call(bf16[128,2048]{1,0:T(8,128)(2,1)S(1)} %tail_rows.3._afte, ...), custom_call_target="tpu_custom_call" | custom-call | flops 4000000000 | bytes 4000000 | tf_op jit(solution)/shard_map/local_rows/pallas_call | solution.py:386
  10.5 1.2 %filter_tables.1 = (bf16[16,2048]{1,0:T(8,128)(2,1)S(1)}, bf16[128,2048]{1,0:T(8,128)(2,1)S(1)}, bf16[128,2048]{1,0:T(8,128)(2,1)S(1)}, f32[16,2048]{1,0:T(8,128)S(1)}, bf16[256,2048]{1,0:T(8,128)(2,1)S(1)}) custom-call(f32[16,2048]{1,0:T(8,128)S(1)} %get-tuple-element.38.rates_ref, f32[16,2048]{1,0:T(8,128)S(1)} %get-tuple-element.39.residues_ref, ...), custom_call_target="tpu_custom_call" | custom-call | flops 1000000 | bytes 1000 | tf_op jit(solution)/shard_map/filter_tables/pallas_call | solution.py:386
  11.7 0.7 %collective-permute-start.1 = (bf16[16,2048]{1,0:T(8,128)(2,1)S(1)}, bf16[16,2048]{1,0:T(8,128)(2,1)S(1)}, u32[]{:S(2)}, u32[]{:S(2)}) collective-permute-start(bf16[16,2048]{1,0:T(8,128)(2,1)S(1)} %get-tuple-element.50), channel_id=1, source_target_pairs={{0,4},{1,5},{2,6},{3,7},{16,20},{17,21},{18,22},{19,23}} | collective-permute-start | bytes 196616 | tf_op jit(solution)/shard_map/ppermute | solution.py:398
  12.4 1.5 %near_late.1._after.refs_4_ = f32[128,2048]{1,0:T(8,128)S(1)} custom-call(bf16[128,2048]{1,0:T(8,128)(2,1)S(1)} %get-tuple-element.37.u_ref, bf16[128,2048]{1,0:T(8,128)(2,1)S(1)} %get-tuple-element.40.litab_ref.refs_16_), custom_call_target="tpu_custom_call" | custom-call | flops 1000000 | bytes 1000 | tf_op jit(solution)/shard_map/near_late/pallas_call | solution.py:386
  13.9 0.0 collective-permute-done.1.before_ref
  14.0 0.7 %collective-permute-start.5 = (bf16[16,2048]{1,0:T(8,128)(2,1)S(1)}, bf16[16,2048]{1,0:T(8,128)(2,1)S(1)}, u32[]{:S(2)}, u32[]{:S(2)}) collective-permute-start(bf16[16,2048]{1,0:T(8,128)(2,1)S(1)} %joined_sums.1._after), channel_id=1, source_target_pairs={{4,12},{5,13},{6,14},{7,15},{20,28},{21,29},{22,30},{23,31}} | collective-permute-start | bytes 196616 | tf_op jit(solution)/shard_map/ppermute | solution.py:398
  14.6 1.3 %collective-permute-start.4 = (bf16[16,2048]{1,0:T(8,128)(2,1)S(1)}, bf16[16,2048]{1,0:T(8,128)(2,1)S(1)}, u32[]{:S(2)}, u32[]{:S(2)}) collective-permute-start(bf16[16,2048]{1,0:T(8,128)(2,1)S(1)} %joined_sums.1._after), channel_id=1, source_target_pairs={{4,8},{5,9},{6,10},{7,11},{20,24},{21,25},{22,26},{23,27}} | collective-permute-start | bytes 196616 | tf_op jit(solution)/shard_map/ppermute | solution.py:398
  15.9 1.3 %collective-permute-done.2.refs_0_ = bf16[128,2048]{1,0:T(8,128)(2,1)S(1)} collective-permute-done((bf16[128,2048]{1,0:T(8,128)(2,1)S(1)}, bf16[128,2048]{1,0:T(8,128)(2,1)S(1)}, u32[]{:S(2)}, u32[]{:S(2)}) %collective-permute-start.2) | collective-permute-done | bytes 524320 | tf_op jit(solution)/shard_map/ppermute | solution.py:398
  17.2 1.7 %rim_rows.3 = (bf16[16,2048]{1,0:T(8,128)(2,1)S(1)}, bf16[128,2048]{1,0:T(8,128)(2,1)S(1)}, bf16[128,2048]{1,0:T(8,128)(2,1)S(1)}, f32[16,2048]{1,0:T(8,128)S(1)}) custom-call(f32[16,2048]{1,0:T(8,128)S(1)} %get-tuple-element.35.late_ref, f32[16,2048]{1,0:T(8,128)S(1)} %get-tuple-element.36.decay_ref.refs_7_, bf16[16,2048]{1,0:T(8,128)(2,1)S(1)} %joined_sums.1._after, ...), custom_call_target="tpu_custom_call" | custom-call | flops 1000000 | bytes 1000 | tf_op jit(solution)/shard_map/rim_rows/pallas_call | solution.py:386
  18.9 1.3 %collective-permute-start.6 = (bf16[16,2048]{1,0:T(8,128)(2,1)S(1)}, bf16[16,2048]{1,0:T(8,128)(2,1)S(1)}, u32[]{:S(2)}, u32[]{:S(2)}) collective-permute-start(bf16[16,2048]{1,0:T(8,128)(2,1)S(1)} %get-tuple-element.56), channel_id=1, source_target_pairs={{8,12},{9,13},{10,14},{11,15},{24,28},{25,29},{26,30},{27,31}} | collective-permute-start | bytes 196616 | tf_op jit(solution)/shard_map/ppermute | solution.py:398
  20.2 1.6 %near_part.1 = (f32[16,2048]{1,0:T(8,128)S(1)}, f32[128,2048]{1,0:T(8,128)S(1)}, bf16[256,2048]{1,0:T(8,128)(2,1)}) custom-call(bf16[128,2048]{1,0:T(8,128)(2,1)S(1)} %get-tuple-element.32.refs_0_, bf16[128,2048]{1,0:T(8,128)(2,1)S(1)} %get-tuple-element.33.refs_1_, f32[16,2048]{1,0:T(8,128)S(1)} %get-tuple-element.34.early_ref.refs_2_, ...), custom_call_target="tpu_custom_call" | custom-call | flops 1000000 | bytes 1000 | tf_op jit(solution)/shard_map/near_part/pallas_call | solution.py:386
  21.9 0.0 collective-permute-done.5
  21.9 1.8 %collective-permute-done.4 = bf16[16,2048]{1,0:T(8,128)(2,1)S(1)} collective-permute-done((bf16[16,2048]{1,0:T(8,128)(2,1)S(1)}, bf16[16,2048]{1,0:T(8,128)(2,1)S(1)}, u32[]{:S(2)}, u32[]{:S(2)}) %collective-permute-start.4) | collective-permute-done | bytes 65568 | tf_op jit(solution)/shard_map/ppermute | solution.py:398
  23.7 0.0 collective-permute-done.6.refs_1_
  23.8 1.3 %far_rows.1 = bf16[256,2048]{1,0:T(8,128)(2,1)} custom-call(f32[16,2048]{1,0:T(8,128)S(1)} %multiply_add_fusion.refs_0_, bf16[16,2048]{1,0:T(8,128)(2,1)S(1)} %collective-permute-done.6.refs_1_, bf16[256,2048]{1,0:T(8,128)(2,1)S(1)} %get-tuple-element.57.refs_2_, f32[128,2048]{1,0:T(8,128)S(1)} %get-tuple-element.58.refs_3_, ...), custom_call_target="tpu_custom_call" | custom-call | flops 1000000000 | bytes 1000000 | tf_op jit(solution)/shard_map/far_rows/pallas_call | solution.py:386
  (8 shorter events, 0.1 us)
Async XLA Ops:
  0.7 13.2 %collective-permute-start = (bf16[128,2048]{1,0:T(8,128)(2,1)S(1)}, bf16[128,2048]{1,0:T(8,128)(2,1)S(1)}, u32[]{:S(2)}, u32[]{:S(2)}) collective-permute-start(bf16[128,2048]{1,0:T(8,128)(2,1)S(1)} %tail_rows.3._after.refs_0_), channel_id=1, source_target_pairs={{0,4},{1,5},{2,6},{3,7},{16,20},{17,21},{18,22},{19,23}} | collective-permute-start | bytes 1572872 | tf_op jit(solution)/shard_map/ppermute | solution.py:398
  1.5 4.5 %copy-start = (bf16[128,128]{1,0:T(8,128)(2,1)S(1)}, bf16[128,128]{1,0:T(8,128)(2,1)}, u32[]{:S(2)}) copy-start(bf16[128,128]{1,0:T(8,128)(2,1)} %refs_3_.1) | copy-start | bytes 98308
  1.5 4.5 %copy-start.1 = (f32[128,16]{0,1:T(8,128)S(1)}, f32[128,16]{0,1:T(8,128)}, u32[]{:S(2)}) copy-start(f32[128,16]{0,1:T(8,128)} %param.14) | copy-start | bytes 24580
  1.5 4.4 %copy-start.2 = (f32[128,16]{0,1:T(8,128)S(1)}, f32[128,16]{0,1:T(8,128)}, u32[]{:S(2)}) copy-start(f32[128,16]{0,1:T(8,128)} %param.15) | copy-start | bytes 24580
  1.5 15.7 %collective-permute-start.2 = (bf16[128,2048]{1,0:T(8,128)(2,1)S(1)}, bf16[128,2048]{1,0:T(8,128)(2,1)S(1)}, u32[]{:S(2)}, u32[]{:S(2)}) collective-permute-start(bf16[128,2048]{1,0:T(8,128)(2,1)S(1)} %tail_rows.4._after.refs_1_), channel_id=1, source_target_pairs={{4,8},{5,9},{6,10},{7,11},{20,24},{21,25},{22,26},{23,27}} | collective-permute-start | bytes 1572872 | tf_op jit(solution)/shard_map/ppermute | solution.py:398
  4.2 16.0 %collective-permute-start.3 = (bf16[128,2048]{1,0:T(8,128)(2,1)S(1)}, bf16[128,2048]{1,0:T(8,128)(2,1)S(1)}, u32[]{:S(2)}, u32[]{:S(2)}) collective-permute-start(bf16[128,2048]{1,0:T(8,128)(2,1)S(1)} %tail_rows.5.refs_2_), channel_id=1, source_target_pairs={{8,12},{9,13},{10,14},{11,15},{24,28},{25,29},{26,30},{27,31}} | collective-permute-start | bytes 1572872 | tf_op jit(solution)/shard_map/ppermute | solution.py:398
  11.7 2.2 %collective-permute-start.1 = (bf16[16,2048]{1,0:T(8,128)(2,1)S(1)}, bf16[16,2048]{1,0:T(8,128)(2,1)S(1)}, u32[]{:S(2)}, u32[]{:S(2)}) collective-permute-start(bf16[16,2048]{1,0:T(8,128)(2,1)S(1)} %get-tuple-element.50), channel_id=1, source_target_pairs={{0,4},{1,5},{2,6},{3,7},{16,20},{17,21},{18,22},{19,23}} | collective-permute-start | bytes 196616 | tf_op jit(solution)/shard_map/ppermute | solution.py:398
  14.0 7.9 %collective-permute-start.5 = (bf16[16,2048]{1,0:T(8,128)(2,1)S(1)}, bf16[16,2048]{1,0:T(8,128)(2,1)S(1)}, u32[]{:S(2)}, u32[]{:S(2)}) collective-permute-start(bf16[16,2048]{1,0:T(8,128)(2,1)S(1)} %joined_sums.1._after), channel_id=1, source_target_pairs={{4,12},{5,13},{6,14},{7,15},{20,28},{21,29},{22,30},{23,31}} | collective-permute-start | bytes 196616 | tf_op jit(solution)/shard_map/ppermute | solution.py:398
  14.6 9.1 %collective-permute-start.4 = (bf16[16,2048]{1,0:T(8,128)(2,1)S(1)}, bf16[16,2048]{1,0:T(8,128)(2,1)S(1)}, u32[]{:S(2)}, u32[]{:S(2)}) collective-permute-start(bf16[16,2048]{1,0:T(8,128)(2,1)S(1)} %joined_sums.1._after), channel_id=1, source_target_pairs={{4,8},{5,9},{6,10},{7,11},{20,24},{21,25},{22,26},{23,27}} | collective-permute-start | bytes 196616 | tf_op jit(solution)/shard_map/ppermute | solution.py:398
  18.9 4.8 %collective-permute-start.6 = (bf16[16,2048]{1,0:T(8,128)(2,1)S(1)}, bf16[16,2048]{1,0:T(8,128)(2,1)S(1)}, u32[]{:S(2)}, u32[]{:S(2)}) collective-permute-start(bf16[16,2048]{1,0:T(8,128)(2,1)S(1)} %get-tuple-element.56), channel_id=1, source_target_pairs={{8,12},{9,13},{10,14},{11,15},{24,28},{25,29},{26,30},{27,31}} | collective-permute-start | bytes 196616 | tf_op jit(solution)/shard_map/ppermute | solution.py:398
